TPU v7x, 32 devices: a whole 2x2x4 slice. The times are simulated.
32 devices in a mesh: depth: 4 (over y, core), lat: 8 (over z, x).
Axes of the slice: x: 2, y: 2, z: 4, core: 2. Of those that a mesh axis runs over, the one named last changes fastest.
Arguments:
- obj_slices: float32 [4, 2, 2048, 512], P('depth', None, 'lat'), as said below
- probe: float32 [2, 256, 256], replicated, may hold values from -6 to 6
- positions: int32 [128, 2], P('lat'), may hold values from 0 to 256, as said below
- exit_cotangent: float32 [128, 2, 256, 256], P('lat'), may hold values from -6 to 6
Outputs:
- object_grad: float32 [4, 2, 2048, 512], P('depth', None, 'lat')
- probe_grad: float32 [2, 256, 256], P(None, 'depth')
Inputs may be any that keep to these rules, and one draw needn't show every extreme that they name: `positions`: for probe p, column 0 is a row offset below 256 within tile p // 16 of 256 rows, column 1 a column offset of at most 256; offset 0, 255 and 256 each occur. `obj_slices`: each slice value is amplitude times exp(i phase) with amplitude near one.
All inputs are finite; a program needn't handle non-finite values.
Results may differ from a plain program's by a relative error of at most 0.013.
Values may be sent and summed in bfloat16 or wider, within the bound.
No kernel may reach another device: no remote copies, remote signals or barrier semaphores. Data moves between devices by JAX's collectives and lax.ppermute only.
A program may use at most 128 MiB of HBM per device.

v0:
```python
import math

import jax
import jax.numpy as jnp
from jax import lax
from jax.sharding import PartitionSpec as P

defocus_scale = 0.7


def shifted(value, axis, steps):
    count = lax.axis_size(axis)
    pairs = [(source, (source + steps) % count) for source in range(count)]
    return lax.ppermute(value, axis, pairs)


def from_behind(value, axis, by):
    length = lax.axis_size(axis)
    pairs = [(i, i + by) for i in range(length) if 0 <= i + by < length]
    return lax.ppermute(value, axis, pairs)


def propagator(size):
    freq_index = jnp.arange(size, dtype=jnp.int32)
    signed = jnp.where(freq_index < size // 2, freq_index, freq_index - size).astype(jnp.float32)
    chirp = -math.pi * defocus_scale * signed * signed / size
    product_mod = freq_index[:, None] * freq_index[None, :] % size
    angles = 2.0 * math.pi * product_mod.astype(jnp.float32) / size + chirp[None, :]
    kernel_real = jnp.sum(jnp.cos(angles), axis=1) / size
    kernel_imag = jnp.sum(jnp.sin(angles), axis=1) / size
    offsets = (freq_index[:, None] - freq_index[None, :]) % size
    return (kernel_real[offsets], kernel_imag[offsets])


def apply_sides(prop_real, prop_imag, waves):
    real_part = waves[:, 0]
    imag_part = waves[:, 1]

    def left(matrix, field):
        return jnp.einsum("jl,bls->bjs", matrix, field, precision=lax.Precision.HIGHEST)

    def right(field, matrix):
        return jnp.einsum("bjl,ls->bjs", field, matrix, precision=lax.Precision.HIGHEST)

    first_real = left(prop_real, real_part) - left(prop_imag, imag_part)
    first_imag = left(prop_real, imag_part) + left(prop_imag, real_part)
    out_real = right(first_real, prop_real) - right(first_imag, prop_imag)
    out_imag = right(first_real, prop_imag) + right(first_imag, prop_real)
    return jnp.stack([out_real, out_imag], axis=1)


def complex_mul(first, second):
    real_part = first[:, 0] * second[:, 0] - first[:, 1] * second[:, 1]
    imag_part = first[:, 0] * second[:, 1] + first[:, 1] * second[:, 0]
    return jnp.stack([real_part, imag_part], axis=1)


def conjugate(values):
    return jnp.stack([values[:, 0], -values[:, 1]], axis=1)


def per_device(obj_slices, probe, positions, exit_cotangent):
    local_slices = obj_slices.shape[0]
    window = probe.shape[-1]
    owned = positions.shape[0]
    depth_count = lax.axis_size("depth")
    depth_index = lax.axis_index("depth")
    prop_real, prop_imag = propagator(window)
    upper_tile = shifted(obj_slices, "lat", -1)
    extended = jnp.concatenate([obj_slices, upper_tile], axis=2)
    grad_ext = jnp.zeros(extended.shape, jnp.float32)

    def add_window(grad_ext, offset, values):
        start = (0, 0, offset[0], offset[1])
        current = lax.dynamic_slice(grad_ext, start, values.shape)
        return lax.dynamic_update_slice(grad_ext, current + values, start)

    group = 1
    batches = owned // group
    wave_shape = (group, 2, window, window)

    def windows(batch):
        offsets = lax.dynamic_slice(positions, (batch * group, 0), (group, 2))

        def cutout(offset):
            return lax.dynamic_slice(
                extended, (0, 0, offset[0], offset[1]), (local_slices, 2, window, window)
            )

        return (offsets, jax.vmap(cutout)(offsets))

    launch = probe[None]

    def forward_batch(wave, batch):
        offsets, cuts = windows(batch)
        entries = [wave]
        wave = apply_sides(prop_real, prop_imag, complex_mul(wave, cuts[:, 0]))
        return (wave, jnp.stack(entries, axis=1))

    stored = jnp.zeros((batches, group, local_slices, 2, window, window), jnp.float32)
    arriving = jnp.zeros(wave_shape, jnp.bfloat16)

    def forward_tick(tick, carry):
        arriving, stored = carry
        batch = tick - depth_index
        active = (batch >= 0) & (batch < batches)
        clipped = jnp.clip(batch, 0, batches - 1)
        wave_in = jnp.where(depth_index == 0, launch, arriving.astype(jnp.float32))

        def forward_run_batch(stored):
            leaving, entries = forward_batch(wave_in, clipped)
            return (leaving, lax.dynamic_update_index_in_dim(stored, entries, clipped, 0))

        def forward_skip_batch(stored):
            return (jnp.zeros_like(wave_in), stored)

        leaving, stored = lax.cond(active, forward_run_batch, forward_skip_batch, stored)
        arriving = from_behind(leaving.astype(jnp.bfloat16), "depth", 1)
        return (arriving, stored)

    arriving, stored = lax.fori_loop(0, batches + depth_count - 1, forward_tick, (arriving, stored))

    def backward_batch(cotan, batch, grad_ext):
        offsets, cuts = windows(batch)
        entries = lax.dynamic_index_in_dim(stored, batch, 0, keepdims=False)
        grads = [None] * local_slices
        for slice_index in reversed(range(local_slices)):
            before = apply_sides(prop_real, -prop_imag, cotan)
            grads[slice_index] = complex_mul(conjugate(entries[:, slice_index]), before)
            cotan = complex_mul(conjugate(cuts[:, slice_index]), before)
        stacked = jnp.stack(grads, axis=1)
        grad_ext = add_window(grad_ext, offsets[0], stacked[0])
        return (cotan, grad_ext)

    probe_part = jnp.zeros(probe.shape, jnp.float32)
    returning = jnp.zeros(wave_shape, jnp.bfloat16)

    def backward_tick(tick, carry):
        returning, grad_ext, probe_part = carry
        batch = tick - (depth_count - 1 - depth_index)
        active = (batch >= 0) & (batch < batches)
        clipped = jnp.clip(batch, 0, batches - 1)
        given = lax.dynamic_slice_in_dim(exit_cotangent, clipped * group, group, 0)
        cotan_in = jnp.where(depth_index == depth_count - 1, given, returning.astype(jnp.float32))

        def backward_run_batch(state):
            leaving, new_ext = backward_batch(cotan_in, clipped, state[0])
            new_part = state[1] + jnp.where(depth_index == 0, jnp.sum(leaving, axis=0), 0.0)
            return (leaving, new_ext, new_part)

        def backward_skip_batch(state):
            return (jnp.zeros_like(cotan_in), state[0], state[1])

        leaving, grad_ext, probe_part = lax.cond(
            active, backward_run_batch, backward_skip_batch, (grad_ext, probe_part)
        )
        returning = from_behind(leaving.astype(jnp.bfloat16), "depth", -1)
        return (returning, grad_ext, probe_part)

    returning, grad_ext, probe_part = lax.fori_loop(
        0, batches + depth_count - 1, backward_tick, (returning, grad_ext, probe_part)
    )
    tile_total = lax.psum(probe_part.astype(jnp.bfloat16), "lat")
    probe_grad = lax.psum_scatter(tile_total, "depth", scatter_dimension=1, tiled=True).astype(
        jnp.float32
    )
    lower_part = shifted(grad_ext[:, :, window:].astype(jnp.bfloat16), "lat", 1).astype(jnp.float32)
    object_grad = grad_ext[:, :, :window] + lower_part
    return (object_grad, probe_grad)


def solution(mesh):
    placed = (P("depth", None, "lat", None), P(), P("lat", None), P("lat", None, None, None))
    return jax.shard_map(
        per_device,
        mesh=mesh,
        in_specs=placed,
        out_specs=(P("depth", None, "lat", None), P(None, "depth", None)),
        check_vma=False,
    )
```

profile of v0, /device:TPU:0, one launch (start us, length us, event | category | flops | bytes accessed | tf_op | source)
XLA Modules:
  0.0 1908.8 jit_solution(9557023437115888671)
XLA Ops:
  14.8 408.0 %gather_fusion = f32[65536]{0:T(1024)S(1)} fusion(f32[256]{0:T(256)S(1)} %get-tuple-element.722, s32[65536]{0:T(1024)S(1)} %broadcast_clamp_fusion), kind=kCustom, calls=%fused_computation | custom fusion | bytes 786432 | tf_op jit(solution)/shard_map/gather | solution.py:32
  422.9 408.0 %gather_fusion.1 = f32[65536]{0:T(1024)S(1)} fusion(f32[256]{0:T(256)S(1)} %get-tuple-element.721, s32[65536]{0:T(1024)S(1)} %broadcast_clamp_fusion), kind=kCustom, calls=%fused_computation.1 | custom fusion | bytes 786432 | tf_op jit(solution)/shard_map/gather | solution.py:32
  838.6 345.8 %while.39 = (s32[]{:T(128)}, bf16[1,2,256,256]{3,2,1,0:T(8,128)(2,1)S(1)}, f32[16,1,1,2,256,256]{5,4,3,2,1,0:T(8,128)}, s32[]{:T(128)}, pred[]{:T(512)}, /*index...) while((s32[]{:T(128)}, ...), condition=%wide.region_5.6_spmd, body=%wide.region_2.5_spmd.sunk | while | flops 1611792384 | bytes 12059583 | solution.py:121
  838.6 11.7 conditional.4
  852.8 11.7 conditional.4
  867.9 11.8 conditional.4
  884.9 11.8 conditional.4
  904.2 11.8 conditional.4
  923.7 11.8 conditional.4
  935.5 6.6 collective-permute-start
  943.2 11.7 conditional.4
  954.9 6.6 collective-permute-start
  962.6 11.8 conditional.4
  982.1 11.8 conditional.4
  993.8 6.6 collective-permute-start
  1001.5 11.8 conditional.4
  1021.0 11.8 conditional.4
  1040.4 11.8 conditional.4
  1052.2 6.6 collective-permute-start
  1059.9 11.8 conditional.4
  1079.4 11.7 conditional.4
  1091.1 6.6 collective-permute-start
  1098.8 11.8 conditional.4
  1110.6 6.6 collective-permute-start
  1118.3 11.8 conditional.4
  1137.8 18.3 collective-permute-start
  1165.0 18.3 collective-permute-start
  1186.1 617.7 %while.40 = (s32[]{:T(128)}, bf16[1,2,256,256]{3,2,1,0:T(8,128)(2,1)S(1)}, f32[1,2,512,512]{3,2,1,0:T(8,128)}, f32[2,256,256]{2,1,0:T(8,128)S(1)}, s32[]{:T(128)...) while((s32[]{:T(128)}, ...), condition=%wide.region_9.10_spmd, body=%wide.region_6.9_spmd.sunk | while | flops 1613103104 | bytes 17302116 | solution.py:160
  1196.8 10.2 collective-permute-done.1
  1209.1 68.7 %collective-permute-done.1 = bf16[1,2,256,256]{3,2,1,0:T(8,128)(2,1)S(1)} collective-permute-done((bf16[1,2,256,256]{3,2,1,0:T(8,128)(2,1)}, bf16[1,2,256,256]{3,2,1,0:T(8,128)(2,1)S(1)}, u32[]{:S(2)}, u32[]{:S(2)}) %collective-permute-start.1) | collective-permute-done | bytes 262176 | tf_op jit(solution)/shard_map/while/body/eval_jaxpr/ppermute | solution.py:20
  1277.7 23.1 %conditional.5 = (bf16[1,2,256,256]{3,2,1,0:T(8,128)(2,1)}, f32[1,2,512,512]{3,2,1,0:T(8,128)}, f32[2,256,256]{2,1,0:T(8,128)S(1)}) conditional(s32[]{:T(128)} %convert_element_type.102, (f32[1,2,512,512]{3,2,1,0:T(8,128)}, f32[2,256,256]{2,1,0:T(8,128)S(1)}) %tuple.124, (s32[]{:T(128)}, s32[16,2]{0,1:T(2,128)S(1)}, f32[1,2,512,512]{3,2,1,0:T(8,128)}, ...), branch_computations={%region_7.7_spmd, %region_8.8_spmd} | conditional | flops 1613103104 | bytes 16253203 | solution.py:154
  1302.1 8.2 collective-permute-done.1
  1310.3 24.7 %conditional.5 = (bf16[1,2,256,256]{3,2,1,0:T(8,128)(2,1)}, f32[1,2,512,512]{3,2,1,0:T(8,128)}, f32[2,256,256]{2,1,0:T(8,128)S(1)}) conditional(s32[]{:T(128)} %convert_element_type.102, (f32[1,2,512,512]{3,2,1,0:T(8,128)}, f32[2,256,256]{2,1,0:T(8,128)S(1)}) %tuple.124, (s32[]{:T(128)}, s32[16,2]{0,1:T(2,128)S(1)}, f32[1,2,512,512]{3,2,1,0:T(8,128)}, ...), branch_computations={%region_7.7_spmd, %region_8.8_spmd} | conditional | flops 1613103104 | bytes 16253203 | solution.py:154
  1336.4 7.1 collective-permute-done.1
  1343.5 25.2 %conditional.5 = (bf16[1,2,256,256]{3,2,1,0:T(8,128)(2,1)}, f32[1,2,512,512]{3,2,1,0:T(8,128)}, f32[2,256,256]{2,1,0:T(8,128)S(1)}) conditional(s32[]{:T(128)} %convert_element_type.102, (f32[1,2,512,512]{3,2,1,0:T(8,128)}, f32[2,256,256]{2,1,0:T(8,128)S(1)}) %tuple.124, (s32[]{:T(128)}, s32[16,2]{0,1:T(2,128)S(1)}, f32[1,2,512,512]{3,2,1,0:T(8,128)}, ...), branch_computations={%region_7.7_spmd, %region_8.8_spmd} | conditional | flops 1613103104 | bytes 16253203 | solution.py:154
  1376.3 25.0 %conditional.5 = (bf16[1,2,256,256]{3,2,1,0:T(8,128)(2,1)}, f32[1,2,512,512]{3,2,1,0:T(8,128)}, f32[2,256,256]{2,1,0:T(8,128)S(1)}) conditional(s32[]{:T(128)} %convert_element_type.102, (f32[1,2,512,512]{3,2,1,0:T(8,128)}, f32[2,256,256]{2,1,0:T(8,128)S(1)}) %tuple.124, (s32[]{:T(128)}, s32[16,2]{0,1:T(2,128)S(1)}, f32[1,2,512,512]{3,2,1,0:T(8,128)}, ...), branch_computations={%region_7.7_spmd, %region_8.8_spmd} | conditional | flops 1613103104 | bytes 16253203 | solution.py:154
  1402.6 7.0 collective-permute-done.1
  1409.6 25.4 %conditional.5 = (bf16[1,2,256,256]{3,2,1,0:T(8,128)(2,1)}, f32[1,2,512,512]{3,2,1,0:T(8,128)}, f32[2,256,256]{2,1,0:T(8,128)S(1)}) conditional(s32[]{:T(128)} %convert_element_type.102, (f32[1,2,512,512]{3,2,1,0:T(8,128)}, f32[2,256,256]{2,1,0:T(8,128)S(1)}) %tuple.124, (s32[]{:T(128)}, s32[16,2]{0,1:T(2,128)S(1)}, f32[1,2,512,512]{3,2,1,0:T(8,128)}, ...), branch_computations={%region_7.7_spmd, %region_8.8_spmd} | conditional | flops 1613103104 | bytes 16253203 | solution.py:154
  1436.3 6.7 collective-permute-done.1
  1442.9 25.4 %conditional.5 = (bf16[1,2,256,256]{3,2,1,0:T(8,128)(2,1)}, f32[1,2,512,512]{3,2,1,0:T(8,128)}, f32[2,256,256]{2,1,0:T(8,128)S(1)}) conditional(s32[]{:T(128)} %convert_element_type.102, (f32[1,2,512,512]{3,2,1,0:T(8,128)}, f32[2,256,256]{2,1,0:T(8,128)S(1)}) %tuple.124, (s32[]{:T(128)}, s32[16,2]{0,1:T(2,128)S(1)}, f32[1,2,512,512]{3,2,1,0:T(8,128)}, ...), branch_computations={%region_7.7_spmd, %region_8.8_spmd} | conditional | flops 1613103104 | bytes 16253203 | solution.py:154
  1460.9 6.6 dynamic_update_slice.10
  1475.8 25.0 %conditional.5 = (bf16[1,2,256,256]{3,2,1,0:T(8,128)(2,1)}, f32[1,2,512,512]{3,2,1,0:T(8,128)}, f32[2,256,256]{2,1,0:T(8,128)S(1)}) conditional(s32[]{:T(128)} %convert_element_type.102, (f32[1,2,512,512]{3,2,1,0:T(8,128)}, f32[2,256,256]{2,1,0:T(8,128)S(1)}) %tuple.124, (s32[]{:T(128)}, s32[16,2]{0,1:T(2,128)S(1)}, f32[1,2,512,512]{3,2,1,0:T(8,128)}, ...), branch_computations={%region_7.7_spmd, %region_8.8_spmd} | conditional | flops 1613103104 | bytes 16253203 | solution.py:154
  1502.0 7.0 collective-permute-done.1
  1509.0 25.4 %conditional.5 = (bf16[1,2,256,256]{3,2,1,0:T(8,128)(2,1)}, f32[1,2,512,512]{3,2,1,0:T(8,128)}, f32[2,256,256]{2,1,0:T(8,128)S(1)}) conditional(s32[]{:T(128)} %convert_element_type.102, (f32[1,2,512,512]{3,2,1,0:T(8,128)}, f32[2,256,256]{2,1,0:T(8,128)S(1)}) %tuple.124, (s32[]{:T(128)}, s32[16,2]{0,1:T(2,128)S(1)}, f32[1,2,512,512]{3,2,1,0:T(8,128)}, ...), branch_computations={%region_7.7_spmd, %region_8.8_spmd} | conditional | flops 1613103104 | bytes 16253203 | solution.py:154
  1535.7 6.7 collective-permute-done.1
  1542.3 25.4 %conditional.5 = (bf16[1,2,256,256]{3,2,1,0:T(8,128)(2,1)}, f32[1,2,512,512]{3,2,1,0:T(8,128)}, f32[2,256,256]{2,1,0:T(8,128)S(1)}) conditional(s32[]{:T(128)} %convert_element_type.102, (f32[1,2,512,512]{3,2,1,0:T(8,128)}, f32[2,256,256]{2,1,0:T(8,128)S(1)}) %tuple.124, (s32[]{:T(128)}, s32[16,2]{0,1:T(2,128)S(1)}, f32[1,2,512,512]{3,2,1,0:T(8,128)}, ...), branch_computations={%region_7.7_spmd, %region_8.8_spmd} | conditional | flops 1613103104 | bytes 16253203 | solution.py:154
  1560.3 6.6 dynamic_update_slice.10
  1575.5 25.3 %conditional.5 = (bf16[1,2,256,256]{3,2,1,0:T(8,128)(2,1)}, f32[1,2,512,512]{3,2,1,0:T(8,128)}, f32[2,256,256]{2,1,0:T(8,128)S(1)}) conditional(s32[]{:T(128)} %convert_element_type.102, (f32[1,2,512,512]{3,2,1,0:T(8,128)}, f32[2,256,256]{2,1,0:T(8,128)S(1)}) %tuple.124, (s32[]{:T(128)}, s32[16,2]{0,1:T(2,128)S(1)}, f32[1,2,512,512]{3,2,1,0:T(8,128)}, ...), branch_computations={%region_7.7_spmd, %region_8.8_spmd} | conditional | flops 1613103104 | bytes 16253203 | solution.py:154
  1608.4 25.0 %conditional.5 = (bf16[1,2,256,256]{3,2,1,0:T(8,128)(2,1)}, f32[1,2,512,512]{3,2,1,0:T(8,128)}, f32[2,256,256]{2,1,0:T(8,128)S(1)}) conditional(s32[]{:T(128)} %convert_element_type.102, (f32[1,2,512,512]{3,2,1,0:T(8,128)}, f32[2,256,256]{2,1,0:T(8,128)S(1)}) %tuple.124, (s32[]{:T(128)}, s32[16,2]{0,1:T(2,128)S(1)}, f32[1,2,512,512]{3,2,1,0:T(8,128)}, ...), branch_computations={%region_7.7_spmd, %region_8.8_spmd} | conditional | flops 1613103104 | bytes 16253203 | solution.py:154
  1634.6 7.2 collective-permute-done.1
  1641.8 25.6 %conditional.5 = (bf16[1,2,256,256]{3,2,1,0:T(8,128)(2,1)}, f32[1,2,512,512]{3,2,1,0:T(8,128)}, f32[2,256,256]{2,1,0:T(8,128)S(1)}) conditional(s32[]{:T(128)} %convert_element_type.102, (f32[1,2,512,512]{3,2,1,0:T(8,128)}, f32[2,256,256]{2,1,0:T(8,128)S(1)}) %tuple.124, (s32[]{:T(128)}, s32[16,2]{0,1:T(2,128)S(1)}, f32[1,2,512,512]{3,2,1,0:T(8,128)}, ...), branch_computations={%region_7.7_spmd, %region_8.8_spmd} | conditional | flops 1613103104 | bytes 16253203 | solution.py:154
  1659.8 6.7 dynamic_update_slice.10
  1668.7 6.6 collective-permute-done.1
  1675.3 25.6 %conditional.5 = (bf16[1,2,256,256]{3,2,1,0:T(8,128)(2,1)}, f32[1,2,512,512]{3,2,1,0:T(8,128)}, f32[2,256,256]{2,1,0:T(8,128)S(1)}) conditional(s32[]{:T(128)} %convert_element_type.102, (f32[1,2,512,512]{3,2,1,0:T(8,128)}, f32[2,256,256]{2,1,0:T(8,128)S(1)}) %tuple.124, (s32[]{:T(128)}, s32[16,2]{0,1:T(2,128)S(1)}, f32[1,2,512,512]{3,2,1,0:T(8,128)}, ...), branch_computations={%region_7.7_spmd, %region_8.8_spmd} | conditional | flops 1613103104 | bytes 16253203 | solution.py:154
  1693.3 6.8 dynamic_update_slice.10
  1702.2 6.6 collective-permute-done.1
  1708.8 25.6 %conditional.5 = (bf16[1,2,256,256]{3,2,1,0:T(8,128)(2,1)}, f32[1,2,512,512]{3,2,1,0:T(8,128)}, f32[2,256,256]{2,1,0:T(8,128)S(1)}) conditional(s32[]{:T(128)} %convert_element_type.102, (f32[1,2,512,512]{3,2,1,0:T(8,128)}, f32[2,256,256]{2,1,0:T(8,128)S(1)}) %tuple.124, (s32[]{:T(128)}, s32[16,2]{0,1:T(2,128)S(1)}, f32[1,2,512,512]{3,2,1,0:T(8,128)}, ...), branch_computations={%region_7.7_spmd, %region_8.8_spmd} | conditional | flops 1613103104 | bytes 16253203 | solution.py:154
  1726.7 6.7 dynamic_update_slice.10
  1735.6 6.5 collective-permute-done.1
  1742.2 25.5 %conditional.5 = (bf16[1,2,256,256]{3,2,1,0:T(8,128)(2,1)}, f32[1,2,512,512]{3,2,1,0:T(8,128)}, f32[2,256,256]{2,1,0:T(8,128)S(1)}) conditional(s32[]{:T(128)} %convert_element_type.102, (f32[1,2,512,512]{3,2,1,0:T(8,128)}, f32[2,256,256]{2,1,0:T(8,128)S(1)}) %tuple.124, (s32[]{:T(128)}, s32[16,2]{0,1:T(2,128)S(1)}, f32[1,2,512,512]{3,2,1,0:T(8,128)}, ...), branch_computations={%region_7.7_spmd, %region_8.8_spmd} | conditional | flops 1613103104 | bytes 16253203 | solution.py:154
  1760.1 6.7 dynamic_update_slice.10
  1775.1 25.0 %conditional.5 = (bf16[1,2,256,256]{3,2,1,0:T(8,128)(2,1)}, f32[1,2,512,512]{3,2,1,0:T(8,128)}, f32[2,256,256]{2,1,0:T(8,128)S(1)}) conditional(s32[]{:T(128)} %convert_element_type.102, (f32[1,2,512,512]{3,2,1,0:T(8,128)}, f32[2,256,256]{2,1,0:T(8,128)S(1)}) %tuple.124, (s32[]{:T(128)}, s32[16,2]{0,1:T(2,128)S(1)}, f32[1,2,512,512]{3,2,1,0:T(8,128)}, ...), branch_computations={%region_7.7_spmd, %region_8.8_spmd} | conditional | flops 1613103104 | bytes 16253203 | solution.py:154
  1809.0 19.2 %reduce-scatter.2.cloned.1.call-done = bf16[2,64,256]{2,1,0:T(8,128)(2,1)} async-done(((bf16[2,256,256]{2,1,0:T(8,128)(2,1)}), bf16[2,64,256]{2,1,0:T(8,128)(2,1)}) %reduce-scatter.2.cloned.1.call-update) | async-done | bytes 65552 | tf_op jit(solution)/shard_map/reduce_scatter | solution.py:164
  1830.6 69.9 %all-reduce.2.cloned.1.call-done = bf16[2,64,256]{2,1,0:T(8,128)(2,1)} async-done(((bf16[2,64,256]{2,1,0:T(8,128)(2,1)}), bf16[2,64,256]{2,1,0:T(8,128)(2,1)}) %all-reduce.2.cloned.1.call-update) | async-done | bytes 65552 | tf_op jit(solution)/shard_map/psum | solution.py:163
  (543 shorter events, 539.0 us)
Async XLA Ops:
  7.2 1821.0 %reduce-scatter.2.cloned.1.call-start = ((), (), s32[]{:S(2)}) async-start(), calls=%async_computation.1 | async-start | bytes 327680 | tf_op jit(solution)/shard_map/reduce_scatter | solution.py:164
  7.2 824.9 %collective-permute-start.2 = (f32[1,2,256,512]{3,2,1,0:T(8,128)}, f32[1,2,256,512]{3,2,1,0:T(8,128)}, u32[]{:S(2)}, u32[]{:S(2)}) collective-permute-start(f32[1,2,256,512]{3,2,1,0:T(8,128)} %param.12), channel_id=1, source_target_pairs={{0,7},{1,0},{2,1},{3,2},{4,3},{5,4},{6,5},{7,6},{8,15},{9,8},{10,9... | collective-permute-start | bytes 3145736 | tf_op jit(solution)/shard_map/ppermute | solution.py:14
  422.9 408.1 %copy-start.1 = (f32[1,2,256,512]{3,2,1,0:T(8,128)S(1)}, f32[1,2,256,512]{3,2,1,0:T(8,128)}, u32[]{:S(2)}) copy-start(f32[1,2,256,512]{3,2,1,0:T(8,128)} %param.12) | copy-start | bytes 3145732
  834.4 4.2 copy-start
  834.4 4.2 copy-start.2
  850.3 2.4 collective-permute-start
  864.5 3.3 collective-permute-start
  879.7 5.2 collective-permute-start
  896.6 7.6 collective-permute-start
  916.0 7.7 collective-permute-start
  935.5 7.7 collective-permute-start
  954.9 7.7 collective-permute-start
  974.4 7.7 collective-permute-start
  993.8 7.7 collective-permute-start
  1013.3 7.7 collective-permute-start
  1032.8 7.7 collective-permute-start
  1052.2 7.7 collective-permute-start
  1071.7 7.7 collective-permute-start
  1091.1 7.7 collective-permute-start
  1110.6 7.7 collective-permute-start
  1130.1 7.7 collective-permute-start
  1137.8 19.4 %collective-permute-start = (bf16[1,2,256,256]{3,2,1,0:T(8,128)(2,1)S(1)}, bf16[1,2,256,256]{3,2,1,0:T(8,128)(2,1)S(1)}, u32[]{:S(2)}, u32[]{:S(2)}) collective-permute-start(bf16[1,2,256,256]{3,2,1,0:T(8,128)(2,1)S(1)} %get-tuple-element.857), channel_id=1, source_target_pairs={{0,8},{8,16},{16,24},{1,9},{9,17},{17,25},{2,10},{10,18},{18,26},{... | collective-permute-start | bytes 786440 | tf_op jit(solution)/shard_map/while/body/eval_jaxpr/ppermute | solution.py:20
  1157.3 7.6 collective-permute-start
  1165.0 19.5 %collective-permute-start = (bf16[1,2,256,256]{3,2,1,0:T(8,128)(2,1)S(1)}, bf16[1,2,256,256]{3,2,1,0:T(8,128)(2,1)S(1)}, u32[]{:S(2)}, u32[]{:S(2)}) collective-permute-start(bf16[1,2,256,256]{3,2,1,0:T(8,128)(2,1)S(1)} %get-tuple-element.857), channel_id=1, source_target_pairs={{0,8},{8,16},{16,24},{1,9},{9,17},{17,25},{2,10},{10,18},{18,26},{... | collective-permute-start | bytes 786440 | tf_op jit(solution)/shard_map/while/body/eval_jaxpr/ppermute | solution.py:20
  1187.0 7.8 collective-permute-start.1
  1195.5 11.5 collective-permute-start.1
  1207.8 70.0 %collective-permute-start.1 = (bf16[1,2,256,256]{3,2,1,0:T(8,128)(2,1)}, bf16[1,2,256,256]{3,2,1,0:T(8,128)(2,1)S(1)}, u32[]{:S(2)}, u32[]{:S(2)}) collective-permute-start(bf16[1,2,256,256]{3,2,1,0:T(8,128)(2,1)} %get-tuple-element.872), channel_id=1, source_target_pairs={{8,0},{16,8},{24,16},{9,1},{17,9},{25,17},{10,2},{18,10},{26,18},{... | collective-permute-start | bytes 786440 | tf_op jit(solution)/shard_map/while/body/eval_jaxpr/ppermute | solution.py:20
  1300.8 9.5 collective-permute-start.1
  1335.1 8.4 collective-permute-start.1
  1368.7 7.6 collective-permute-start.1
  1401.3 8.3 collective-permute-start.1
  1435.0 7.9 collective-permute-start.1
  1468.3 7.4 collective-permute-start.1
  1500.7 8.3 collective-permute-start.1
  1534.4 7.9 collective-permute-start.1
  1567.7 7.8 collective-permute-start.1
  1600.8 7.6 collective-permute-start.1
  1633.3 8.5 collective-permute-start.1
  1667.4 7.9 collective-permute-start.1
  1700.9 7.9 collective-permute-start.1
  1734.4 7.8 collective-permute-start.1
  1767.7 7.4 collective-permute-start.1
  1800.1 3.6 collective-permute-start.1
  1804.5 96.0 %all-reduce.2.cloned.1.call-start = ((), (), s32[]{:S(2)}) async-start(), calls=%async_computation.2 | async-start | bytes 131072 | tf_op jit(solution)/shard_map/psum | solution.py:163
  1805.8 22.4 %collective-permute-start.3 = (bf16[1,2,256,512]{3,2,1,0:T(8,128)(2,1)S(1)}, bf16[1,2,256,512]{3,2,1,0:T(8,128)(2,1)S(1)}, u32[]{:S(2)}, u32[]{:S(2)}) collective-permute-start(bf16[1,2,256,512]{3,2,1,0:T(8,128)(2,1)S(1)} %slice.166), channel_id=1, source_target_pairs={{0,1},{1,2},{2,3},{3,4},{4,5},{5,6},{6,7},{7,0},{8,9},{9,10},{10,1... | collective-permute-start | bytes 1572872 | tf_op jit(solution)/shard_map/ppermute | solution.py:14
Sparse Core Ops, SparseCore 0:
  1804.6 23.5 reduce-scatter.1
  1832.0 68.4 all-reduce.1
where the time goes:
time: 1920 us; the launch traced here: 1910 us
  local copies, waits for them, and re-layouts  967 us (50%)
  waiting for transfers between devices  299 us (16%)
  loops' own time  188 us (10%)
  matrix products  174 us (9%)
  starting transfers between devices  169 us (9%)
  other arithmetic  96.2 us (5%)
    gather x4, local copies, waits for them, and re-layouts, propagator(): return (kernel_real[offsets], kernel_imag[offsets])  816 us
    ppermute x38, waiting for transfers between devices, from_behind(): return lax.ppermute(value, axis, pairs)  210 us
    ppermute x38, starting transfers between devices, from_behind(): return lax.ppermute(value, axis, pairs)  160 us
    another operation x19, loops' own time, backward_tick(): lax.cond(active, backward_run_batch, backward_skip_batch, (grad_ext, prob...  123 us
    dynamic_update_slice x16, local copies, waits for them, and re-layouts, add_window(): return lax.dynamic_update_slice(grad_ext, current + values, start)  101 us
    dot_general x128, matrix products, right(): jnp.einsum('bjl,ls->bjs', field, matrix, precision=lax.Precision.HIGHEST)  97.7 us
    dot_general x128, matrix products, left(): jnp.einsum('jl,bls->bjs', matrix, field, precision=lax.Precision.HIGHEST)  76.5 us
    psum x1, waiting for transfers between devices, per_device(): tile_total = lax.psum(probe_part.astype(jnp.bfloat16), 'lat')  69.9 us
  transfers between devices with their start and end apart: 42, of which 40 were waited for; matrix products, arithmetic and copies ran while one was open for 43% of the time, Pallas kernels for 0%

commit v1 on v0

v1 whole, which is shorter than its diff:
```python
import functools
import math

import jax
import jax.numpy as jnp
import ml_dtypes
import numpy as np
from jax import lax
from jax.experimental import pallas as pl
from jax.experimental.pallas import tpu as pltpu
from jax.sharding import PartitionSpec as P

defocus_scale = 0.7
gain = 1.457627118644068 * np.exp(0.14208207981059368j)
f32 = jnp.float32
bf16 = jnp.bfloat16
CHUNK = 16
VMEM_LIMIT = 56 * 2**20


def propagator(size):
    index = np.arange(size)
    signed = np.where(index < size // 2, index, index - size).astype(np.float64)
    chirp = -math.pi * defocus_scale * signed * signed / size
    angles = 2.0 * math.pi * ((index[:, None] * index[None, :]) % size) / size + chirp[None, :]
    kernel = np.exp(1j * angles).sum(axis=1) / size
    return kernel[(index[:, None] - index[None, :]) % size] * gain


def sides(size):
    matrix = propagator(size)
    real, imag = matrix.real, matrix.imag
    right = np.block([[real, imag], [-imag, real]])
    left = np.block([[real, -imag], [imag, real]])
    return right.astype(ml_dtypes.bfloat16), left.astype(ml_dtypes.bfloat16)


def propagate(x, right, left, z_ref):
    w = right.shape[0] // 2
    z = jnp.dot(x, right, preferred_element_type=f32)
    z_ref[:w] = z[:, :w].astype(bf16)
    z_ref[w:] = z[:, w:].astype(bf16)
    y = jnp.dot(left, z_ref[...], preferred_element_type=f32)
    return y[:w], y[w:]


def masks(meta_ref, p, chunk, w):
    r = meta_ref[2 + 2 * p]
    q = meta_ref[3 + 2 * p]
    rows = lax.broadcasted_iota(jnp.int32, (CHUNK, w), 0) + chunk * CHUNK
    cols = lax.broadcasted_iota(jnp.int32, (CHUNK, w), 1)
    return rows < r, cols < q


def window(ext_ref, at, plane, chunk, halo_row, right_col):
    w = halo_row.shape[1]
    start = pl.multiple_of(chunk * CHUNK, CHUNK)
    own = ext_ref[at, plane, pl.ds(start, CHUNK), :].astype(f32)
    halo = ext_ref[at, plane, pl.ds(w + start, CHUNK), :].astype(f32)
    own = jnp.where(right_col, own[:, w:], own[:, :w])
    halo = jnp.where(right_col, halo[:, w:], halo[:, :w])
    return jnp.where(halo_row, halo, own)


def times_window(meta_ref, ext_ref, at, probes, w, read, write):
    def step(chunk, _):
        rows = pl.ds(pl.multiple_of(chunk * CHUNK, CHUNK), CHUNK)
        for p in range(probes):
            halo_row, right_col = masks(meta_ref, p, chunk, w)
            wr = window(ext_ref, at, 0, chunk, halo_row, right_col)
            wi = window(ext_ref, at, 1, chunk, halo_row, right_col)
            ar, ai = read(p, rows)
            write(p, rows, ar * wr - ai * wi, ar * wi + ai * wr)
        return 0

    lax.fori_loop(0, w // CHUNK, step, 0)


def add_gradients(meta_ref, g_ref, at, probes, w, read_a, read_b):
    def step(chunk, _):
        rows = pl.ds(pl.multiple_of(chunk * CHUNK, CHUNK), CHUNK)
        sums = [[[None, None], [None, None]], [[None, None], [None, None]]]
        for p in range(probes):
            halo_row, right_col = masks(meta_ref, p, chunk, w)
            ar, ai = read_a(p, rows)
            br, bi = read_b(p, rows)
            planes = (ar * br - ai * bi, -(ar * bi + ai * br))
            for plane in range(2):
                whole = planes[plane]
                halo = jnp.where(halo_row, whole, 0.0)
                parts = (whole - halo, halo)
                for tile in range(2):
                    right = jnp.where(right_col, parts[tile], 0.0)
                    for col, part in enumerate((parts[tile] - right, right)):
                        old = sums[plane][tile][col]
                        sums[plane][tile][col] = part if old is None else old + part
        for plane in range(2):
            for tile in range(2):
                at_rows = pl.ds(pl.multiple_of(tile * w + chunk * CHUNK, CHUNK), CHUNK)
                for col in range(2):
                    g_ref[at, plane, at_rows, col * w : (col + 1) * w] = sums[plane][tile][
                        col
                    ].astype(bf16)
        return 0

    lax.fori_loop(0, w // CHUNK, step, 0)


def slot_of(meta_ref, depth, order):
    d = meta_ref[0]
    high = (d >= depth // 2).astype(jnp.int32)
    return jnp.bitwise_xor(jnp.bitwise_xor(order, high * (depth - 1)), d)


def start_kernel(probes, scale, meta_ref, probe_ref, cot_ref, right_ref, left_ref, init_ref, x_ref, z_ref):
    w = probe_ref.shape[-1]
    high = meta_ref[1]
    kr, ki = float(scale.real), float(scale.imag)
    for p in range(probes):
        r = meta_ref[2 + 2 * p]
        q = lax.rem(meta_ref[3 + 2 * p], w)

        def moved(plane):
            return pltpu.roll(pltpu.roll(plane, r, 0), q, 1)

        init_ref[high, p, 0] = moved(probe_ref[0])
        init_ref[high, p, 1] = moved(probe_ref[1])
        lr = moved(cot_ref[p, 0])
        li = moved(cot_ref[p, 1])
        x_ref[:, :w] = (kr * lr + ki * li).astype(bf16)
        x_ref[:, w:] = (ki * lr - kr * li).astype(bf16)
        yr, yi = propagate(x_ref[...], right_ref[...], left_ref[...], z_ref)
        init_ref[1 - high, p, 0] = yr
        init_ref[1 - high, p, 1] = yi


def load_pieces(pieces, piece_refs, ext_ref, sems, w):
    copies = []
    for number, (at, tile, plane) in enumerate(pieces):
        rows = pl.ds(tile * w, w)
        dst = ext_ref.at[at, :, rows, :] if plane is None else ext_ref.at[at, plane, rows, :]
        copies.append(pltpu.make_async_copy(piece_refs[number], dst, sems.at[number]))
    for copy in copies:
        copy.start()
    return copies


def first_kernel(probes, depth, pieces, meta_ref, init_ref, right_ref, left_ref, *refs):
    n = len(pieces)
    piece_refs, (a_ref, ext_ref, x_ref, z_ref, sems) = refs[:n], refs[n:]
    w = init_ref.shape[-1]
    half = depth // 2
    for copy in load_pieces(pieces, piece_refs, ext_ref, sems, w):
        copy.wait()

    def write(p, rows, xr, xi):
        x_ref[p, rows, :w] = xr.astype(bf16)
        x_ref[p, rows, w:] = xi.astype(bf16)

    def step(k, _):
        at = slot_of(meta_ref, depth, k)

        def read(p, rows):
            return a_ref[k, p, 0, rows, :], a_ref[k, p, 1, rows, :]

        times_window(meta_ref, ext_ref, at, probes, w, read, write)
        for p in range(probes):
            yr, yi = propagate(x_ref[p], right_ref[...], left_ref[...], z_ref.at[p])
            a_ref[k + 1, p, 0] = yr
            a_ref[k + 1, p, 1] = yi
        return 0

    a_ref[0] = init_ref[0]
    lax.fori_loop(0, half, step, 0)


def add_probe_gradient(meta_ref, ext_ref, at, probes, w, depth, read, lam_ref, m_ref):
    d = meta_ref[0]

    def write(p, rows, xr, xi):
        m_ref[p, 0, rows, :] = xr
        m_ref[p, 1, rows, :] = -xi

    times_window(meta_ref, ext_ref, at, probes, w, read, write)
    for plane in range(2):
        total = None
        for p in range(probes):
            r = meta_ref[2 + 2 * p]
            q = meta_ref[3 + 2 * p]
            back = pltpu.roll(
                pltpu.roll(m_ref[p, plane], lax.rem(w - r, w), 0), lax.rem(2 * w - q, w), 1
            )
            total = back if total is None else total + back
        m_ref[0, plane] = total
    rows = w // depth
    for slot in range(depth):
        block = pl.multiple_of(jnp.bitwise_xor(d, slot) * rows, rows)
        for plane in range(2):
            lam_ref[slot, plane] = m_ref[0, plane, pl.ds(block, rows), :]


def second_kernel(probes, depth, pieces, meta_ref, init_ref, a_in_ref, right_ref, left_ref, *refs):
    n = len(pieces)
    half = depth // 2
    piece_refs, refs = refs[:n], refs[n:]
    g_refs, refs = refs[:half], refs[half:]
    (next_ref, lam_ref, ext_ref, g_ref, a_ref, b_ref, x_ref, z_ref, sems, out_sems) = refs
    w = init_ref.shape[-1]
    copies = load_pieces(pieces, piece_refs, ext_ref, sems, w)
    a_ref[0] = a_in_ref[0]
    b_ref[...] = init_ref[0]
    for copy in copies:
        copy.wait()

    def write(p, rows, xr, xi):
        x_ref[p, rows, :w] = xr.astype(bf16)
        x_ref[p, rows, w:] = xi.astype(bf16)

    def slot(order):
        return slot_of(meta_ref, depth, order) - half

    def read_a(k):
        return lambda p, rows: (a_ref[k, p, 0, rows, :], a_ref[k, p, 1, rows, :])

    def read_b(p, rows):
        return b_ref[p, 0, rows, :], b_ref[p, 1, rows, :]

    def a_step(k, _):
        times_window(meta_ref, ext_ref, slot(half + k), probes, w, read_a(k), write)
        for p in range(probes):
            yr, yi = propagate(x_ref[p], right_ref[...], left_ref[...], z_ref.at[p])
            a_ref[k + 1, p, 0] = yr
            a_ref[k + 1, p, 1] = yi
        return 0

    lax.fori_loop(0, half - 1, a_step, 0)

    def b_step(k, _):
        at = slot(depth - 1 - k)
        add_gradients(meta_ref, g_ref, at, probes, w, read_a(half - 1 - k), read_b)
        times_window(meta_ref, ext_ref, at, probes, w, read_b, write)

        @pl.when(k < half - 1)
        def _():
            for p in range(probes):
                yr, yi = propagate(x_ref[p], right_ref[...], left_ref[...], z_ref.at[p])
                b_ref[p, 0] = yr
                b_ref[p, 1] = yi

        return 0

    lax.fori_loop(0, half, b_step, 0)
    outs = [pltpu.make_async_copy(g_ref.at[i], g_refs[i], out_sems.at[i]) for i in range(half)]
    for copy in outs:
        copy.start()
    next_ref[...] = x_ref[...]
    high = meta_ref[1]

    @pl.when(high == 1)
    def _():
        add_probe_gradient(
            meta_ref, ext_ref, slot(depth - 1), probes, w, depth, read_a(half - 1), lam_ref, b_ref
        )

    @pl.when(high == 0)
    def _():
        lam_ref[...] = jnp.zeros(lam_ref.shape, f32)

    for copy in outs:
        copy.wait()


def third_kernel(probes, depth, pieces, meta_ref, next_ref, a_ref, lam_in_ref, right_ref, left_ref, *refs):
    n = len(pieces)
    half = depth // 2
    piece_refs, refs = refs[:n], refs[n:]
    g_refs, refs = refs[:half], refs[half:]
    (lam_ref, ext_ref, g_ref, b_ref, x_ref, z_ref, sems, out_sems) = refs
    w = a_ref.shape[-1]
    copies = load_pieces(pieces, piece_refs, ext_ref, sems, w)
    x_ref[...] = next_ref[...]
    for copy in copies:
        copy.wait()

    def write(p, rows, xr, xi):
        x_ref[p, rows, :w] = xr.astype(bf16)
        x_ref[p, rows, w:] = xi.astype(bf16)

    def read_b(p, rows):
        return b_ref[p, 0, rows, :], b_ref[p, 1, rows, :]

    def b_step(k, _):
        for p in range(probes):
            yr, yi = propagate(x_ref[p], right_ref[...], left_ref[...], z_ref.at[p])
            b_ref[p, 0] = yr
            b_ref[p, 1] = yi
        order = half - 1 - k
        at = slot_of(meta_ref, depth, order)

        def read_a(p, rows):
            return a_ref[order, p, 0, rows, :], a_ref[order, p, 1, rows, :]

        add_gradients(meta_ref, g_ref, at, probes, w, read_a, read_b)

        @pl.when(k < half - 1)
        def _():
            times_window(meta_ref, ext_ref, at, probes, w, read_b, write)

        return 0

    lax.fori_loop(0, half, b_step, 0)
    outs = [pltpu.make_async_copy(g_ref.at[i], g_refs[i], out_sems.at[i]) for i in range(half)]
    for copy in outs:
        copy.start()
    high = meta_ref[1]

    @pl.when(high == 0)
    def _():
        at = slot_of(meta_ref, depth, 0)
        add_probe_gradient(meta_ref, ext_ref, at, probes, w, depth, read_b, lam_ref, b_ref)

    @pl.when(high == 1)
    def _():
        lam_ref[...] = lam_in_ref[...]

    for copy in outs:
        copy.wait()


def cost(probes, steps, w):
    return pl.CostEstimate(
        flops=probes * steps * 16 * w**3, bytes_accessed=8 * 2**20, transcendentals=0
    )


def per_device(obj_slices, probe, positions, exit_cotangent):
    depth = lax.axis_size("depth")
    lat = lax.axis_size("lat")
    d = lax.axis_index("depth")
    w = probe.shape[-1]
    columns = obj_slices.shape[-1]
    half = depth // 2
    probes = positions.shape[0] // depth
    bits = [1 << i for i in range(depth.bit_length() - 1)]

    def across(value, bit):
        return lax.ppermute(value, "depth", [(i, i ^ bit) for i in range(depth)])

    def along(value, steps):
        return lax.ppermute(value, "lat", [(i, (i + steps) % lat) for i in range(lat)])

    def along_xor(value, bit):
        return lax.ppermute(value, "lat", [(i, i ^ bit) for i in range(lat)])

    right, left = sides(w)
    right, left = jnp.asarray(right), jnp.asarray(left)
    scale = gain ** (-2 * depth)

    my_positions = lax.dynamic_slice(positions, (d * probes, 0), (probes, 2))
    meta = jnp.concatenate(
        [jnp.stack([d, (d >= half).astype(jnp.int32)]).astype(jnp.int32), my_positions.reshape(-1)]
    )
    cotangent = lax.dynamic_slice_in_dim(exit_cotangent, d * probes, probes, 0)

    own = obj_slices[0].astype(bf16)
    tiles = {0: own}
    halos = {0: along(own, -1)}
    for bit in reversed(bits[1:]):
        for slot in sorted(tiles):
            tiles[slot | bit] = across(tiles[slot], bit)
        for slot in sorted(s for s in tiles if s & bit):
            kept = halos[slot ^ bit]
            kept = kept if isinstance(kept, tuple) else (kept[0], kept[1])
            halos[slot] = (across(kept[0], bit), along(tiles[slot][1], -1))
    for slot in sorted(tiles):
        tiles[slot | 1] = across(tiles[slot], 1)
        halos[slot | 1] = jax.tree.map(lambda x: across(x, 1), halos[slot])

    def pieces_of(slots, base):
        names, arrays = [], []
        for slot in slots:
            names.append((slot - base, 0, None))
            arrays.append(tiles[slot])
            if isinstance(halos[slot], tuple):
                for plane in range(2):
                    names.append((slot - base, 1, plane))
                    arrays.append(halos[slot][plane])
            else:
                names.append((slot - base, 1, None))
                arrays.append(halos[slot])
        return names, arrays

    smem = pl.BlockSpec(memory_space=pltpu.SMEM)
    vmem = pl.BlockSpec(memory_space=pltpu.VMEM)
    anywhere = pl.BlockSpec(memory_space=pl.ANY)
    params = pltpu.CompilerParams(vmem_limit_bytes=VMEM_LIMIT)
    wave = (probes, 2, w, w)
    x_scratch = pltpu.VMEM((probes, w, 2 * w), bf16)
    z_scratch = pltpu.VMEM((probes, 2 * w, w), bf16)
    ext_scratch = pltpu.VMEM((half, 2, 2 * w, columns), bf16)
    g_shape = (2, 2 * w, columns)
    lam_shape = (depth, 2, w // depth, w)

    init = pl.pallas_call(
        functools.partial(start_kernel, probes, scale),
        out_shape=jax.ShapeDtypeStruct((2,) + wave, f32),
        in_specs=[smem, vmem, vmem, vmem, vmem],
        out_specs=vmem,
        scratch_shapes=[pltpu.VMEM((w, 2 * w), bf16), pltpu.VMEM((2 * w, w), bf16)],
        compiler_params=params,
        cost_estimate=cost(probes, 1, w),
    )(meta, probe, cotangent, right, left)

    names, arrays = pieces_of(range(half), 0)
    a_waves = pl.pallas_call(
        functools.partial(first_kernel, probes, depth, names),
        out_shape=jax.ShapeDtypeStruct((half + 1,) + wave, f32),
        grid=(1,),
        in_specs=[smem, pl.BlockSpec((1,) + wave, lambda i: (0, 0, 0, 0, 0)), vmem, vmem]
        + [anywhere] * len(names),
        out_specs=vmem,
        scratch_shapes=[
            ext_scratch,
            x_scratch,
            z_scratch,
            pltpu.SemaphoreType.DMA((len(names),)),
        ],
        compiler_params=params,
        cost_estimate=cost(probes, half, w),
    )(meta, init, right, left, *arrays)

    other_names, other_arrays = pieces_of(range(half, depth), half)
    results = pl.pallas_call(
        functools.partial(second_kernel, probes, depth, other_names),
        out_shape=[jax.ShapeDtypeStruct(g_shape, bf16)] * half
        + [
            jax.ShapeDtypeStruct((probes, w, 2 * w), bf16),
            jax.ShapeDtypeStruct(lam_shape, f32),
        ],
        grid=(1,),
        in_specs=[
            smem,
            pl.BlockSpec((1,) + wave, lambda i: (1, 0, 0, 0, 0)),
            pl.BlockSpec((1,) + wave, lambda i: (half, 0, 0, 0, 0)),
            vmem,
            vmem,
        ]
        + [anywhere] * len(other_names),
        out_specs=[anywhere] * half + [vmem, vmem],
        scratch_shapes=[
            ext_scratch,
            pltpu.VMEM((half,) + g_shape, bf16),
            pltpu.VMEM((half,) + wave, f32),
            pltpu.VMEM(wave, f32),
            x_scratch,
            z_scratch,
            pltpu.SemaphoreType.DMA((len(other_names),)),
            pltpu.SemaphoreType.DMA((half,)),
        ],
        compiler_params=params,
        cost_estimate=cost(probes, half, w),
    )(meta, init, a_waves, right, left, *other_arrays)
    far_grads, next_x, lam = results[:half], results[half], results[half + 1]

    results = pl.pallas_call(
        functools.partial(third_kernel, probes, depth, names),
        out_shape=[jax.ShapeDtypeStruct(g_shape, bf16)] * half
        + [jax.ShapeDtypeStruct(lam_shape, f32)],
        grid=(1,),
        in_specs=[
            smem,
            vmem,
            pl.BlockSpec((half,) + wave, lambda i: (0, 0, 0, 0, 0)),
            vmem,
            vmem,
            vmem,
        ]
        + [anywhere] * len(names),
        out_specs=[anywhere] * half + [vmem],
        scratch_shapes=[
            ext_scratch,
            pltpu.VMEM((half,) + g_shape, bf16),
            pltpu.VMEM(wave, f32),
            x_scratch,
            z_scratch,
            pltpu.SemaphoreType.DMA((len(names),)),
            pltpu.SemaphoreType.DMA((half,)),
        ],
        compiler_params=params,
        cost_estimate=cost(probes, half, w),
    )(meta, next_x, a_waves, lam, right, left, *arrays)
    near_grads, lam = results[:half], results[half]

    def total(first, second):
        return (first.astype(f32) + second.astype(f32)).astype(bf16)

    grads = {slot: g for slot, g in enumerate(list(near_grads) + list(far_grads))}
    owns, halo_grads = {}, {}
    for slot in sorted((s for s in grads if not s & 1), reverse=True):
        both = total(grads[slot], across(grads[slot | 1], 1))
        owns[slot] = both[:, :w]
        halo_grads[slot] = (both[0, w:], both[1, w:])
    for bit in bits[1:]:
        for slot in sorted((s for s in owns if s & bit), reverse=True):
            halo_real, halo_imag = halo_grads.pop(slot)
            kept = halo_grads[slot ^ bit]
            halo_grads[slot ^ bit] = (total(kept[0], across(halo_real, bit)), kept[1])
            shifted_imag = along(halo_imag, 1)
            sent = owns.pop(slot)
            sent = jnp.stack([sent[0], total(sent[1], shifted_imag)])
            owns[slot ^ bit] = total(owns[slot ^ bit], across(sent, bit))
    from_below = along(jnp.stack(halo_grads[0]), 1)
    object_grad = (owns[0].astype(f32) + from_below.astype(f32))[None]

    part = lam
    for bit in reversed(bits):
        part = part[:bit] + across(part[bit : 2 * bit].astype(bf16), bit).astype(f32)
    part = part[0]
    if lat & (lat - 1):
        part = lax.psum(part, "lat")
    else:
        for bit in [1 << i for i in range(lat.bit_length() - 1)]:
            sent = part.astype(bf16)
            part = sent.astype(f32) + along_xor(sent, bit).astype(f32)
    return (object_grad, part)


def solution(mesh):
    placed = (P("depth", None, "lat", None), P(), P("lat", None), P("lat", None, None, None))
    return jax.shard_map(
        per_device,
        mesh=mesh,
        in_specs=placed,
        out_specs=(P("depth", None, "lat", None), P(None, "depth", None)),
        check_vma=False,
    )
```

time: 1920 us -> 122 us (0.06)
  local copies, waits for them, and re-layouts: 967 us -> 7.89 us
  waiting for transfers between devices: 299 us -> 40 us
  loops' own time: 188 us -> 0 us
  matrix products: 174 us -> 0 us
  starting transfers between devices: 169 us -> 22.4 us
  other arithmetic: 96.2 us -> 5.64 us
  Pallas kernels: 0 us -> 45.1 us
    gather x4 -> x0, local copies, waits for them, and re-layouts: 816 us -> none  [propagator(): return (kernel_real[offsets], kernel_imag[offsets])]
    another operation x40 -> x0, loops' own time: 188 us -> none  [the longest x19 123 us: backward_tick(): lax.cond(active, backward_run_batch, backward_skip_batch, (grad_ext, prob...]
    dot_general x256 -> x0, matrix products: 174 us -> none  [the longest x128 97.7 us: right(): jnp.einsum('bjl,ls->bjs', field, matrix, precision=lax.Precision.HIGHEST)]
    ppermute x40 -> x20, waiting for transfers between devices: 210 us -> 40 us  [the longest x13 20.2 us: across(): return lax.ppermute(value, 'depth', [(i, i ^ bit) for i in range(depth)])]
    ppermute x40 -> x20, starting transfers between devices: 169 us -> 22.4 us  [the longest x13 10.5 us: across(): return lax.ppermute(value, 'depth', [(i, i ^ bit) for i in range(depth)])]
    dynamic_update_slice x16 -> x0, local copies, waits for them, and re-layouts: 101 us -> none  [add_window(): return lax.dynamic_update_slice(grad_ext, current + values, start)]
    psum x1 -> x0, waiting for transfers between devices: 69.9 us -> none  [per_device(): tile_total = lax.psum(probe_part.astype(jnp.bfloat16), 'lat')]
    add x49 -> x2, other arithmetic: 59.9 us -> 1.64 us  [the longest x1 0.97 us: per_device(): part = part[:bit] + across(part[bit:2 * bit].astype(bf16), bit).astype(f32)]
  transfers between devices with their start and end apart: 42 -> 20, of which waited for: 40 -> 9; matrix products, arithmetic and copies ran while one was open for 43% -> 6% of each run, Pallas kernels for 0% -> 26%
where the time goes in v1:
time: 122 us
  Pallas kernels  45.1 us (37%)
  waiting for transfers between devices  40 us (33%)
  starting transfers between devices  22.4 us (18%)
  local copies, waits for them, and re-layouts  7.89 us (6%)
  other arithmetic  5.64 us (5%)
    ppermute x13, waiting for transfers between devices, across(): return lax.ppermute(value, 'depth', [(i, i ^ bit) for i in range(depth)])  20.2 us
    pallas_call x1, Pallas kernels, per_device(): pl.pallas_call(functools.partial(second_kernel, probes, depth, other_name...  14 us
    pallas_call x1, Pallas kernels, per_device(): pl.pallas_call(functools.partial(third_kernel, probes, depth, names), out...  13.1 us
    ppermute x4, waiting for transfers between devices, along(): lax.ppermute(value, 'lat', [(i, (i + steps) % lat) for i in range(lat)])  12.1 us
    pallas_call x1, Pallas kernels, per_device(): pl.pallas_call(functools.partial(first_kernel, probes, depth, names), out...  10.8 us
    ppermute x13, starting transfers between devices, across(): return lax.ppermute(value, 'depth', [(i, i ^ bit) for i in range(depth)])  10.5 us
    ppermute x4, starting transfers between devices, along(): lax.ppermute(value, 'lat', [(i, (i + steps) % lat) for i in range(lat)])  10 us
    ppermute x3, waiting for transfers between devices, along_xor(): return lax.ppermute(value, 'lat', [(i, i ^ bit) for i in range(lat)])  7.74 us
  transfers between devices with their start and end apart: 20, of which 9 were waited for; matrix products, arithmetic and copies ran while one was open for 6% of the time, Pallas kernels for 26%

profile of v1, /device:TPU:0, one launch (start us, length us, event | category | flops | bytes accessed | tf_op | source)
XLA Modules:
  0.0 121.9 jit_solution(1710673699924005325)
XLA Ops:
  0.6 0.0 copy-start
  0.6 1.3 %convert_bitcast_fusion.refs_0_ = bf16[2,256,512]{2,1,0:T(8,128)(2,1)S(1)} fusion(f32[1,2,256,512]{3,2,1,0:T(8,128)} %param.6), kind=kLoop, calls=%fused_computation.10 | loop fusion | flops 262144 | bytes 1572864 | tf_op jit(solution)/shard_map/convert_element_type | solution.py:365
  2.0 3.0 %collective-permute-start.3 = (bf16[2,256,512]{2,1,0:T(8,128)(2,1)S(1)}, bf16[2,256,512]{2,1,0:T(8,128)(2,1)S(1)}, u32[]{:S(2)}, u32[]{:S(2)}) collective-permute-start(bf16[2,256,512]{2,1,0:T(8,128)(2,1)S(1)} %convert_bitcast_fusion.refs_0_), channel_id=1, source_target_pairs={{0,16},{8,24},{16,0},{24,8},{1,17},{9,25},{17,1},{25,9},{2,18},{10... | collective-permute-start | bytes 1572872 | tf_op jit(solution)/shard_map/ppermute | solution.py:347
  5.0 4.5 %collective-permute-start = (bf16[2,256,512]{2,1,0:T(8,128)(2,1)S(1)}, bf16[2,256,512]{2,1,0:T(8,128)(2,1)S(1)}, u32[]{:S(2)}, u32[]{:S(2)}) collective-permute-start(bf16[2,256,512]{2,1,0:T(8,128)(2,1)S(1)} %convert_bitcast_fusion.refs_0_), channel_id=1, source_target_pairs={{0,7},{1,0},{2,1},{3,2},{4,3},{5,4},{6,5},{7,6},{8,15},{9,8},{10,9... | collective-permute-start | bytes 1572872 | tf_op jit(solution)/shard_map/ppermute | solution.py:350
  9.5 0.0 collective-permute-start.1
  9.5 0.1 constant_dynamic-slice_fusion.1
  9.6 0.1 copy.9
  9.7 0.1 reshape.13
  9.8 7.1 %collective-permute-done.3.refs_0_ = bf16[2,256,512]{2,1,0:T(8,128)(2,1)S(1)} collective-permute-done((bf16[2,256,512]{2,1,0:T(8,128)(2,1)S(1)}, bf16[2,256,512]{2,1,0:T(8,128)(2,1)S(1)}, u32[]{:S(2)}, u32[]{:S(2)}) %collective-permute-start.3) | collective-permute-done | bytes 524320 | tf_op jit(solution)/shard_map/ppermute | solution.py:347
  16.9 4.8 %collective-permute-start.5 = (bf16[256,512]{1,0:T(8,128)(2,1)S(1)}, bf16[256,512]{1,0:T(8,128)(2,1)S(1)}, u32[]{:S(2)}, u32[]{:S(2)}) collective-permute-start(bf16[256,512]{1,0:T(8,128)(2,1)S(1)} %slice_bitcast_fusion.4), channel_id=1, source_target_pairs={{0,7},{1,0},{2,1},{3,2},{4,3},{5,4},{6,5},{7,6},{8,15},{9,8},{10,9... | collective-permute-start | bytes 786440 | tf_op jit(solution)/shard_map/ppermute | solution.py:350
  21.7 0.0 collective-permute-done.refs_1_
  21.7 0.0 collective-permute-start.2
  21.8 1.6 %collective-permute-start.4 = (bf16[256,512]{1,0:T(8,128)(2,1)S(1)}, bf16[256,512]{1,0:T(8,128)(2,1)S(1)}, u32[]{:S(2)}, u32[]{:S(2)}) collective-permute-start(bf16[256,512]{1,0:T(8,128)(2,1)S(1)} %slice_bitcast_fusion.5), channel_id=1, source_target_pairs={{0,16},{8,24},{16,0},{24,8},{1,17},{9,25},{17,1},{25,9},{2,18},{10... | collective-permute-start | bytes 786440 | tf_op jit(solution)/shard_map/ppermute | solution.py:347
  23.4 0.2 collective-permute-start.6
  23.6 0.7 pad_add_fusion.meta_ref
  24.2 3.1 %constant_dynamic-slice_fusion.cot_ref = f32[4,2,256,256]{3,2,1,0:T(8,128)} fusion(f32[16,2,256,256]{3,2,1,0:T(8,128)} %param.9, s32[]{:T(128)S(6)} %select_n.4), kind=kLoop, calls=%fused_computation.29 | loop fusion | bytes 4194308 | tf_op jit(solution)/shard_map/dynamic_slice | solution.py:363
  27.3 0.0 collective-permute-done.5.refs_2_
  27.3 0.4 collective-permute-start.8
  27.7 2.9 %collective-permute-done.4.refs_1_ = bf16[256,512]{1,0:T(8,128)(2,1)S(1)} collective-permute-done((bf16[256,512]{1,0:T(8,128)(2,1)S(1)}, bf16[256,512]{1,0:T(8,128)(2,1)S(1)}, u32[]{:S(2)}, u32[]{:S(2)}) %collective-permute-start.4) | collective-permute-done | bytes 262176 | tf_op jit(solution)/shard_map/ppermute | solution.py:347
  30.6 0.0 collective-permute-start.7
  30.6 7.3 %shard_map.77.init_ref = f32[2,4,2,256,256]{4,3,2,1,0:T(8,128)} custom-call(s32[10]{0:T(128)} %pad_add_fusion.meta_ref, f32[2,256,256]{2,1,0:T(8,128)} %probe_ref.1, f32[4,2,256,256]{3,2,1,0:T(8,128)} %constant_dynamic-slice_fusion.cot_ref, bf16[512,512]{1,0:T(8,128)(2,1)} %constant.17.clone.right_ref, bf16[512,512]{1,0:T(8,128)(2,1)} %constant.18.clone.left_ref), custom_call_target="tpu_custom_call" | custom-call | flops 1073741824 | bytes 8388608 | tf_op jit(solution)/shard_map/pallas_call | solution.py:404
  37.8 0.0 collective-permute-done.1.refs_2_
  37.9 0.0 collective-permute-done.2.refs_3_
  37.9 0.8 copy-done.3
  38.6 0.8 copy-done.4
  39.4 10.8 %shard_map.78.a_in_ref.a_ref = f32[3,4,2,256,256]{4,3,2,1,0:T(8,128)} custom-call(s32[10]{0:T(128)} %pad_add_fusion.meta_ref, f32[2,4,2,256,256]{4,3,2,1,0:T(8,128)} %shard_map.77.init_ref, bf16[512,512]{1,0:T(8,128)(2,1)} %constant.17.clone.right_ref, bf16[512,512]{1,0:T(8,128)(2,1)} %constant.18.clone.left_ref, bf16[2,256,512]{2,1,0:T(8,128)(2,1)} %copy-done.1, ...), custom_call_target="tpu_custom_call" | custom-call | flops 2147483648 | bytes 8388608 | tf_op jit(solution)/shard_map/pallas_call | solution.py:415
  50.2 0.0 collective-permute-done.8.refs_5_
  50.2 0.0 collective-permute-done.6.refs_3_
  50.2 0.7 copy-done.11
  50.9 0.2 copy-done.8
  51.1 0.7 copy-done.12
  51.8 14.0 %shard_map.79 = (bf16[2,512,512]{2,1,0:T(8,128)(2,1)}, bf16[2,512,512]{2,1,0:T(8,128)(2,1)}, bf16[4,256,512]{2,1,0:T(8,128)(2,1)}, f32[4,2,64,256]{3,2,1,0:T(8,128)}) custom-call(s32[10]{0:T(128)} %pad_add_fusion.meta_ref, f32[2,4,2,256,256]{4,3,2,1,0:T(8,128)} %shard_map.77.init_ref, f32[3,4,2,256,256]{4,3,2,1,0:T(8,128)} %shard_map.78.a_in_ref.a_ref, ...), custom_call_target="tpu_custom_call" | custom-call | flops 2147483648 | bytes 8388608 | tf_op jit(solution)/shard_map/pallas_call | solution.py:433
  65.8 0.5 collective-permute-start.10
  66.3 13.1 %shard_map.80 = (bf16[2,512,512]{2,1,0:T(8,128)(2,1)}, bf16[2,512,512]{2,1,0:T(8,128)(2,1)}, f32[4,2,64,256]{3,2,1,0:T(8,128)}) custom-call(s32[10]{0:T(128)} %pad_add_fusion.meta_ref, bf16[4,256,512]{2,1,0:T(8,128)(2,1)} %get-tuple-element.9.next_ref, f32[3,4,2,256,256]{4,3,2,1,0:T(8,128)} %shard_map.78.a_in_ref.a_ref, ...), custom_call_target="tpu_custom_call" | custom-call | flops 2147483648 | bytes 8388608 | tf_op jit(solution)/shard_map/pallas_call | solution.py:465
  79.4 0.0 copy-start.7
  79.4 1.1 slice.88
  80.4 1.5 %collective-permute-start.15 = (bf16[2,2,64,256]{3,2,1,0:T(8,128)(2,1)S(1)}, bf16[2,2,64,256]{3,2,1,0:T(8,128)(2,1)S(1)}, u32[]{:S(2)}, u32[]{:S(2)}) collective-permute-start(bf16[2,2,64,256]{3,2,1,0:T(8,128)(2,1)S(1)} %slice.88), channel_id=1, source_target_pairs={{0,16},{8,24},{16,0},{24,8},{1,17},{9,25},{17,1},{25,9},{2,18},{10... | collective-permute-start | bytes 393224 | tf_op jit(solution)/shard_map/ppermute | solution.py:347
  82.0 4.0 %collective-permute-done.15 = bf16[2,2,64,256]{3,2,1,0:T(8,128)(2,1)S(1)} collective-permute-done((bf16[2,2,64,256]{3,2,1,0:T(8,128)(2,1)S(1)}, bf16[2,2,64,256]{3,2,1,0:T(8,128)(2,1)S(1)}, u32[]{:S(2)}, u32[]{:S(2)}) %collective-permute-start.15) | collective-permute-done | bytes 131104 | tf_op jit(solution)/shard_map/ppermute | solution.py:347
  86.0 1.0 convert_add_fusion.2
  87.0 0.1 collective-permute-start.16
  87.1 0.5 collective-permute-start.9
  87.6 0.7 collective-permute-done.16
  88.3 0.1 collective-permute-start.17
  88.4 4.3 %collective-permute-done.17 = bf16[2,64,256]{2,1,0:T(8,128)(2,1)S(1)} collective-permute-done((bf16[2,64,256]{2,1,0:T(8,128)(2,1)S(1)}, bf16[2,64,256]{2,1,0:T(8,128)(2,1)S(1)}, u32[]{:S(2)}, u32[]{:S(2)}) %collective-permute-start.17) | collective-permute-done | bytes 65568 | tf_op jit(solution)/shard_map/ppermute | solution.py:353
  92.7 0.1 collective-permute-start.18
  92.8 0.3 add_convert_fusion
  93.1 0.1 fusion.6
  93.2 0.6 collective-permute-start.11
  93.8 0.2 copy-done.6
  94.0 0.3 add_convert_fusion.1
  94.3 1.5 %collective-permute-start.13 = (bf16[256,512]{1,0:T(8,128)(2,1)S(1)}, bf16[256,512]{1,0:T(8,128)(2,1)S(1)}, u32[]{:S(2)}, u32[]{:S(2)}) collective-permute-start(bf16[256,512]{1,0:T(8,128)(2,1)S(1)} %get-tuple-element.17), channel_id=1, source_target_pairs={{0,16},{8,24},{16,0},{24,8},{1,17},{9,25},{17,1},{25,9},{2,18},{10... | collective-permute-start | bytes 786440 | tf_op jit(solution)/shard_map/ppermute | solution.py:347
  95.9 7.9 %collective-permute-done.11 = bf16[256,512]{1,0:T(8,128)(2,1)S(1)} collective-permute-done((bf16[256,512]{1,0:T(8,128)(2,1)S(1)}, bf16[256,512]{1,0:T(8,128)(2,1)S(1)}, u32[]{:S(2)}, u32[]{:S(2)}) %collective-permute-start.11) | collective-permute-done | bytes 262176 | tf_op jit(solution)/shard_map/ppermute | solution.py:350
  103.8 0.1 fusion.2
  103.9 0.1 pad_maximum_fusion
  104.0 1.2 collective-permute-start.12
  105.1 0.1 fusion.3
  105.2 0.1 pad_maximum_fusion.1
  105.3 0.1 collective-permute-start.14
  105.4 1.7 %collective-permute-start.19 = (bf16[2,64,256]{2,1,0:T(8,128)(2,1)S(1)}, bf16[2,64,256]{2,1,0:T(8,128)(2,1)S(1)}, u32[]{:S(2)}, u32[]{:S(2)}) collective-permute-start(bf16[2,64,256]{2,1,0:T(8,128)(2,1)S(1)} %add_convert_fusion.3), channel_id=1, source_target_pairs={{0,4},{1,5},{2,6},{3,7},{4,0},{5,1},{6,2},{7,3},{8,12},{9,13},{10,... | collective-permute-start | bytes 196616 | tf_op jit(solution)/shard_map/ppermute | solution.py:353
  107.1 3.5 %collective-permute-done.19 = bf16[2,64,256]{2,1,0:T(8,128)(2,1)S(1)} collective-permute-done((bf16[2,64,256]{2,1,0:T(8,128)(2,1)S(1)}, bf16[2,64,256]{2,1,0:T(8,128)(2,1)S(1)}, u32[]{:S(2)}, u32[]{:S(2)}) %collective-permute-start.19) | collective-permute-done | bytes 65568 | tf_op jit(solution)/shard_map/ppermute | solution.py:353
  110.6 0.7 convert_add_fusion.3
  111.3 5.4 %collective-permute-done.12 = bf16[2,256,512]{2,1,0:T(8,128)(2,1)S(1)} collective-permute-done((bf16[2,256,512]{2,1,0:T(8,128)(2,1)S(1)}, bf16[2,256,512]{2,1,0:T(8,128)(2,1)S(1)}, u32[]{:S(2)}, u32[]{:S(2)}) %collective-permute-start.12) | collective-permute-done | bytes 524320 | tf_op jit(solution)/shard_map/ppermute | solution.py:347
  116.7 4.1 %collective-permute-done.14 = bf16[2,256,512]{2,1,0:T(8,128)(2,1)S(1)} collective-permute-done((bf16[2,256,512]{2,1,0:T(8,128)(2,1)S(1)}, bf16[2,256,512]{2,1,0:T(8,128)(2,1)S(1)}, u32[]{:S(2)}, u32[]{:S(2)}) %collective-permute-start.14) | collective-permute-done | bytes 524320 | tf_op jit(solution)/shard_map/ppermute | solution.py:350
  120.8 1.2 add_bitcast_fusion
  (30 shorter events, 0.2 us)
Async XLA Ops:
  0.6 8.9 %copy-start = (s32[16,2]{0,1:T(2,128)S(1)}, s32[16,2]{0,1:T(2,128)}, u32[]{:S(2)}) copy-start(s32[16,2]{0,1:T(2,128)} %param.8) | copy-start | bytes 388
  1.9 25.4 %copy-start.1 = (bf16[2,256,512]{2,1,0:T(8,128)(2,1)}, bf16[2,256,512]{2,1,0:T(8,128)(2,1)S(1)}, u32[]{:S(2)}) copy-start(bf16[2,256,512]{2,1,0:T(8,128)(2,1)S(1)} %convert_bitcast_fusion.refs_0_) | copy-start | bytes 1572868
  2.0 15.0 %collective-permute-start.3 = (bf16[2,256,512]{2,1,0:T(8,128)(2,1)S(1)}, bf16[2,256,512]{2,1,0:T(8,128)(2,1)S(1)}, u32[]{:S(2)}, u32[]{:S(2)}) collective-permute-start(bf16[2,256,512]{2,1,0:T(8,128)(2,1)S(1)} %convert_bitcast_fusion.refs_0_), channel_id=1, source_target_pairs={{0,16},{8,24},{16,0},{24,8},{1,17},{9,25},{17,1},{25,9},{2,18},{10... | collective-permute-start | bytes 1572872 | tf_op jit(solution)/shard_map/ppermute | solution.py:347
  5.0 16.8 %collective-permute-start = (bf16[2,256,512]{2,1,0:T(8,128)(2,1)S(1)}, bf16[2,256,512]{2,1,0:T(8,128)(2,1)S(1)}, u32[]{:S(2)}, u32[]{:S(2)}) collective-permute-start(bf16[2,256,512]{2,1,0:T(8,128)(2,1)S(1)} %convert_bitcast_fusion.refs_0_), channel_id=1, source_target_pairs={{0,7},{1,0},{2,1},{3,2},{4,3},{5,4},{6,5},{7,6},{8,15},{9,8},{10,9... | collective-permute-start | bytes 1572872 | tf_op jit(solution)/shard_map/ppermute | solution.py:350
  9.5 28.3 %collective-permute-start.1 = (bf16[2,256,512]{2,1,0:T(8,128)(2,1)S(1)}, bf16[2,256,512]{2,1,0:T(8,128)(2,1)S(1)}, u32[]{:S(2)}, u32[]{:S(2)}) collective-permute-start(bf16[2,256,512]{2,1,0:T(8,128)(2,1)S(1)} %convert_bitcast_fusion.refs_0_), channel_id=1, source_target_pairs={{0,8},{8,0},{16,24},{24,16},{1,9},{9,1},{17,25},{25,17},{2,10},{10... | collective-permute-start | bytes 1572872 | tf_op jit(solution)/shard_map/ppermute | solution.py:347
  16.9 10.4 %copy-start.5 = (bf16[2,256,512]{2,1,0:T(8,128)(2,1)}, bf16[2,256,512]{2,1,0:T(8,128)(2,1)S(1)}, u32[]{:S(2)}) copy-start(bf16[2,256,512]{2,1,0:T(8,128)(2,1)S(1)} %collective-permute-done.3.refs_0_) | copy-start | bytes 1572868
  16.9 10.4 %collective-permute-start.5 = (bf16[256,512]{1,0:T(8,128)(2,1)S(1)}, bf16[256,512]{1,0:T(8,128)(2,1)S(1)}, u32[]{:S(2)}, u32[]{:S(2)}) collective-permute-start(bf16[256,512]{1,0:T(8,128)(2,1)S(1)} %slice_bitcast_fusion.4), channel_id=1, source_target_pairs={{0,7},{1,0},{2,1},{3,2},{4,3},{5,4},{6,5},{7,6},{8,15},{9,8},{10,9... | collective-permute-start | bytes 786440 | tf_op jit(solution)/shard_map/ppermute | solution.py:350
  21.7 5.6 %copy-start.2 = (bf16[2,256,512]{2,1,0:T(8,128)(2,1)}, bf16[2,256,512]{2,1,0:T(8,128)(2,1)S(1)}, u32[]{:S(2)}) copy-start(bf16[2,256,512]{2,1,0:T(8,128)(2,1)S(1)} %collective-permute-done.refs_1_) | copy-start | bytes 1572868
  21.7 16.1 %collective-permute-start.2 = (bf16[2,256,512]{2,1,0:T(8,128)(2,1)S(1)}, bf16[2,256,512]{2,1,0:T(8,128)(2,1)S(1)}, u32[]{:S(2)}, u32[]{:S(2)}) collective-permute-start(bf16[2,256,512]{2,1,0:T(8,128)(2,1)S(1)} %collective-permute-done.refs_1_), channel_id=1, source_target_pairs={{0,8},{8,0},{16,24},{24,16},{1,9},{9,1},{17,25},{25,17},{2,10},{10... | collective-permute-start | bytes 1572872 | tf_op jit(solution)/shard_map/ppermute | solution.py:347
  21.8 8.8 %collective-permute-start.4 = (bf16[256,512]{1,0:T(8,128)(2,1)S(1)}, bf16[256,512]{1,0:T(8,128)(2,1)S(1)}, u32[]{:S(2)}, u32[]{:S(2)}) collective-permute-start(bf16[256,512]{1,0:T(8,128)(2,1)S(1)} %slice_bitcast_fusion.5), channel_id=1, source_target_pairs={{0,16},{8,24},{16,0},{24,8},{1,17},{9,25},{17,1},{25,9},{2,18},{10... | collective-permute-start | bytes 786440 | tf_op jit(solution)/shard_map/ppermute | solution.py:347
  23.4 26.9 %collective-permute-start.6 = (bf16[2,256,512]{2,1,0:T(8,128)(2,1)S(1)}, bf16[2,256,512]{2,1,0:T(8,128)(2,1)S(1)}, u32[]{:S(2)}, u32[]{:S(2)}) collective-permute-start(bf16[2,256,512]{2,1,0:T(8,128)(2,1)S(1)} %collective-permute-done.3.refs_0_), channel_id=1, source_target_pairs={{0,8},{8,0},{16,24},{24,16},{1,9},{9,1},{17,25},{25,17},{2,10},{10... | collective-permute-start | bytes 1572872 | tf_op jit(solution)/shard_map/ppermute | solution.py:347
  27.3 10.5 %copy-start.9 = (bf16[256,512]{1,0:T(8,128)(2,1)}, bf16[256,512]{1,0:T(8,128)(2,1)S(1)}, u32[]{:S(2)}) copy-start(bf16[256,512]{1,0:T(8,128)(2,1)S(1)} %collective-permute-done.5.refs_2_) | copy-start | bytes 786436
  27.3 22.9 %collective-permute-start.8 = (bf16[256,512]{1,0:T(8,128)(2,1)S(1)}, bf16[256,512]{1,0:T(8,128)(2,1)S(1)}, u32[]{:S(2)}, u32[]{:S(2)}) collective-permute-start(bf16[256,512]{1,0:T(8,128)(2,1)S(1)} %collective-permute-done.5.refs_2_), channel_id=1, source_target_pairs={{0,8},{8,0},{16,24},{24,16},{1,9},{9,1},{17,25},{25,17},{2,10},{10... | collective-permute-start | bytes 786440 | tf_op jit(solution)/shard_map/ppermute | solution.py:347
  30.6 7.3 %copy-start.10 = (bf16[256,512]{1,0:T(8,128)(2,1)}, bf16[256,512]{1,0:T(8,128)(2,1)S(1)}, u32[]{:S(2)}) copy-start(bf16[256,512]{1,0:T(8,128)(2,1)S(1)} %collective-permute-done.4.refs_1_) | copy-start | bytes 786436
  30.6 19.7 %collective-permute-start.7 = (bf16[256,512]{1,0:T(8,128)(2,1)S(1)}, bf16[256,512]{1,0:T(8,128)(2,1)S(1)}, u32[]{:S(2)}, u32[]{:S(2)}) collective-permute-start(bf16[256,512]{1,0:T(8,128)(2,1)S(1)} %collective-permute-done.4.refs_1_), channel_id=1, source_target_pairs={{0,8},{8,0},{16,24},{24,16},{1,9},{9,1},{17,25},{25,17},{2,10},{10... | collective-permute-start | bytes 786440 | tf_op jit(solution)/shard_map/ppermute | solution.py:347
  37.8 0.8 copy-start.3
  38.6 0.8 copy-start.4
  50.2 0.7 copy-start.11
  50.2 0.9 copy-start.8
  51.1 0.7 copy-start.12
  65.8 27.0 %collective-permute-start.10 = (bf16[2,512,512]{2,1,0:T(8,128)(2,1)}, bf16[2,512,512]{2,1,0:T(8,128)(2,1)S(1)}, u32[]{:S(2)}, u32[]{:S(2)}) collective-permute-start(bf16[2,512,512]{2,1,0:T(8,128)(2,1)} %get-tuple-element.14), channel_id=1, source_target_pairs={{0,8},{8,0},{16,24},{24,16},{1,9},{9,1},{17,25},{25,17},{2,10},{10... | collective-permute-start | bytes 3145736 | tf_op jit(solution)/shard_map/ppermute | solution.py:347
  79.4 13.4 %copy-start.7 = (bf16[2,512,512]{2,1,0:T(8,128)(2,1)S(1)}, bf16[2,512,512]{2,1,0:T(8,128)(2,1)}, u32[]{:S(2)}) copy-start(bf16[2,512,512]{2,1,0:T(8,128)(2,1)} %get-tuple-element.13) | copy-start | bytes 3145732
  80.4 5.6 %collective-permute-start.15 = (bf16[2,2,64,256]{3,2,1,0:T(8,128)(2,1)S(1)}, bf16[2,2,64,256]{3,2,1,0:T(8,128)(2,1)S(1)}, u32[]{:S(2)}, u32[]{:S(2)}) collective-permute-start(bf16[2,2,64,256]{3,2,1,0:T(8,128)(2,1)S(1)} %slice.88), channel_id=1, source_target_pairs={{0,16},{8,24},{16,0},{24,8},{1,17},{9,25},{17,1},{25,9},{2,18},{10... | collective-permute-start | bytes 393224 | tf_op jit(solution)/shard_map/ppermute | solution.py:347
  87.0 1.3 %collective-permute-start.16 = (bf16[1,2,64,256]{3,2,1,0:T(8,128)(2,1)S(1)}, bf16[1,2,64,256]{3,2,1,0:T(8,128)(2,1)S(1)}, u32[]{:S(2)}, u32[]{:S(2)}) collective-permute-start(bf16[1,2,64,256]{3,2,1,0:T(8,128)(2,1)S(1)} %slice.89), channel_id=1, source_target_pairs={{0,8},{8,0},{16,24},{24,16},{1,9},{9,1},{17,25},{25,17},{2,10},{10... | collective-permute-start | bytes 196616 | tf_op jit(solution)/shard_map/ppermute | solution.py:347
  87.1 6.7 %collective-permute-start.9 = (bf16[2,512,512]{2,1,0:T(8,128)(2,1)}, bf16[2,512,512]{2,1,0:T(8,128)(2,1)S(1)}, u32[]{:S(2)}, u32[]{:S(2)}) collective-permute-start(bf16[2,512,512]{2,1,0:T(8,128)(2,1)} %get-tuple-element.12), channel_id=1, source_target_pairs={{0,8},{8,0},{16,24},{24,16},{1,9},{9,1},{17,25},{25,17},{2,10},{10... | collective-permute-start | bytes 3145736 | tf_op jit(solution)/shard_map/ppermute | solution.py:347
  88.3 4.3 %collective-permute-start.17 = (bf16[2,64,256]{2,1,0:T(8,128)(2,1)S(1)}, bf16[2,64,256]{2,1,0:T(8,128)(2,1)S(1)}, u32[]{:S(2)}, u32[]{:S(2)}) collective-permute-start(bf16[2,64,256]{2,1,0:T(8,128)(2,1)S(1)} %fusion.5), channel_id=1, source_target_pairs={{0,1},{1,0},{2,3},{3,2},{4,5},{5,4},{6,7},{7,6},{8,9},{9,8},{10,11... | collective-permute-start | bytes 196616 | tf_op jit(solution)/shard_map/ppermute | solution.py:353
  92.7 12.6 %collective-permute-start.18 = (bf16[2,64,256]{2,1,0:T(8,128)(2,1)S(1)}, bf16[2,64,256]{2,1,0:T(8,128)(2,1)S(1)}, u32[]{:S(2)}, u32[]{:S(2)}) collective-permute-start(bf16[2,64,256]{2,1,0:T(8,128)(2,1)S(1)} %add_convert_fusion.4), channel_id=1, source_target_pairs={{0,2},{1,3},{2,0},{3,1},{4,6},{5,7},{6,4},{7,5},{8,10},{9,11},{10,... | collective-permute-start | bytes 196616 | tf_op jit(solution)/shard_map/ppermute | solution.py:353
  92.8 1.2 %copy-start.6 = (bf16[2,512,512]{2,1,0:T(8,128)(2,1)S(1)}, bf16[2,512,512]{2,1,0:T(8,128)(2,1)}, u32[]{:S(2)}) copy-start(bf16[2,512,512]{2,1,0:T(8,128)(2,1)} %get-tuple-element.11) | copy-start | bytes 3145732
  93.2 10.7 %collective-permute-start.11 = (bf16[256,512]{1,0:T(8,128)(2,1)S(1)}, bf16[256,512]{1,0:T(8,128)(2,1)S(1)}, u32[]{:S(2)}, u32[]{:S(2)}) collective-permute-start(bf16[256,512]{1,0:T(8,128)(2,1)S(1)} %get-tuple-element.18), channel_id=1, source_target_pairs={{0,1},{1,2},{2,3},{3,4},{4,5},{5,6},{6,7},{7,0},{8,9},{9,10},{10,1... | collective-permute-start | bytes 786440 | tf_op jit(solution)/shard_map/ppermute | solution.py:350
  94.3 10.8 %collective-permute-start.13 = (bf16[256,512]{1,0:T(8,128)(2,1)S(1)}, bf16[256,512]{1,0:T(8,128)(2,1)S(1)}, u32[]{:S(2)}, u32[]{:S(2)}) collective-permute-start(bf16[256,512]{1,0:T(8,128)(2,1)S(1)} %get-tuple-element.17), channel_id=1, source_target_pairs={{0,16},{8,24},{16,0},{24,8},{1,17},{9,25},{17,1},{25,9},{2,18},{10... | collective-permute-start | bytes 786440 | tf_op jit(solution)/shard_map/ppermute | solution.py:347
  104.0 12.7 %collective-permute-start.12 = (bf16[2,256,512]{2,1,0:T(8,128)(2,1)S(1)}, bf16[2,256,512]{2,1,0:T(8,128)(2,1)S(1)}, u32[]{:S(2)}, u32[]{:S(2)}) collective-permute-start(bf16[2,256,512]{2,1,0:T(8,128)(2,1)S(1)} %pad_maximum_fusion), channel_id=1, source_target_pairs={{0,16},{8,24},{16,0},{24,8},{1,17},{9,25},{17,1},{25,9},{2,18},{10... | collective-permute-start | bytes 1572872 | tf_op jit(solution)/shard_map/ppermute | solution.py:347
  105.3 15.5 %collective-permute-start.14 = (bf16[2,256,512]{2,1,0:T(8,128)(2,1)S(1)}, bf16[2,256,512]{2,1,0:T(8,128)(2,1)S(1)}, u32[]{:S(2)}, u32[]{:S(2)}) collective-permute-start(bf16[2,256,512]{2,1,0:T(8,128)(2,1)S(1)} %pad_maximum_fusion.1), channel_id=1, source_target_pairs={{0,1},{1,2},{2,3},{3,4},{4,5},{5,6},{6,7},{7,0},{8,9},{9,10},{10,1... | collective-permute-start | bytes 1572872 | tf_op jit(solution)/shard_map/ppermute | solution.py:350
  105.4 5.2 %collective-permute-start.19 = (bf16[2,64,256]{2,1,0:T(8,128)(2,1)S(1)}, bf16[2,64,256]{2,1,0:T(8,128)(2,1)S(1)}, u32[]{:S(2)}, u32[]{:S(2)}) collective-permute-start(bf16[2,64,256]{2,1,0:T(8,128)(2,1)S(1)} %add_convert_fusion.3), channel_id=1, source_target_pairs={{0,4},{1,5},{2,6},{3,7},{4,0},{5,1},{6,2},{7,3},{8,12},{9,13},{10,... | collective-permute-start | bytes 196616 | tf_op jit(solution)/shard_map/ppermute | solution.py:353

commit v2 on v0

v2 whole, which is shorter than its diff:
```python
import functools
import math

import jax
import jax.numpy as jnp
import ml_dtypes
import numpy as np
from jax import lax
from jax.experimental import pallas as pl
from jax.experimental.pallas import tpu as pltpu
from jax.sharding import PartitionSpec as P

defocus_scale = 0.7
gain = 1.457627118644068 * np.exp(0.14208207981059368j)
f32 = jnp.float32
bf16 = jnp.bfloat16
CHUNK = 16
VMEM_LIMIT = 60 * 2**20
COST = 6


def propagator(size):
    index = np.arange(size)
    signed = np.where(index < size // 2, index, index - size).astype(np.float64)
    chirp = -math.pi * defocus_scale * signed * signed / size
    angles = 2.0 * math.pi * ((index[:, None] * index[None, :]) % size) / size + chirp[None, :]
    kernel = np.exp(1j * angles).sum(axis=1) / size
    return kernel[(index[:, None] - index[None, :]) % size] * gain


def sides(size):
    matrix = propagator(size)
    real, imag = matrix.real, matrix.imag
    right = np.block([[real, imag], [-imag, real]])
    left = np.block([[real, -imag], [imag, real]])
    return right.astype(ml_dtypes.bfloat16), left.astype(ml_dtypes.bfloat16)


def propagate(x_ref, right_ref, left_ref, z_ref, out_ref):
    w = z_ref.shape[1]
    z = jnp.dot(x_ref[...], right_ref[...], preferred_element_type=f32)
    z_ref[:w] = z[:, :w].astype(bf16)
    z_ref[w:] = z[:, w:].astype(bf16)
    y = jnp.dot(left_ref[...], z_ref[...], preferred_element_type=f32)
    out_ref[0] = y[:w].astype(out_ref.dtype)
    out_ref[1] = y[w:].astype(out_ref.dtype)


class Alternating:
    def __init__(self):
        self.waiting = None

    def flush(self):
        if self.waiting is not None:
            self.waiting()
        self.waiting = None

    def matrix(self, task):
        self.flush()
        self.waiting = task

    def vector(self, task):
        task()
        self.flush()


class Copies:
    def __init__(self, sems):
        self.sems = sems
        self.count = 0

    def start(self, src, dst):
        copy = pltpu.make_async_copy(src, dst, self.sems.at[self.count])
        self.count += 1
        copy.start()
        return copy


def order_of(meta_ref, depth, slot):
    return jnp.bitwise_xor(jnp.bitwise_xor(slot, meta_ref[0]), meta_ref[1] * (depth - 1))


def shifts(meta_ref, p):
    return meta_ref[2 + 2 * p], meta_ref[3 + 2 * p]


def load_pieces(meta_ref, depth, copies, pieces, piece_refs, ext_ref, base, w):
    started = []
    for (slot, tile, plane), ref in zip(pieces, piece_refs):
        at = order_of(meta_ref, depth, slot) - base
        rows = pl.ds(tile * w, w)
        dst = ext_ref.at[at, :, rows, :] if plane is None else ext_ref.at[at, plane, rows, :]
        started.append(copies.start(ref, dst))
    return started


def times_window(meta_ref, ext_ref, at, p, wave_ref, write):
    w = wave_ref.shape[-1]
    r, q = (value.astype(jnp.int16) for value in shifts(meta_ref, p))
    cols = lax.broadcasted_iota(jnp.int16, (CHUNK, w), 1) < q
    index = lax.broadcasted_iota(jnp.int16, (CHUNK, w), 0)
    for start in range(0, w, CHUNK):
        rows = slice(start, start + CHUNK)
        below = slice(w + start, w + start + CHUNK)
        halo_row = index + jnp.int16(start) < r
        planes = []
        for plane in range(2):
            own = jnp.where(cols, ext_ref[at, plane, rows, w:], ext_ref[at, plane, rows, :w])
            halo = jnp.where(cols, ext_ref[at, plane, below, w:], ext_ref[at, plane, below, :w])
            planes.append(jnp.where(halo_row, halo, own).astype(f32))
        wr, wi = planes
        ar, ai = wave_ref[0, rows, :].astype(f32), wave_ref[1, rows, :].astype(f32)
        write(rows, ar * wr - ai * wi, ar * wi + ai * wr)


def to_product(x_ref):
    w = x_ref.shape[0]

    def write(rows, real, imag):
        x_ref[rows, :w] = real.astype(bf16)
        x_ref[rows, w:] = imag.astype(bf16)

    return write


def gradient_rows(meta_ref, g_ref, waves_a, waves_b, start):
    w = waves_a[0].shape[-1]
    rows = slice(start, start + CHUNK)
    index = lax.broadcasted_iota(jnp.int32, (CHUNK, w), 0) + start
    cols = lax.broadcasted_iota(jnp.int32, (CHUNK, w), 1)
    sums = [None, None]
    for p, (a_ref, b_ref) in enumerate(zip(waves_a, waves_b)):
        r, q = shifts(meta_ref, p)
        halo_row, right_col = index < r, cols < q
        ar, ai = a_ref[0, rows, :].astype(f32), a_ref[1, rows, :].astype(f32)
        br, bi = b_ref[0, rows, :].astype(f32), b_ref[1, rows, :].astype(f32)
        for plane, whole in enumerate((ar * br - ai * bi, -(ar * bi + ai * br))):
            halo = jnp.where(halo_row, whole, 0.0)
            parts = (
                whole,
                halo,
                jnp.where(right_col, whole, 0.0),
                jnp.where(right_col, halo, 0.0),
            )
            old = sums[plane]
            sums[plane] = parts if old is None else tuple(x + y for x, y in zip(old, parts))
    for plane in range(2):
        whole, halo, right, both = sums[plane]
        below = slice(w + start, w + start + CHUNK)
        g_ref[plane, rows, :w] = ((whole - halo) - (right - both)).astype(bf16)
        g_ref[plane, rows, w:] = (right - both).astype(bf16)
        g_ref[plane, below, :w] = (halo - both).astype(bf16)
        g_ref[plane, below, w:] = both.astype(bf16)


def gradient_parts(meta_ref, g_ref, waves_a, waves_b, parts):
    starts = list(range(0, waves_a[0].shape[-1], CHUNK))
    size = -(-len(starts) // parts)

    def task(part):
        def run():
            for start in starts[part * size : (part + 1) * size]:
                gradient_rows(meta_ref, g_ref, waves_a, waves_b, start)

        return run

    return [task(part) for part in range(parts)]


def each(ref, count):
    return [ref.at[i] for i in range(count)]


def start_kernel(
    probes, scale, meta_ref, probe_ref, cot_hbm, right_ref, left_ref, init_hbm, cot_ref, init_ref, x_ref, z_ref, sems
):
    w = probe_ref.shape[-1]
    copies = Copies(sems)
    high = meta_ref[1]
    kr, ki = float(scale.real), float(scale.imag)
    arriving = [
        copies.start(cot_hbm.at[meta_ref[0] * probes + p], cot_ref.at[p]) for p in range(probes)
    ]
    leaving = []
    tasks = Alternating()

    def moved(p, plane):
        r, q = shifts(meta_ref, p)
        return pltpu.roll(pltpu.roll(plane, r, 0), lax.rem(q, w), 1)

    def cotangent(p):
        arriving[p].wait()
        lr, li = moved(p, cot_ref[p, 0]), moved(p, cot_ref[p, 1])
        x_ref[p, :, :w] = (kr * lr + ki * li).astype(bf16)
        x_ref[p, :, w:] = (ki * lr - kr * li).astype(bf16)

    def spread(p):
        propagate(x_ref.at[p], right_ref, left_ref, z_ref.at[p % 2], init_ref.at[1, p])
        leaving.append(copies.start(init_ref.at[1, p], init_hbm.at[1 - high, p]))

    def launch(p):
        init_ref[0, p, 0] = moved(p, probe_ref[0])
        init_ref[0, p, 1] = moved(p, probe_ref[1])
        leaving.append(copies.start(init_ref.at[0, p], init_hbm.at[high, p]))

    for p in range(probes):
        tasks.vector(functools.partial(cotangent, p))
        tasks.matrix(functools.partial(spread, p))
        tasks.vector(functools.partial(launch, p))
    tasks.flush()
    for copy in leaving:
        copy.wait()


def near_kernel(probes, depth, pieces, meta_ref, init_hbm, right_ref, left_ref, *refs):
    n = len(pieces)
    half = depth // 2
    piece_refs, (a_hbm, ext_ref, a_ref, x_ref, z_ref, sems) = refs[:n], refs[n:]
    w = a_ref.shape[-1]
    copies = Copies(sems)
    arriving = [copies.start(init_hbm.at[0, p], a_ref.at[0, p]) for p in range(probes)]
    for copy in load_pieces(meta_ref, depth, copies, pieces, piece_refs, ext_ref, 0, w):
        copy.wait()
    leaving = []
    tasks = Alternating()

    def spread(k, p):
        propagate(x_ref.at[p], right_ref, left_ref, z_ref.at[p % 2], a_ref.at[k + 1, p])
        leaving.append(copies.start(a_ref.at[k + 1, p], a_hbm.at[k, p]))

    for k in range(half):
        for p in range(probes):
            if k == 0:
                arriving[p].wait()
            if probes == 1:
                tasks.flush()
            tasks.vector(
                lambda: times_window(meta_ref, ext_ref, k, p, a_ref.at[k, p], to_product(x_ref.at[p]))
            )
            tasks.matrix(functools.partial(spread, k, p))
    tasks.flush()
    for copy in leaving:
        copy.wait()


def far_kernel(probes, depth, pieces, meta_ref, init_hbm, a_hbm, right_ref, left_ref, *refs):
    n = len(pieces)
    half = depth // 2
    piece_refs, refs = refs[:n], refs[n:]
    g_hbm, refs = refs[:half], refs[half:]
    next_hbm, v_hbm, ext_ref, g_ref, a_ref, b_ref, xa_ref, xb_ref, z_ref, sems = refs
    w = a_ref.shape[-1]
    high = meta_ref[1]
    copies = Copies(sems)
    a_in = [copies.start(a_hbm.at[half - 1, p], a_ref.at[0, p]) for p in range(probes)]
    b_in = [copies.start(init_hbm.at[1, p], b_ref.at[0, p]) for p in range(probes)]
    for copy in load_pieces(meta_ref, depth, copies, pieces, piece_refs, ext_ref, half, w):
        copy.wait()
    tasks = Alternating()

    def spread(p, x, out):
        propagate(x, right_ref, left_ref, z_ref.at[p % 2], out)

    for k in range(half - 1):
        for p in range(probes):
            if k == 0:
                a_in[p].wait()
            if probes == 1:
                tasks.flush()
            tasks.vector(
                lambda: times_window(
                    meta_ref, ext_ref, k, p, a_ref.at[k, p], to_product(xa_ref.at[p])
                )
            )
            tasks.matrix(functools.partial(spread, p, xa_ref.at[p], a_ref.at[k + 1, p]))
    leaving = []
    for k in range(half):
        last = k == half - 1
        now, later = k % 2, (k + 1) % 2
        at = half - 1 - k
        parts = gradient_parts(
            meta_ref, g_ref.at[at], each(a_ref.at[at], probes), each(b_ref.at[now], probes), probes
        )
        for p in range(probes):
            if k == 0:
                b_in[p].wait()
            if probes == 1:
                tasks.flush()
            tasks.vector(
                lambda: times_window(
                    meta_ref, ext_ref, at, p, b_ref.at[now, p], to_product(xb_ref.at[p])
                )
            )
            if last:
                leaving.append(copies.start(xb_ref.at[p], next_hbm.at[p]))
        for p in range(probes):
            if not last:
                tasks.matrix(functools.partial(spread, p, xb_ref.at[p], b_ref.at[later, p]))
            tasks.vector(parts[p])
        tasks.flush()
        if k == 0:

            @pl.when(high == 1)
            def _():
                for p in range(probes):

                    def write(rows, real, imag):
                        v_ref = xa_ref.at[p]
                        v_ref[rows, :w] = real.astype(bf16)
                        v_ref[rows, w:] = -imag.astype(bf16)

                    times_window(meta_ref, ext_ref, half - 1, p, a_ref.at[half - 1, p], write)

    leaving.append(copies.start(xa_ref, v_hbm))
    for slot in range(half):
        order = order_of(meta_ref, depth, slot + half) - half
        leaving.append(copies.start(g_ref.at[order], g_hbm[slot]))
    for copy in leaving:
        copy.wait()


def return_kernel(probes, depth, pieces, orders, meta_ref, x_hbm, a_hbm, before_hbm, right_ref, left_ref, *refs):
    n = len(pieces)
    half = depth // 2
    whole = orders[-1] == 0
    piece_refs, refs = refs[:n], refs[n:]
    g_hbm, refs = refs[: half if whole else 1], refs[half if whole else 1 :]
    x_out, ext_ref, g_ref, a_ref, b_ref, x_ref, z_ref, sems = refs
    copies = Copies(sems)
    x_in = [copies.start(x_hbm.at[p], x_ref.at[p]) for p in range(probes)]
    arrived = load_pieces(meta_ref, depth, copies, pieces, piece_refs, ext_ref, 0, ext_ref.shape[2] // 2)
    a_in = [
        copies.start(a_hbm.at[0 if whole else order - 1], a_ref.at[number])
        for number, order in enumerate(orders)
    ]
    if whole:
        arrived.append(copies.start(before_hbm, g_ref.at[pl.ds(1, half - 1)]))
    tasks = Alternating()
    leaving = []

    def spread(p):
        propagate(x_ref.at[p], right_ref, left_ref, z_ref.at[p % 2], b_ref.at[p])

    for number, order in enumerate(orders):
        if number == 0:
            for copy in x_in + arrived:
                copy.wait()
        for p in range(probes):
            tasks.matrix(functools.partial(spread, p))
            if p:
                tasks.vector(
                    lambda: times_window(
                        meta_ref, ext_ref, order, p - 1, b_ref.at[p - 1], to_product(x_ref.at[p - 1])
                    )
                )
        tasks.flush()
        p = probes - 1
        times_window(meta_ref, ext_ref, order, p, b_ref.at[p], to_product(x_ref.at[p]))
        if number == len(orders) - 1:
            leaving.append(copies.start(x_ref, x_out))
        a_in[number].wait()
        for part in gradient_parts(
            meta_ref,
            g_ref.at[order if whole else order - 1],
            each(a_ref.at[number], probes),
            each(b_ref, probes),
            1,
        ):
            part()
    if whole:
        for slot in range(half):
            leaving.append(copies.start(g_ref.at[order_of(meta_ref, depth, slot)], g_hbm[slot]))
    else:
        leaving.append(copies.start(g_ref, g_hbm[0]))
    for copy in leaving:
        copy.wait()


def probe_kernel(probes, depth, meta_ref, x_ref, v_ref, lam_ref, t_ref):
    w = x_ref.shape[1]
    d = meta_ref[0]
    low = meta_ref[1] == 0
    for plane in range(2):
        total = None
        for p in range(probes):
            r, q = shifts(meta_ref, p)
            cols = slice(plane * w, (plane + 1) * w)
            mine = x_ref[p, :, cols].astype(f32)
            mine = -mine if plane else mine
            wave = jnp.where(low, mine, v_ref[p, :, cols].astype(f32))
            back = pltpu.roll(pltpu.roll(wave, lax.rem(w - r, w), 0), lax.rem(2 * w - q, w), 1)
            total = back if total is None else total + back
        t_ref[plane] = total
    rows = w // depth
    for slot in range(depth):
        block = pl.multiple_of(jnp.bitwise_xor(d, slot) * rows, rows)
        for plane in range(2):
            lam_ref[slot, plane] = t_ref[plane, pl.ds(block, rows), :].astype(bf16)


def cost(probes, steps, w):
    return pl.CostEstimate(
        flops=COST * probes * steps * 16 * w**3, bytes_accessed=8 * 2**20, transcendentals=0
    )

def after(value, *others):
    return lax.optimization_barrier((value, others))[0]


def total(first, second):
    return (first.astype(f32) + second.astype(f32)).astype(bf16)


def per_device(obj_slices, probe, positions, exit_cotangent):
    depth = lax.axis_size("depth")
    lat = lax.axis_size("lat")
    d = lax.axis_index("depth")
    w = probe.shape[-1]
    columns = obj_slices.shape[-1]
    half = depth // 2
    probes = positions.shape[0] // depth
    bits = [1 << i for i in range(depth.bit_length() - 1)]

    def across(value, bit):
        return lax.ppermute(value, "depth", [(i, i ^ bit) for i in range(depth)])

    def along(value, steps):
        return lax.ppermute(value, "lat", [(i, (i + steps) % lat) for i in range(lat)])

    def along_xor(value, bit):
        return lax.ppermute(value, "lat", [(i, i ^ bit) for i in range(lat)])

    right, left = sides(w)
    right, left = jnp.asarray(right), jnp.asarray(left)
    scale = gain ** (-2 * depth)
    own = obj_slices[0].astype(bf16)

    my_positions = lax.dynamic_slice(positions, (d * probes, 0), (probes, 2))
    meta = jnp.concatenate(
        [jnp.stack([d, (d >= half).astype(jnp.int32)]).astype(jnp.int32), my_positions.reshape(-1)]
    )

    smem = pl.BlockSpec(memory_space=pltpu.SMEM)
    vmem = pl.BlockSpec(memory_space=pltpu.VMEM)
    anywhere = pl.BlockSpec(memory_space=pl.ANY)
    wave = (probes, 2, w, w)
    product = (probes, w, 2 * w)
    g_shape = (2, 2 * w, columns)
    z_scratch = pltpu.VMEM((2, 2 * w, w), bf16)
    ext_scratch = pltpu.VMEM((half, 2, 2 * w, columns), bf16)

    def call(kernel, name, steps, outs, ins, scratch, copies):
        flat, structure = jax.tree.flatten(outs)
        results = pl.pallas_call(
            kernel,
            out_shape=flat,
            in_specs=[spec for spec, _ in ins],
            out_specs=[anywhere] * len(flat),
            scratch_shapes=scratch + [pltpu.SemaphoreType.DMA((copies,))],
            compiler_params=pltpu.CompilerParams(vmem_limit_bytes=VMEM_LIMIT),
            cost_estimate=cost(probes, steps, w),
            name=name,
        )(*[array for _, array in ins])
        return jax.tree.unflatten(structure, results)

    shape = jax.ShapeDtypeStruct
    sides_in = [(vmem, right), (vmem, left)]

    init = call(
        functools.partial(start_kernel, probes, scale),
        "first_waves",
        1,
        shape((2,) + wave, f32),
        [(smem, meta), (vmem, probe), (anywhere, exit_cotangent)] + sides_in,
        [
            pltpu.VMEM(wave, f32),
            pltpu.VMEM((2,) + wave, f32),
            pltpu.VMEM(product, bf16),
            z_scratch,
        ],
        3 * probes,
    )

    tiles = {0: own}
    halos = {0: along(own, -1)}
    for bit in reversed(bits[1:]):
        for slot in sorted(tiles):
            tiles[slot | bit] = across(tiles[slot], bit)
        for slot in sorted(s for s in tiles if s & bit):
            kept = halos[slot ^ bit]
            kept = kept if isinstance(kept, tuple) else (kept[0], kept[1])
            halos[slot] = (
                across(after(kept[0], init), bit),
                along(after(tiles[slot][1], init), -1),
            )

    def to_both_cores(slots, earlier):
        for slot in slots:
            sent = tiles[slot] if slot == 0 else after(tiles[slot], earlier)
            tiles[slot | 1] = across(sent, 1)
            halos[slot | 1] = jax.tree.map(lambda x: across(after(x, earlier), 1), halos[slot])

    def pieces_of(slots):
        names, arrays = [], []
        for slot in slots:
            names.append((slot, 0, None))
            arrays.append((anywhere, tiles[slot]))
            if isinstance(halos[slot], tuple):
                for plane in range(2):
                    names.append((slot, 1, plane))
                    arrays.append((anywhere, halos[slot][plane]))
            else:
                names.append((slot, 1, None))
                arrays.append((anywhere, halos[slot]))
        return names, arrays

    to_both_cores(range(0, half, 2), init)
    names, arrays = pieces_of(range(half))
    a_waves = call(
        functools.partial(near_kernel, probes, depth, names),
        "near_slices",
        half,
        shape((half,) + wave, f32),
        [(smem, meta), (anywhere, init)] + sides_in + arrays,
        [ext_scratch, pltpu.VMEM((half + 1,) + wave, f32), pltpu.VMEM(product, bf16), z_scratch],
        probes * (half + 1) + len(names),
    )

    to_both_cores(range(half, depth, 2), a_waves)
    far_names, far_arrays = pieces_of(range(half, depth))
    far_grads, next_x, v = call(
        functools.partial(far_kernel, probes, depth, far_names),
        "far_slices",
        half,
        ([shape(g_shape, bf16)] * half, shape(product, bf16), shape(product, bf16)),
        [(smem, meta), (anywhere, init), (anywhere, a_waves)] + sides_in + far_arrays,
        [
            ext_scratch,
            pltpu.VMEM((half,) + g_shape, bf16),
            pltpu.VMEM((half,) + wave, f32),
            pltpu.VMEM((2,) + wave, f32),
            pltpu.VMEM(product, bf16),
            pltpu.VMEM(product, bf16),
            z_scratch,
        ],
        3 * probes + len(far_names) + half + 1,
    )

    def core_sums(grads):
        return {
            slot: total(grads[slot], across(grads[slot | 1], 1)) for slot in grads if not slot & 1
        }

    def go_back(name, orders, x, a, before, kept):
        whole = orders[-1] == 0
        return call(
            functools.partial(return_kernel, probes, depth, names, orders),
            name,
            len(orders),
            (
                [shape(g_shape, bf16)] * half if whole else [shape((half - 1,) + g_shape, bf16)],
                shape(product, bf16),
            ),
            [(smem, meta), (anywhere, x), (anywhere, a), (anywhere, before)] + sides_in + arrays,
            [
                ext_scratch,
                pltpu.VMEM((kept,) + g_shape, bf16),
                pltpu.VMEM((len(orders),) + wave, f32),
                pltpu.VMEM(wave, f32),
                pltpu.VMEM(product, bf16),
                z_scratch,
            ],
            probes + len(names) + len(orders) + half + 2,
        )

    far_sums = core_sums({slot + half: g for slot, g in enumerate(far_grads)})
    (part_grads,), x = go_back(
        "return_first", list(range(half - 1, 0, -1)), next_x, a_waves, next_x, half - 1
    )
    owns, halo_grads = {}, {}
    for slot, both in far_sums.items():
        both = after(both, x)
        owns[slot] = (both[0, :w], both[1, :w])
        halo_grads[slot] = (both[0, w:], both[1, w:])
    shifted = {slot: along(halo_grads[slot][1], 1) for slot in owns}
    crossed = {slot: across(halo_grads[slot][0], half) for slot in owns if slot & half}
    near_grads, x = go_back("return_last", [0], after(x, far_sums), init, part_grads, half)
    for slot in list(owns):
        real, imag = owns[slot]
        owns[slot] = (real, total(imag, after(shifted[slot], x)))
    crossed = {slot: after(value, x) for slot, value in crossed.items()}
    near_grads = after(near_grads, owns, crossed)
    near_sums = core_sums(dict(enumerate(near_grads)))
    for slot, both in near_sums.items():
        owns[slot] = (both[0, :w], both[1, :w])
        halo_grads[slot] = (both[0, w:], both[1, w:])
    for bit in bits[1:]:
        for slot in sorted((s for s in owns if s & bit), reverse=True):
            halo_real, halo_imag = halo_grads.pop(slot)
            real, imag = owns.pop(slot)
            halo_real = crossed[slot] if bit == half else across(halo_real, bit)
            real = across(real, bit)
            if slot not in shifted:
                imag = total(imag, along(halo_imag, 1))
            imag = across(imag, bit)
            kept = halo_grads[slot ^ bit]
            halo_grads[slot ^ bit] = (total(kept[0], halo_real), kept[1])
            kept = owns[slot ^ bit]
            owns[slot ^ bit] = (total(kept[0], real), total(kept[1], imag))
    from_below = [along(plane, 1) for plane in halo_grads[0]]
    object_grad = jnp.stack(
        [kept.astype(f32) + moved.astype(f32) for kept, moved in zip(owns[0], from_below)]
    )[None]

    part = pl.pallas_call(
        functools.partial(probe_kernel, probes, depth),
        out_shape=shape((depth, 2, w // depth, w), bf16),
        in_specs=[smem, vmem, vmem],
        out_specs=vmem,
        scratch_shapes=[pltpu.VMEM((2, w, w), f32)],
        compiler_params=pltpu.CompilerParams(vmem_limit_bytes=VMEM_LIMIT),
        cost_estimate=pl.CostEstimate(flops=0, bytes_accessed=2**17, transcendentals=0),
        name="probe_part",
    )(meta, after(x, *near_sums.values()), v)
    for bit in reversed(bits):
        part = total(part[:bit], across(part[bit : 2 * bit], bit))
    part = part[0]
    if lat & (lat - 1):
        part = lax.psum(part.astype(f32), "lat")
    else:
        for bit in [1 << i for i in range(lat.bit_length() - 1)]:
            part = total(part, along_xor(part, bit))
    return (object_grad, part.astype(f32))


def solution(mesh):
    placed = (P("depth", None, "lat", None), P(), P("lat", None), P("lat", None, None, None))
    return jax.shard_map(
        per_device,
        mesh=mesh,
        in_specs=placed,
        out_specs=(P("depth", None, "lat", None), P(None, "depth", None)),
        check_vma=False,
    )
```

time: 1920 us -> 115 us (0.06)
  local copies, waits for them, and re-layouts: 967 us -> 4.41 us
  waiting for transfers between devices: 299 us -> 36.4 us
  loops' own time: 188 us -> 0 us
  matrix products: 174 us -> 0 us
  starting transfers between devices: 169 us -> 21.2 us
  other arithmetic: 96.2 us -> 6.72 us
  Pallas kernels: 0 us -> 45.4 us
    gather x4 -> x0, local copies, waits for them, and re-layouts: 816 us -> none  [propagator(): return (kernel_real[offsets], kernel_imag[offsets])]
    another operation x40 -> x0, loops' own time: 188 us -> none  [the longest x19 123 us: backward_tick(): lax.cond(active, backward_run_batch, backward_skip_batch, (grad_ext, prob...]
    dot_general x256 -> x0, matrix products: 174 us -> none  [the longest x128 97.7 us: right(): jnp.einsum('bjl,ls->bjs', field, matrix, precision=lax.Precision.HIGHEST)]
    ppermute x40 -> x22, waiting for transfers between devices: 210 us -> 36.4 us  [the longest x5 16.5 us: along(): lax.ppermute(value, 'lat', [(i, (i + steps) % lat) for i in range(lat)])]
    ppermute x40 -> x22, starting transfers between devices: 169 us -> 21.2 us  [the longest x5 11.8 us: along(): lax.ppermute(value, 'lat', [(i, (i + steps) % lat) for i in range(lat)])]
    dynamic_update_slice x16 -> x0, local copies, waits for them, and re-layouts: 101 us -> none  [add_window(): return lax.dynamic_update_slice(grad_ext, current + values, start)]
    psum x1 -> x0, waiting for transfers between devices: 69.9 us -> none  [per_device(): tile_total = lax.psum(probe_part.astype(jnp.bfloat16), 'lat')]
    add x49 -> x0, other arithmetic: 59.9 us -> none  [the longest x16 21.9 us: add_window(): return lax.dynamic_update_slice(grad_ext, current + values, start)]
  transfers between devices with their start and end apart: 42 -> 22, of which waited for: 40 -> 12; matrix products, arithmetic and copies ran while one was open for 43% -> 3% of each run, Pallas kernels for 0% -> 26%
where the time goes in v2:
time: 115 us
  Pallas kernels  45.4 us (39%)
  waiting for transfers between devices  36.4 us (32%)
  starting transfers between devices  21.2 us (18%)
  other arithmetic  6.72 us (6%)
  local copies, waits for them, and re-layouts  4.41 us (4%)
    pallas_call x5, Pallas kernels, call(): pl.pallas_call(kernel, out_shape=flat, in_specs=[spec for spec, _ in ins]...  42 us
    ppermute x5, waiting for transfers between devices, along(): lax.ppermute(value, 'lat', [(i, (i + steps) % lat) for i in range(lat)])  16.5 us
    ppermute x14, waiting for transfers between devices, across(): return lax.ppermute(value, 'depth', [(i, i ^ bit) for i in range(depth)])  13.7 us
    ppermute x5, starting transfers between devices, along(): lax.ppermute(value, 'lat', [(i, (i + steps) % lat) for i in range(lat)])  11.8 us
    ppermute x14, starting transfers between devices, across(): return lax.ppermute(value, 'depth', [(i, i ^ bit) for i in range(depth)])  9.13 us
    ppermute x3, waiting for transfers between devices, along_xor(): return lax.ppermute(value, 'lat', [(i, i ^ bit) for i in range(lat)])  6.21 us
    pallas_call x1, Pallas kernels, per_device(): pl.pallas_call(functools.partial(probe_kernel, probes, depth), out_shape=...  3.39 us
    unnamed x24, local copies, waits for them, and re-layouts  3.13 us
  transfers between devices with their start and end apart: 22, of which 12 were waited for; matrix products, arithmetic and copies ran while one was open for 3% of the time, Pallas kernels for 26%

profile of v2, /device:TPU:0, one launch (start us, length us, event | category | flops | bytes accessed | tf_op | source)
XLA Modules:
  0.0 115.1 jit_solution(8390665046871665256)
XLA Ops:
  0.6 0.0 copy-start
  0.6 1.3 %convert_bitcast_fusion.refs_0_ = bf16[2,256,512]{2,1,0:T(8,128)(2,1)S(1)} fusion(f32[1,2,256,512]{3,2,1,0:T(8,128)} %param.6), kind=kLoop, calls=%fused_computation.13 | loop fusion | flops 262144 | bytes 1572864 | tf_op jit(solution)/shard_map/convert_element_type | solution.py:436
  2.0 3.0 %collective-permute-start.3 = (bf16[2,256,512]{2,1,0:T(8,128)(2,1)S(1)}, bf16[2,256,512]{2,1,0:T(8,128)(2,1)S(1)}, u32[]{:S(2)}, u32[]{:S(2)}) collective-permute-start(bf16[2,256,512]{2,1,0:T(8,128)(2,1)S(1)} %convert_bitcast_fusion.refs_0_), channel_id=1, source_target_pairs={{0,16},{8,24},{16,0},{24,8},{1,17},{9,25},{17,1},{25,9},{2,18},{10... | collective-permute-start | bytes 1572872 | tf_op jit(solution)/shard_map/ppermute | solution.py:425
  5.0 0.0 collective-permute-start.1
  5.0 4.5 %collective-permute-start = (bf16[2,256,512]{2,1,0:T(8,128)(2,1)S(1)}, bf16[2,256,512]{2,1,0:T(8,128)(2,1)S(1)}, u32[]{:S(2)}, u32[]{:S(2)}) collective-permute-start(bf16[2,256,512]{2,1,0:T(8,128)(2,1)S(1)} %convert_bitcast_fusion.refs_0_), channel_id=1, source_target_pairs={{0,7},{1,0},{2,1},{3,2},{4,3},{5,4},{6,5},{7,6},{8,15},{9,8},{10,9... | collective-permute-start | bytes 1572872 | tf_op jit(solution)/shard_map/ppermute | solution.py:428
  9.5 0.1 constant_dynamic-slice_fusion
  9.6 0.1 copy.9
  9.7 0.1 reshape.16
  9.8 0.6 pad_add_fusion.meta_ref
  10.4 6.8 %first_waves.1.init_hbm.a_hbm = f32[2,4,2,256,256]{4,3,2,1,0:T(8,128)} custom-call(s32[10]{0:T(128)} %pad_add_fusion.meta_ref, f32[2,256,256]{2,1,0:T(8,128)} %probe_ref.1, f32[16,2,256,256]{3,2,1,0:T(8,128)} %cot_hbm.1, bf16[512,512]{1,0:T(8,128)(2,1)} %constant.17.clone.right_ref, bf16[512,512]{1,0:T(8,128)(2,1)} %constant.18.clone.left_ref), custom_call_target="tpu_custom_call" | custom-call | flops 6442450944 | bytes 8388608 | tf_op jit(solution)/shard_map/first_waves/pallas_call | solution.py:454
  17.2 4.1 %collective-permute-done.refs_1_ = bf16[2,256,512]{2,1,0:T(8,128)(2,1)S(1)} collective-permute-done((bf16[2,256,512]{2,1,0:T(8,128)(2,1)S(1)}, bf16[2,256,512]{2,1,0:T(8,128)(2,1)S(1)}, u32[]{:S(2)}, u32[]{:S(2)}) %collective-permute-start) | collective-permute-done | bytes 524320 | tf_op jit(solution)/shard_map/ppermute | solution.py:428
  21.4 0.0 collective-permute-start.2
  21.4 0.0 collective-permute-done.3.refs_0_
  21.4 0.6 collective-permute-start.4
  22.0 5.2 %collective-permute-start.5 = (bf16[256,512]{1,0:T(8,128)(2,1)S(1)}, bf16[256,512]{1,0:T(8,128)(2,1)S(1)}, u32[]{:S(2)}, u32[]{:S(2)}) collective-permute-start(bf16[256,512]{1,0:T(8,128)(2,1)S(1)} %slice_bitcast_fusion.4), channel_id=1, source_target_pairs={{0,7},{1,0},{2,1},{3,2},{4,3},{5,4},{6,5},{7,6},{8,15},{9,8},{10,9... | collective-permute-start | bytes 786440 | tf_op jit(solution)/shard_map/ppermute | solution.py:428
  27.2 0.0 collective-permute-done.1.refs_2_
  27.2 0.0 collective-permute-done.2.refs_3_
  27.2 0.8 copy-done.5
  28.0 0.8 copy-done.6
  28.8 8.0 %near_slices.1.a_hbm = f32[2,4,2,256,256]{4,3,2,1,0:T(8,128)} custom-call(s32[10]{0:T(128)} %pad_add_fusion.meta_ref, f32[2,4,2,256,256]{4,3,2,1,0:T(8,128)} %first_waves.1.init_hbm.a_hbm, bf16[512,512]{1,0:T(8,128)(2,1)} %constant.17.clone.right_ref, bf16[512,512]{1,0:T(8,128)(2,1)} %constant.18.clone.left_ref, bf16[2,256,512]{2,1,0:T(8,128)(2,1)} %copy-done.2, ...), custom_call_target="tpu_custom_call" | custom-call | flops 12884901888 | bytes 8388608 | tf_op jit(solution)/shard_map/near_slices/pallas_call | solution.py:454
  36.8 0.1 collective-permute-start.6
  36.9 0.0 collective-permute-done.5.refs_2_
  36.9 0.5 collective-permute-start.7
  37.5 0.1 collective-permute-start.8
  37.5 1.6 %collective-permute-done.7.refs_4_ = bf16[256,512]{1,0:T(8,128)(2,1)S(1)} collective-permute-done((bf16[256,512]{1,0:T(8,128)(2,1)S(1)}, bf16[256,512]{1,0:T(8,128)(2,1)S(1)}, u32[]{:S(2)}, u32[]{:S(2)}) %collective-permute-start.7) | collective-permute-done | bytes 262176 | tf_op jit(solution)/shard_map/ppermute | solution.py:425
  39.2 0.4 collective-permute-done.8.refs_5_
  39.6 0.3 copy-done.10
  39.9 0.4 copy-done.11
  40.2 0.8 copy-done.7
  41.1 12.3 %far_slices.1 = (bf16[2,512,512]{2,1,0:T(8,128)(2,1)}, bf16[2,512,512]{2,1,0:T(8,128)(2,1)}, bf16[4,256,512]{2,1,0:T(8,128)(2,1)}, bf16[4,256,512]{2,1,0:T(8,128)(2,1)}) custom-call(s32[10]{0:T(128)} %pad_add_fusion.meta_ref, f32[2,4,2,256,256]{4,3,2,1,0:T(8,128)} %first_waves.1.init_hbm.a_hbm, f32[2,4,2,256,256]{4,3,2,1,0:T(8,128)} %near_slices.1.a_hbm, ...), custom_call_target="tpu_custom_call" | custom-call | flops 12884901888 | bytes 8388608 | tf_op jit(solution)/shard_map/far_slices/pallas_call | solution.py:454
  53.4 0.2 collective-permute-start.9
  53.6 6.8 %return_first.1 = (bf16[1,2,512,512]{3,2,1,0:T(8,128)(2,1)}, bf16[4,256,512]{2,1,0:T(8,128)(2,1)}) custom-call(s32[10]{0:T(128)} %pad_add_fusion.meta_ref, bf16[4,256,512]{2,1,0:T(8,128)(2,1)} %get-tuple-element.30.x_hbm.before_hbm, f32[2,4,2,256,256]{4,3,2,1,0:T(8,128)} %near_slices.1.a_hbm, bf16[4,256,512]{2,1,0:T(8,128)(2,1)} %get-tuple-element.30.x_hbm.before_hbm, ...), custom_call_target="tpu_custom_call" | custom-call | flops 6442450944 | bytes 8388608 | tf_op jit(solution)/shard_map/return_first/pallas_call | solution.py:454
  60.5 0.3 add_convert_fusion.1
  60.8 0.1 slice_bitcast_fusion.6
  60.8 2.0 %collective-permute-start.11 = (bf16[256,512]{1,0:T(8,128)(2,1)S(1)}, bf16[256,512]{1,0:T(8,128)(2,1)S(1)}, u32[]{:S(2)}, u32[]{:S(2)}) collective-permute-start(bf16[256,512]{1,0:T(8,128)(2,1)S(1)} %get-tuple-element.48), channel_id=1, source_target_pairs={{0,16},{8,24},{16,0},{24,8},{1,17},{9,25},{17,1},{25,9},{2,18},{10... | collective-permute-start | bytes 786440 | tf_op jit(solution)/shard_map/ppermute | solution.py:425
  62.9 8.0 %return_last.1 = (bf16[2,512,512]{2,1,0:T(8,128)(2,1)}, bf16[2,512,512]{2,1,0:T(8,128)(2,1)}, bf16[4,256,512]{2,1,0:T(8,128)(2,1)}) custom-call(s32[10]{0:T(128)} %pad_add_fusion.meta_ref, bf16[4,256,512]{2,1,0:T(8,128)(2,1)} %get-tuple-element.34.x_hbm, f32[2,4,2,256,256]{4,3,2,1,0:T(8,128)} %first_waves.1.init_hbm.a_hbm, ...), custom_call_target="tpu_custom_call" | custom-call | flops 6442450944 | bytes 8388608 | tf_op jit(solution)/shard_map/return_last/pallas_call | solution.py:454
  70.9 2.9 %collective-permute-done.10 = bf16[256,512]{1,0:T(8,128)(2,1)S(1)} collective-permute-done((bf16[256,512]{1,0:T(8,128)(2,1)S(1)}, bf16[256,512]{1,0:T(8,128)(2,1)S(1)}, u32[]{:S(2)}, u32[]{:S(2)}) %collective-permute-start.10) | collective-permute-done | bytes 262176 | tf_op jit(solution)/shard_map/ppermute | solution.py:428
  73.9 0.1 fusion.3
  73.9 0.1 collective-permute-start.12
  74.0 2.9 %collective-permute-done.12 = bf16[2,512,512]{2,1,0:T(8,128)(2,1)S(1)} collective-permute-done((bf16[2,512,512]{2,1,0:T(8,128)(2,1)}, bf16[2,512,512]{2,1,0:T(8,128)(2,1)S(1)}, u32[]{:S(2)}, u32[]{:S(2)}) %collective-permute-start.12) | collective-permute-done | bytes 1048608 | tf_op jit(solution)/shard_map/ppermute | solution.py:425
  76.9 1.5 %add_convert_fusion = bf16[2,512,512]{2,1,0:T(8,128)(2,1)S(1)} fusion(bf16[2,512,512]{2,1,0:T(8,128)(2,1)S(1)} %collective-permute-done.12, bf16[2,512,512]{2,1,0:T(8,128)(2,1)} %get-tuple-element.42), kind=kLoop, calls=%fused_computation | loop fusion | flops 2097152 | bytes 3145728 | tf_op jit(solution)/shard_map/convert_element_type | solution.py:411
  78.4 3.4 %probe_part.1 = bf16[4,2,64,256]{3,2,1,0:T(8,128)(2,1)} custom-call(s32[10]{0:T(128)} %pad_add_fusion.meta_ref, bf16[4,256,512]{2,1,0:T(8,128)(2,1)} %get-tuple-element.44.x_ref, bf16[4,256,512]{2,1,0:T(8,128)(2,1)} %get-tuple-element.45.v_ref), custom_call_target="tpu_custom_call" | custom-call | bytes 131072 | tf_op jit(solution)/shard_map/probe_part/pallas_call | solution.py:615
  81.8 0.9 slice.63
  82.7 0.4 collective-permute-start.17
  83.1 1.7 %collective-permute-start.13 = (bf16[256,512]{1,0:T(8,128)(2,1)S(1)}, bf16[256,512]{1,0:T(8,128)(2,1)S(1)}, u32[]{:S(2)}, u32[]{:S(2)}) collective-permute-start(bf16[256,512]{1,0:T(8,128)(2,1)S(1)} %get-tuple-element.50), channel_id=1, source_target_pairs={{0,16},{8,24},{16,0},{24,8},{1,17},{9,25},{17,1},{25,9},{2,18},{10... | collective-permute-start | bytes 786440 | tf_op jit(solution)/shard_map/ppermute | solution.py:425
  84.8 0.3 collective-permute-start.15
  85.1 4.0 %collective-permute-done.17 = bf16[2,2,64,256]{3,2,1,0:T(8,128)(2,1)S(1)} collective-permute-done((bf16[2,2,64,256]{3,2,1,0:T(8,128)(2,1)S(1)}, bf16[2,2,64,256]{3,2,1,0:T(8,128)(2,1)S(1)}, u32[]{:S(2)}, u32[]{:S(2)}) %collective-permute-start.17) | collective-permute-done | bytes 131104 | tf_op jit(solution)/shard_map/ppermute | solution.py:425
  89.1 0.9 add_convert_fusion.2
  90.0 0.1 collective-permute-start.18
  90.1 0.1 fusion.1
  90.2 1.2 %collective-permute-done.18 = bf16[1,2,64,256]{3,2,1,0:T(8,128)(2,1)S(1)} collective-permute-done((bf16[1,2,64,256]{3,2,1,0:T(8,128)(2,1)S(1)}, bf16[1,2,64,256]{3,2,1,0:T(8,128)(2,1)S(1)}, u32[]{:S(2)}, u32[]{:S(2)}) %collective-permute-start.18) | collective-permute-done | bytes 65568 | tf_op jit(solution)/shard_map/ppermute | solution.py:425
  91.4 0.1 collective-permute-start.19
  91.5 2.1 %collective-permute-start.16 = (bf16[256,512]{1,0:T(8,128)(2,1)S(1)}, bf16[256,512]{1,0:T(8,128)(2,1)S(1)}, u32[]{:S(2)}, u32[]{:S(2)}) collective-permute-start(bf16[256,512]{1,0:T(8,128)(2,1)S(1)} %slice_bitcast_fusion), channel_id=1, source_target_pairs={{0,1},{1,2},{2,3},{3,4},{4,5},{5,6},{6,7},{7,0},{8,9},{9,10},{10,1... | collective-permute-start | bytes 786440 | tf_op jit(solution)/shard_map/ppermute | solution.py:428
  93.5 0.1 collective-permute-start.14
  93.6 2.1 %collective-permute-done.19 = bf16[2,64,256]{2,1,0:T(8,128)(2,1)S(1)} collective-permute-done((bf16[2,64,256]{2,1,0:T(8,128)(2,1)S(1)}, bf16[2,64,256]{2,1,0:T(8,128)(2,1)S(1)}, u32[]{:S(2)}, u32[]{:S(2)}) %collective-permute-start.19) | collective-permute-done | bytes 65568 | tf_op jit(solution)/shard_map/ppermute | solution.py:431
  95.7 0.1 collective-permute-start.20
  95.8 3.7 %collective-permute-done.15 = bf16[256,512]{1,0:T(8,128)(2,1)S(1)} collective-permute-done((bf16[256,512]{1,0:T(8,128)(2,1)S(1)}, bf16[256,512]{1,0:T(8,128)(2,1)S(1)}, u32[]{:S(2)}, u32[]{:S(2)}) %collective-permute-start.15) | collective-permute-done | bytes 262176 | tf_op jit(solution)/shard_map/ppermute | solution.py:425
  99.5 4.0 %collective-permute-done.16 = bf16[256,512]{1,0:T(8,128)(2,1)S(1)} collective-permute-done((bf16[256,512]{1,0:T(8,128)(2,1)S(1)}, bf16[256,512]{1,0:T(8,128)(2,1)S(1)}, u32[]{:S(2)}, u32[]{:S(2)}) %collective-permute-start.16) | collective-permute-done | bytes 262176 | tf_op jit(solution)/shard_map/ppermute | solution.py:428
  103.5 5.4 %collective-permute-done.14 = bf16[256,512]{1,0:T(8,128)(2,1)S(1)} collective-permute-done((bf16[256,512]{1,0:T(8,128)(2,1)S(1)}, bf16[256,512]{1,0:T(8,128)(2,1)S(1)}, u32[]{:S(2)}, u32[]{:S(2)}) %collective-permute-start.14) | collective-permute-done | bytes 262176 | tf_op jit(solution)/shard_map/ppermute | solution.py:428
  108.9 0.2 add_bitcast_fusion.1
  109.2 0.1 collective-permute-start.21
  109.2 1.0 maximum_bitcast_fusion
  110.3 4.1 %collective-permute-done.21 = bf16[2,64,256]{2,1,0:T(8,128)(2,1)S(1)} collective-permute-done((bf16[2,64,256]{2,1,0:T(8,128)(2,1)S(1)}, bf16[2,64,256]{2,1,0:T(8,128)(2,1)S(1)}, u32[]{:S(2)}, u32[]{:S(2)}) %collective-permute-start.21) | collective-permute-done | bytes 65568 | tf_op jit(solution)/shard_map/ppermute | solution.py:431
  114.4 0.7 fusion.5
  (32 shorter events, 0.2 us)
Async XLA Ops:
  0.6 8.9 %copy-start = (s32[16,2]{0,1:T(2,128)S(1)}, s32[16,2]{0,1:T(2,128)}, u32[]{:S(2)}) copy-start(s32[16,2]{0,1:T(2,128)} %param.8) | copy-start | bytes 388
  1.9 15.3 %copy-start.2 = (bf16[2,256,512]{2,1,0:T(8,128)(2,1)}, bf16[2,256,512]{2,1,0:T(8,128)(2,1)S(1)}, u32[]{:S(2)}) copy-start(bf16[2,256,512]{2,1,0:T(8,128)(2,1)S(1)} %convert_bitcast_fusion.refs_0_) | copy-start | bytes 1572868
  2.0 19.4 %collective-permute-start.3 = (bf16[2,256,512]{2,1,0:T(8,128)(2,1)S(1)}, bf16[2,256,512]{2,1,0:T(8,128)(2,1)S(1)}, u32[]{:S(2)}, u32[]{:S(2)}) collective-permute-start(bf16[2,256,512]{2,1,0:T(8,128)(2,1)S(1)} %convert_bitcast_fusion.refs_0_), channel_id=1, source_target_pairs={{0,16},{8,24},{16,0},{24,8},{1,17},{9,25},{17,1},{25,9},{2,18},{10... | collective-permute-start | bytes 1572872 | tf_op jit(solution)/shard_map/ppermute | solution.py:425
  5.0 22.2 %collective-permute-start.1 = (bf16[2,256,512]{2,1,0:T(8,128)(2,1)S(1)}, bf16[2,256,512]{2,1,0:T(8,128)(2,1)S(1)}, u32[]{:S(2)}, u32[]{:S(2)}) collective-permute-start(bf16[2,256,512]{2,1,0:T(8,128)(2,1)S(1)} %convert_bitcast_fusion.refs_0_), channel_id=1, source_target_pairs={{0,8},{8,0},{16,24},{24,16},{1,9},{9,1},{17,25},{25,17},{2,10},{10... | collective-permute-start | bytes 1572872 | tf_op jit(solution)/shard_map/ppermute | solution.py:425
  5.0 16.4 %collective-permute-start = (bf16[2,256,512]{2,1,0:T(8,128)(2,1)S(1)}, bf16[2,256,512]{2,1,0:T(8,128)(2,1)S(1)}, u32[]{:S(2)}, u32[]{:S(2)}) collective-permute-start(bf16[2,256,512]{2,1,0:T(8,128)(2,1)S(1)} %convert_bitcast_fusion.refs_0_), channel_id=1, source_target_pairs={{0,7},{1,0},{2,1},{3,2},{4,3},{5,4},{6,5},{7,6},{8,15},{9,8},{10,9... | collective-permute-start | bytes 1572872 | tf_op jit(solution)/shard_map/ppermute | solution.py:428
  21.4 5.8 %copy-start.3 = (bf16[2,256,512]{2,1,0:T(8,128)(2,1)}, bf16[2,256,512]{2,1,0:T(8,128)(2,1)S(1)}, u32[]{:S(2)}) copy-start(bf16[2,256,512]{2,1,0:T(8,128)(2,1)S(1)} %collective-permute-done.refs_1_) | copy-start | bytes 1572868
  21.4 5.8 %collective-permute-start.2 = (bf16[2,256,512]{2,1,0:T(8,128)(2,1)S(1)}, bf16[2,256,512]{2,1,0:T(8,128)(2,1)S(1)}, u32[]{:S(2)}, u32[]{:S(2)}) collective-permute-start(bf16[2,256,512]{2,1,0:T(8,128)(2,1)S(1)} %collective-permute-done.refs_1_), channel_id=1, source_target_pairs={{0,8},{8,0},{16,24},{24,16},{1,9},{9,1},{17,25},{25,17},{2,10},{10... | collective-permute-start | bytes 1572872 | tf_op jit(solution)/shard_map/ppermute | solution.py:425
  21.4 15.4 %copy-start.4 = (bf16[2,256,512]{2,1,0:T(8,128)(2,1)}, bf16[2,256,512]{2,1,0:T(8,128)(2,1)S(1)}, u32[]{:S(2)}) copy-start(bf16[2,256,512]{2,1,0:T(8,128)(2,1)S(1)} %collective-permute-done.3.refs_0_) | copy-start | bytes 1572868
  21.4 15.5 %collective-permute-start.4 = (bf16[256,512]{1,0:T(8,128)(2,1)S(1)}, bf16[256,512]{1,0:T(8,128)(2,1)S(1)}, u32[]{:S(2)}, u32[]{:S(2)}) collective-permute-start(bf16[256,512]{1,0:T(8,128)(2,1)S(1)} %slice_bitcast_fusion.5), channel_id=1, source_target_pairs={{0,16},{8,24},{16,0},{24,8},{1,17},{9,25},{17,1},{25,9},{2,18},{10... | collective-permute-start | bytes 786440 | tf_op jit(solution)/shard_map/ppermute | solution.py:425
  22.0 14.9 %collective-permute-start.5 = (bf16[256,512]{1,0:T(8,128)(2,1)S(1)}, bf16[256,512]{1,0:T(8,128)(2,1)S(1)}, u32[]{:S(2)}, u32[]{:S(2)}) collective-permute-start(bf16[256,512]{1,0:T(8,128)(2,1)S(1)} %slice_bitcast_fusion.4), channel_id=1, source_target_pairs={{0,7},{1,0},{2,1},{3,2},{4,3},{5,4},{6,5},{7,6},{8,15},{9,8},{10,9... | collective-permute-start | bytes 786440 | tf_op jit(solution)/shard_map/ppermute | solution.py:428
  27.2 0.8 copy-start.5
  28.0 0.8 copy-start.6
  36.8 2.7 %collective-permute-start.6 = (bf16[2,256,512]{2,1,0:T(8,128)(2,1)S(1)}, bf16[2,256,512]{2,1,0:T(8,128)(2,1)S(1)}, u32[]{:S(2)}, u32[]{:S(2)}) collective-permute-start(bf16[2,256,512]{2,1,0:T(8,128)(2,1)S(1)} %collective-permute-done.3.refs_0_), channel_id=1, source_target_pairs={{0,8},{8,0},{16,24},{24,16},{1,9},{9,1},{17,25},{25,17},{2,10},{10... | collective-permute-start | bytes 1572872 | tf_op jit(solution)/shard_map/ppermute | solution.py:425
  36.9 2.6 %copy-start.9 = (bf16[256,512]{1,0:T(8,128)(2,1)}, bf16[256,512]{1,0:T(8,128)(2,1)S(1)}, u32[]{:S(2)}) copy-start(bf16[256,512]{1,0:T(8,128)(2,1)S(1)} %collective-permute-done.5.refs_2_) | copy-start | bytes 786436
  36.9 2.6 %copy-start.8 = (bf16[256,512]{1,0:T(8,128)(2,1)}, bf16[256,512]{1,0:T(8,128)(2,1)S(1)}, u32[]{:S(2)}) copy-start(bf16[256,512]{1,0:T(8,128)(2,1)S(1)} %collective-permute-done.4.refs_1_) | copy-start | bytes 786436
  36.9 2.2 %collective-permute-start.7 = (bf16[256,512]{1,0:T(8,128)(2,1)S(1)}, bf16[256,512]{1,0:T(8,128)(2,1)S(1)}, u32[]{:S(2)}, u32[]{:S(2)}) collective-permute-start(bf16[256,512]{1,0:T(8,128)(2,1)S(1)} %collective-permute-done.4.refs_1_), channel_id=1, source_target_pairs={{0,8},{8,0},{16,24},{24,16},{1,9},{9,1},{17,25},{25,17},{2,10},{10... | collective-permute-start | bytes 786440 | tf_op jit(solution)/shard_map/ppermute | solution.py:425
  37.5 2.1 %collective-permute-start.8 = (bf16[256,512]{1,0:T(8,128)(2,1)S(1)}, bf16[256,512]{1,0:T(8,128)(2,1)S(1)}, u32[]{:S(2)}, u32[]{:S(2)}) collective-permute-start(bf16[256,512]{1,0:T(8,128)(2,1)S(1)} %collective-permute-done.5.refs_2_), channel_id=1, source_target_pairs={{0,8},{8,0},{16,24},{24,16},{1,9},{9,1},{17,25},{25,17},{2,10},{10... | collective-permute-start | bytes 786440 | tf_op jit(solution)/shard_map/ppermute | solution.py:425
  39.2 0.7 copy-start.10
  39.5 0.7 copy-start.11
  40.2 0.8 copy-start.7
  53.4 7.1 %collective-permute-start.9 = (bf16[2,512,512]{2,1,0:T(8,128)(2,1)}, bf16[2,512,512]{2,1,0:T(8,128)(2,1)S(1)}, u32[]{:S(2)}, u32[]{:S(2)}) collective-permute-start(bf16[2,512,512]{2,1,0:T(8,128)(2,1)} %get-tuple-element.33), channel_id=1, source_target_pairs={{0,8},{8,0},{16,24},{24,16},{1,9},{9,1},{17,25},{25,17},{2,10},{10... | collective-permute-start | bytes 3145736 | tf_op jit(solution)/shard_map/ppermute | solution.py:425
  53.6 6.9 %copy-start.1 = (bf16[2,512,512]{2,1,0:T(8,128)(2,1)S(1)}, bf16[2,512,512]{2,1,0:T(8,128)(2,1)}, u32[]{:S(2)}) copy-start(bf16[2,512,512]{2,1,0:T(8,128)(2,1)} %get-tuple-element.32) | copy-start | bytes 3145732
  60.8 10.1 %collective-permute-start.11 = (bf16[256,512]{1,0:T(8,128)(2,1)S(1)}, bf16[256,512]{1,0:T(8,128)(2,1)S(1)}, u32[]{:S(2)}, u32[]{:S(2)}) collective-permute-start(bf16[256,512]{1,0:T(8,128)(2,1)S(1)} %get-tuple-element.48), channel_id=1, source_target_pairs={{0,16},{8,24},{16,0},{24,8},{1,17},{9,25},{17,1},{25,9},{2,18},{10... | collective-permute-start | bytes 786440 | tf_op jit(solution)/shard_map/ppermute | solution.py:425
  62.9 11.0 %collective-permute-start.10 = (bf16[256,512]{1,0:T(8,128)(2,1)S(1)}, bf16[256,512]{1,0:T(8,128)(2,1)S(1)}, u32[]{:S(2)}, u32[]{:S(2)}) collective-permute-start(bf16[256,512]{1,0:T(8,128)(2,1)S(1)} %get-tuple-element.49), channel_id=1, source_target_pairs={{0,1},{1,2},{2,3},{3,4},{4,5},{5,6},{6,7},{7,0},{8,9},{9,10},{10,1... | collective-permute-start | bytes 786440 | tf_op jit(solution)/shard_map/ppermute | solution.py:428
  73.9 2.9 %collective-permute-start.12 = (bf16[2,512,512]{2,1,0:T(8,128)(2,1)}, bf16[2,512,512]{2,1,0:T(8,128)(2,1)S(1)}, u32[]{:S(2)}, u32[]{:S(2)}) collective-permute-start(bf16[2,512,512]{2,1,0:T(8,128)(2,1)} %get-tuple-element.43), channel_id=1, source_target_pairs={{0,8},{8,0},{16,24},{24,16},{1,9},{9,1},{17,25},{25,17},{2,10},{10... | collective-permute-start | bytes 3145736 | tf_op jit(solution)/shard_map/ppermute | solution.py:425
  82.7 6.4 %collective-permute-start.17 = (bf16[2,2,64,256]{3,2,1,0:T(8,128)(2,1)S(1)}, bf16[2,2,64,256]{3,2,1,0:T(8,128)(2,1)S(1)}, u32[]{:S(2)}, u32[]{:S(2)}) collective-permute-start(bf16[2,2,64,256]{3,2,1,0:T(8,128)(2,1)S(1)} %slice.63), channel_id=1, source_target_pairs={{0,16},{8,24},{16,0},{24,8},{1,17},{9,25},{17,1},{25,9},{2,18},{10... | collective-permute-start | bytes 393224 | tf_op jit(solution)/shard_map/ppermute | solution.py:425
  83.1 12.7 %collective-permute-start.13 = (bf16[256,512]{1,0:T(8,128)(2,1)S(1)}, bf16[256,512]{1,0:T(8,128)(2,1)S(1)}, u32[]{:S(2)}, u32[]{:S(2)}) collective-permute-start(bf16[256,512]{1,0:T(8,128)(2,1)S(1)} %get-tuple-element.50), channel_id=1, source_target_pairs={{0,16},{8,24},{16,0},{24,8},{1,17},{9,25},{17,1},{25,9},{2,18},{10... | collective-permute-start | bytes 786440 | tf_op jit(solution)/shard_map/ppermute | solution.py:425
  84.8 14.7 %collective-permute-start.15 = (bf16[256,512]{1,0:T(8,128)(2,1)S(1)}, bf16[256,512]{1,0:T(8,128)(2,1)S(1)}, u32[]{:S(2)}, u32[]{:S(2)}) collective-permute-start(bf16[256,512]{1,0:T(8,128)(2,1)S(1)} %fusion.3), channel_id=1, source_target_pairs={{0,16},{8,24},{16,0},{24,8},{1,17},{9,25},{17,1},{25,9},{2,18},{10... | collective-permute-start | bytes 786440 | tf_op jit(solution)/shard_map/ppermute | solution.py:425
  90.0 1.3 %collective-permute-start.18 = (bf16[1,2,64,256]{3,2,1,0:T(8,128)(2,1)S(1)}, bf16[1,2,64,256]{3,2,1,0:T(8,128)(2,1)S(1)}, u32[]{:S(2)}, u32[]{:S(2)}) collective-permute-start(bf16[1,2,64,256]{3,2,1,0:T(8,128)(2,1)S(1)} %slice.65), channel_id=1, source_target_pairs={{0,8},{8,0},{16,24},{24,16},{1,9},{9,1},{17,25},{25,17},{2,10},{10... | collective-permute-start | bytes 196616 | tf_op jit(solution)/shard_map/ppermute | solution.py:425
  91.4 4.3 %collective-permute-start.19 = (bf16[2,64,256]{2,1,0:T(8,128)(2,1)S(1)}, bf16[2,64,256]{2,1,0:T(8,128)(2,1)S(1)}, u32[]{:S(2)}, u32[]{:S(2)}) collective-permute-start(bf16[2,64,256]{2,1,0:T(8,128)(2,1)S(1)} %fusion.4), channel_id=1, source_target_pairs={{0,1},{1,0},{2,3},{3,2},{4,5},{5,4},{6,7},{7,6},{8,9},{9,8},{10,11... | collective-permute-start | bytes 196616 | tf_op jit(solution)/shard_map/ppermute | solution.py:431
  91.5 12.0 %collective-permute-start.16 = (bf16[256,512]{1,0:T(8,128)(2,1)S(1)}, bf16[256,512]{1,0:T(8,128)(2,1)S(1)}, u32[]{:S(2)}, u32[]{:S(2)}) collective-permute-start(bf16[256,512]{1,0:T(8,128)(2,1)S(1)} %slice_bitcast_fusion), channel_id=1, source_target_pairs={{0,1},{1,2},{2,3},{3,4},{4,5},{5,6},{6,7},{7,0},{8,9},{9,10},{10,1... | collective-permute-start | bytes 786440 | tf_op jit(solution)/shard_map/ppermute | solution.py:428
  93.5 15.4 %collective-permute-start.14 = (bf16[256,512]{1,0:T(8,128)(2,1)S(1)}, bf16[256,512]{1,0:T(8,128)(2,1)S(1)}, u32[]{:S(2)}, u32[]{:S(2)}) collective-permute-start(bf16[256,512]{1,0:T(8,128)(2,1)S(1)} %fusion.1), channel_id=1, source_target_pairs={{0,1},{1,2},{2,3},{3,4},{4,5},{5,6},{6,7},{7,0},{8,9},{9,10},{10,1... | collective-permute-start | bytes 786440 | tf_op jit(solution)/shard_map/ppermute | solution.py:428
  95.7 13.4 %collective-permute-start.20 = (bf16[2,64,256]{2,1,0:T(8,128)(2,1)S(1)}, bf16[2,64,256]{2,1,0:T(8,128)(2,1)S(1)}, u32[]{:S(2)}, u32[]{:S(2)}) collective-permute-start(bf16[2,64,256]{2,1,0:T(8,128)(2,1)S(1)} %add_convert_fusion.5), channel_id=1, source_target_pairs={{0,2},{1,3},{2,0},{3,1},{4,6},{5,7},{6,4},{7,5},{8,10},{9,11},{10,... | collective-permute-start | bytes 196616 | tf_op jit(solution)/shard_map/ppermute | solution.py:431
  109.2 5.2 %collective-permute-start.21 = (bf16[2,64,256]{2,1,0:T(8,128)(2,1)S(1)}, bf16[2,64,256]{2,1,0:T(8,128)(2,1)S(1)}, u32[]{:S(2)}, u32[]{:S(2)}) collective-permute-start(bf16[2,64,256]{2,1,0:T(8,128)(2,1)S(1)} %add_convert_fusion.4), channel_id=1, source_target_pairs={{0,4},{1,5},{2,6},{3,7},{4,0},{5,1},{6,2},{7,3},{8,12},{9,13},{10,... | collective-permute-start | bytes 196616 | tf_op jit(solution)/shard_map/ppermute | solution.py:431

commit v3 on v2

--- a/solution.py
+++ b/solution.py
@@ -15,7 +15,7 @@
 f32 = jnp.float32
 bf16 = jnp.bfloat16
 CHUNK = 16
-VMEM_LIMIT = 60 * 2**20
+VMEM_LIMIT = 54 * 2**20
 COST = 6
 
 
@@ -212,13 +212,13 @@
         copy.wait()
 
 
-def near_kernel(probes, depth, pieces, meta_ref, init_hbm, right_ref, left_ref, *refs):
+def near_kernel(probes, depth, pieces, meta_ref, _, right_ref, left_ref, *refs):
     n = len(pieces)
     half = depth // 2
-    piece_refs, (a_hbm, ext_ref, a_ref, x_ref, z_ref, sems) = refs[:n], refs[n:]
+    piece_refs, (waves_hbm, ext_ref, a_ref, x_ref, z_ref, sems) = refs[:n], refs[n:]
     w = a_ref.shape[-1]
     copies = Copies(sems)
-    arriving = [copies.start(init_hbm.at[0, p], a_ref.at[0, p]) for p in range(probes)]
+    arriving = [copies.start(waves_hbm.at[0, p], a_ref.at[0, p]) for p in range(probes)]
     for copy in load_pieces(meta_ref, depth, copies, pieces, piece_refs, ext_ref, 0, w):
         copy.wait()
     leaving = []
@@ -226,7 +226,7 @@
 
     def spread(k, p):
         propagate(x_ref.at[p], right_ref, left_ref, z_ref.at[p % 2], a_ref.at[k + 1, p])
-        leaving.append(copies.start(a_ref.at[k + 1, p], a_hbm.at[k, p]))
+        leaving.append(copies.start(a_ref.at[k + 1, p], waves_hbm.at[2 + k, p]))
 
     for k in range(half):
         for p in range(probes):
@@ -243,17 +243,17 @@
         copy.wait()
 
 
-def far_kernel(probes, depth, pieces, meta_ref, init_hbm, a_hbm, right_ref, left_ref, *refs):
+def far_kernel(probes, depth, pieces, meta_ref, _, right_ref, left_ref, *refs):
     n = len(pieces)
     half = depth // 2
     piece_refs, refs = refs[:n], refs[n:]
     g_hbm, refs = refs[:half], refs[half:]
-    next_hbm, v_hbm, ext_ref, g_ref, a_ref, b_ref, xa_ref, xb_ref, z_ref, sems = refs
+    waves_hbm, next_hbm, v_hbm, ext_ref, g_ref, a_ref, b_ref, xa_ref, xb_ref, z_ref, sems = refs
     w = a_ref.shape[-1]
     high = meta_ref[1]
     copies = Copies(sems)
-    a_in = [copies.start(a_hbm.at[half - 1, p], a_ref.at[0, p]) for p in range(probes)]
-    b_in = [copies.start(init_hbm.at[1, p], b_ref.at[0, p]) for p in range(probes)]
+    a_in = [copies.start(waves_hbm.at[1 + half, p], a_ref.at[0, p]) for p in range(probes)]
+    b_in = [copies.start(waves_hbm.at[1, p], b_ref.at[0, p]) for p in range(probes)]
     for copy in load_pieces(meta_ref, depth, copies, pieces, piece_refs, ext_ref, half, w):
         copy.wait()
     tasks = Alternating()
@@ -319,66 +319,40 @@
         copy.wait()
 
 
-def return_kernel(probes, depth, pieces, orders, meta_ref, x_hbm, a_hbm, before_hbm, right_ref, left_ref, *refs):
+def return_kernel(probes, depth, pieces, meta_ref, _, x_hbm, v_hbm, right_ref, left_ref, *refs):
     n = len(pieces)
     half = depth // 2
-    whole = orders[-1] == 0
     piece_refs, refs = refs[:n], refs[n:]
-    g_hbm, refs = refs[: half if whole else 1], refs[half if whole else 1 :]
-    x_out, ext_ref, g_ref, a_ref, b_ref, x_ref, z_ref, sems = refs
+    waves_hbm, lam_hbm, ext_ref, b_ref, x_ref, v_ref, z_ref, t_ref, lam_ref, sems = refs
+    w = x_ref.shape[1]
     copies = Copies(sems)
     x_in = [copies.start(x_hbm.at[p], x_ref.at[p]) for p in range(probes)]
-    arrived = load_pieces(meta_ref, depth, copies, pieces, piece_refs, ext_ref, 0, ext_ref.shape[2] // 2)
-    a_in = [
-        copies.start(a_hbm.at[0 if whole else order - 1], a_ref.at[number])
-        for number, order in enumerate(orders)
-    ]
-    if whole:
-        arrived.append(copies.start(before_hbm, g_ref.at[pl.ds(1, half - 1)]))
+    arrived = load_pieces(meta_ref, depth, copies, pieces, piece_refs, ext_ref, 0, w)
+    arrived.append(copies.start(v_hbm, v_ref))
     tasks = Alternating()
     leaving = []
 
-    def spread(p):
-        propagate(x_ref.at[p], right_ref, left_ref, z_ref.at[p % 2], b_ref.at[p])
-
-    for number, order in enumerate(orders):
-        if number == 0:
-            for copy in x_in + arrived:
+    def spread(k, p):
+        propagate(x_ref.at[p], right_ref, left_ref, z_ref.at[p % 2], b_ref.at[k, p])
+        leaving.append(copies.start(b_ref.at[k, p], waves_hbm.at[2 + half + k, p]))
+
+    def multiply(k, p):
+        if k == 0 and p == 0:
+            for copy in arrived:
                 copy.wait()
+        times_window(
+            meta_ref, ext_ref, half - 1 - k, p, b_ref.at[k, p], to_product(x_ref.at[p])
+        )
+
+    for k in range(half):
         for p in range(probes):
-            tasks.matrix(functools.partial(spread, p))
+            if k == 0:
+                x_in[p].wait()
+            tasks.matrix(functools.partial(spread, k, p))
             if p:
-                tasks.vector(
-                    lambda: times_window(
-                        meta_ref, ext_ref, order, p - 1, b_ref.at[p - 1], to_product(x_ref.at[p - 1])
-                    )
-                )
+                tasks.vector(functools.partial(multiply, k, p - 1))
         tasks.flush()
-        p = probes - 1
-        times_window(meta_ref, ext_ref, order, p, b_ref.at[p], to_product(x_ref.at[p]))
-        if number == len(orders) - 1:
-            leaving.append(copies.start(x_ref, x_out))
-        a_in[number].wait()
-        for part in gradient_parts(
-            meta_ref,
-            g_ref.at[order if whole else order - 1],
-            each(a_ref.at[number], probes),
-            each(b_ref, probes),
-            1,
-        ):
-            part()
-    if whole:
-        for slot in range(half):
-            leaving.append(copies.start(g_ref.at[order_of(meta_ref, depth, slot)], g_hbm[slot]))
-    else:
-        leaving.append(copies.start(g_ref, g_hbm[0]))
-    for copy in leaving:
-        copy.wait()
-
-
-def probe_kernel(probes, depth, meta_ref, x_ref, v_ref, lam_ref, t_ref):
-    w = x_ref.shape[1]
-    d = meta_ref[0]
+        multiply(k, probes - 1)
     low = meta_ref[1] == 0
     for plane in range(2):
         total = None
@@ -393,9 +367,43 @@
         t_ref[plane] = total
     rows = w // depth
     for slot in range(depth):
-        block = pl.multiple_of(jnp.bitwise_xor(d, slot) * rows, rows)
+        block = pl.multiple_of(jnp.bitwise_xor(meta_ref[0], slot) * rows, rows)
         for plane in range(2):
             lam_ref[slot, plane] = t_ref[plane, pl.ds(block, rows), :].astype(bf16)
+    leaving.append(copies.start(lam_ref, lam_hbm))
+    for copy in leaving:
+        copy.wait()
+
+
+def gradient_kernel(probes, depth, meta_ref, _, *refs):
+    half = depth // 2
+    g_hbm, (waves_hbm, g_ref, a_ref, b_ref, sems) = refs[:half], refs[half:]
+    copies = Copies(sems)
+    arriving = []
+    for k in range(half):
+        order = half - 1 - k
+        arriving.append(
+            (
+                copies.start(waves_hbm.at[1 + order if order else 0], a_ref.at[k]),
+                copies.start(waves_hbm.at[2 + half + k], b_ref.at[k]),
+            )
+        )
+    for k in range(half):
+        for copy in arriving[k]:
+            copy.wait()
+        for part in gradient_parts(
+            meta_ref,
+            g_ref.at[half - 1 - k],
+            each(a_ref.at[k], probes),
+            each(b_ref.at[k], probes),
+            1,
+        ):
+            part()
+    leaving = [
+        copies.start(g_ref.at[order_of(meta_ref, depth, slot)], g_hbm[slot]) for slot in range(half)
+    ]
+    for copy in leaving:
+        copy.wait()
 
 
 def cost(probes, steps, w):
@@ -443,13 +451,14 @@
     smem = pl.BlockSpec(memory_space=pltpu.SMEM)
     vmem = pl.BlockSpec(memory_space=pltpu.VMEM)
     anywhere = pl.BlockSpec(memory_space=pl.ANY)
+    hbm = pl.BlockSpec(memory_space=pltpu.HBM)
     wave = (probes, 2, w, w)
     product = (probes, w, 2 * w)
     g_shape = (2, 2 * w, columns)
     z_scratch = pltpu.VMEM((2, 2 * w, w), bf16)
     ext_scratch = pltpu.VMEM((half, 2, 2 * w, columns), bf16)
 
-    def call(kernel, name, steps, outs, ins, scratch, copies):
+    def call(kernel, name, steps, outs, ins, scratch, copies, limit=VMEM_LIMIT, aliases={}):
         flat, structure = jax.tree.flatten(outs)
         results = pl.pallas_call(
             kernel,
@@ -457,8 +466,9 @@
             in_specs=[spec for spec, _ in ins],
             out_specs=[anywhere] * len(flat),
             scratch_shapes=scratch + [pltpu.SemaphoreType.DMA((copies,))],
-            compiler_params=pltpu.CompilerParams(vmem_limit_bytes=VMEM_LIMIT),
+            compiler_params=pltpu.CompilerParams(vmem_limit_bytes=limit),
             cost_estimate=cost(probes, steps, w),
+            input_output_aliases=aliases,
             name=name,
         )(*[array for _, array in ins])
         return jax.tree.unflatten(structure, results)
@@ -466,12 +476,13 @@
     shape = jax.ShapeDtypeStruct
     sides_in = [(vmem, right), (vmem, left)]
 
+    all_waves = shape((2 + depth,) + wave, f32)
     init = call(
         functools.partial(start_kernel, probes, scale),
         "first_waves",
         1,
-        shape((2,) + wave, f32),
-        [(smem, meta), (vmem, probe), (anywhere, exit_cotangent)] + sides_in,
+        all_waves,
+        [(smem, meta), (vmem, probe), (hbm, exit_cotangent)] + sides_in,
         [
             pltpu.VMEM(wave, f32),
             pltpu.VMEM((2,) + wave, f32),
@@ -479,6 +490,7 @@
             z_scratch,
         ],
         3 * probes,
+        60 * 2**20,
     )
 
     tiles = {0: own}
@@ -516,24 +528,25 @@
 
     to_both_cores(range(0, half, 2), init)
     names, arrays = pieces_of(range(half))
-    a_waves = call(
+    waves = call(
         functools.partial(near_kernel, probes, depth, names),
         "near_slices",
         half,
-        shape((half,) + wave, f32),
-        [(smem, meta), (anywhere, init)] + sides_in + arrays,
+        all_waves,
+        [(smem, meta), (hbm, init)] + sides_in + arrays,
         [ext_scratch, pltpu.VMEM((half + 1,) + wave, f32), pltpu.VMEM(product, bf16), z_scratch],
         probes * (half + 1) + len(names),
-    )
-
-    to_both_cores(range(half, depth, 2), a_waves)
+        aliases={1: 0},
+    )
+
+    to_both_cores(range(half, depth, 2), waves)
     far_names, far_arrays = pieces_of(range(half, depth))
-    far_grads, next_x, v = call(
+    far_grads, waves, next_x, v = call(
         functools.partial(far_kernel, probes, depth, far_names),
         "far_slices",
         half,
-        ([shape(g_shape, bf16)] * half, shape(product, bf16), shape(product, bf16)),
-        [(smem, meta), (anywhere, init), (anywhere, a_waves)] + sides_in + far_arrays,
+        ([shape(g_shape, bf16)] * half, all_waves, shape(product, bf16), shape(product, bf16)),
+        [(smem, meta), (hbm, waves)] + sides_in + far_arrays,
         [
             ext_scratch,
             pltpu.VMEM((half,) + g_shape, bf16),
@@ -544,6 +557,26 @@
             z_scratch,
         ],
         3 * probes + len(far_names) + half + 1,
+        aliases={1: half},
+    )
+
+    waves, part = call(
+        functools.partial(return_kernel, probes, depth, names),
+        "return_waves",
+        half,
+        (all_waves, shape((depth, 2, w // depth, w), bf16)),
+        [(smem, meta), (hbm, waves), (hbm, next_x), (hbm, v)] + sides_in + arrays,
+        [
+            ext_scratch,
+            pltpu.VMEM((half,) + wave, f32),
+            pltpu.VMEM(product, bf16),
+            pltpu.VMEM(product, bf16),
+            z_scratch,
+            pltpu.VMEM((2, w, w), f32),
+            pltpu.VMEM((depth, 2, w // depth, w), bf16),
+        ],
+        probes * (half + 1) + len(names) + 2,
+        aliases={1: 0},
     )
 
     def core_sums(grads):
@@ -551,85 +584,71 @@
             slot: total(grads[slot], across(grads[slot | 1], 1)) for slot in grads if not slot & 1
         }
 
-    def go_back(name, orders, x, a, before, kept):
-        whole = orders[-1] == 0
-        return call(
-            functools.partial(return_kernel, probes, depth, names, orders),
-            name,
-            len(orders),
-            (
-                [shape(g_shape, bf16)] * half if whole else [shape((half - 1,) + g_shape, bf16)],
-                shape(product, bf16),
-            ),
-            [(smem, meta), (anywhere, x), (anywhere, a), (anywhere, before)] + sides_in + arrays,
-            [
-                ext_scratch,
-                pltpu.VMEM((kept,) + g_shape, bf16),
-                pltpu.VMEM((len(orders),) + wave, f32),
-                pltpu.VMEM(wave, f32),
-                pltpu.VMEM(product, bf16),
-                z_scratch,
-            ],
-            probes + len(names) + len(orders) + half + 2,
-        )
-
     far_sums = core_sums({slot + half: g for slot, g in enumerate(far_grads)})
-    (part_grads,), x = go_back(
-        "return_first", list(range(half - 1, 0, -1)), next_x, a_waves, next_x, half - 1
-    )
     owns, halo_grads = {}, {}
     for slot, both in far_sums.items():
-        both = after(both, x)
+        both = after(both, waves)
         owns[slot] = (both[0, :w], both[1, :w])
         halo_grads[slot] = (both[0, w:], both[1, w:])
     shifted = {slot: along(halo_grads[slot][1], 1) for slot in owns}
     crossed = {slot: across(halo_grads[slot][0], half) for slot in owns if slot & half}
-    near_grads, x = go_back("return_last", [0], after(x, far_sums), init, part_grads, half)
+    part_sum = part[0].astype(f32)
+    arriving = [across(part[slot], slot) for slot in range(1, depth)]
+    near_grads, _ = call(
+        functools.partial(gradient_kernel, probes, depth),
+        "near_gradients",
+        half,
+        ([shape(g_shape, bf16)] * half, all_waves),
+        [(smem, after(meta, far_sums)), (hbm, waves)],
+        [
+            pltpu.VMEM((half,) + g_shape, bf16),
+            pltpu.VMEM((half,) + wave, f32),
+            pltpu.VMEM((half,) + wave, f32),
+        ],
+        3 * half,
+        aliases={1: half},
+    )
+    for moved in after(arriving, near_grads):
+        part_sum = part_sum + moved.astype(f32)
+    part = part_sum.astype(bf16)
+    shifted, crossed = after((shifted, crossed), near_grads)
     for slot in list(owns):
         real, imag = owns[slot]
-        owns[slot] = (real, total(imag, after(shifted[slot], x)))
-    crossed = {slot: after(value, x) for slot, value in crossed.items()}
-    near_grads = after(near_grads, owns, crossed)
+        owns[slot] = (real, total(imag, shifted[slot]))
+    near_grads = after(near_grads, owns, crossed, part)
     near_sums = core_sums(dict(enumerate(near_grads)))
+    lat_bits = [1 << i for i in range(lat.bit_length() - 1)]
+    butterfly = not lat & (lat - 1)
+    if butterfly:
+        moved = along_xor(part, lat_bits[0])
+        part = total(part, after(moved, near_sums))
     for slot, both in near_sums.items():
+        halo_grads[slot] = (both[0, w:], both[1, w:])
+        both = after(both, halo_grads[slot], part)
         owns[slot] = (both[0, :w], both[1, :w])
-        halo_grads[slot] = (both[0, w:], both[1, w:])
+    from_below = None
     for bit in bits[1:]:
         for slot in sorted((s for s in owns if s & bit), reverse=True):
             halo_real, halo_imag = halo_grads.pop(slot)
             real, imag = owns.pop(slot)
             halo_real = crossed[slot] if bit == half else across(halo_real, bit)
-            real = across(real, bit)
             if slot not in shifted:
                 imag = total(imag, along(halo_imag, 1))
-            imag = across(imag, bit)
+            sent = across(jnp.stack([real, imag]), bit)
             kept = halo_grads[slot ^ bit]
             halo_grads[slot ^ bit] = (total(kept[0], halo_real), kept[1])
+            if len(halo_grads) == 1:
+                from_below = along(jnp.stack(halo_grads[0]), 1)
+                sent = after(sent, from_below)
             kept = owns[slot ^ bit]
-            owns[slot ^ bit] = (total(kept[0], real), total(kept[1], imag))
-    from_below = [along(plane, 1) for plane in halo_grads[0]]
-    object_grad = jnp.stack(
-        [kept.astype(f32) + moved.astype(f32) for kept, moved in zip(owns[0], from_below)]
-    )[None]
-
-    part = pl.pallas_call(
-        functools.partial(probe_kernel, probes, depth),
-        out_shape=shape((depth, 2, w // depth, w), bf16),
-        in_specs=[smem, vmem, vmem],
-        out_specs=vmem,
-        scratch_shapes=[pltpu.VMEM((2, w, w), f32)],
-        compiler_params=pltpu.CompilerParams(vmem_limit_bytes=VMEM_LIMIT),
-        cost_estimate=pl.CostEstimate(flops=0, bytes_accessed=2**17, transcendentals=0),
-        name="probe_part",
-    )(meta, after(x, *near_sums.values()), v)
-    for bit in reversed(bits):
-        part = total(part[:bit], across(part[bit : 2 * bit], bit))
-    part = part[0]
-    if lat & (lat - 1):
+            owns[slot ^ bit] = (total(kept[0], sent[0]), total(kept[1], sent[1]))
+    object_grad = (jnp.stack(owns[0]).astype(f32) + from_below.astype(f32))[None]
+
+    if butterfly:
+        for bit in lat_bits[1:]:
+            part = total(part, along_xor(part, bit))
+    else:
         part = lax.psum(part.astype(f32), "lat")
-    else:
-        for bit in [1 << i for i in range(lat.bit_length() - 1)]:
-            part = total(part, along_xor(part, bit))
     return (object_grad, part.astype(f32))
 
 

time: 115 us -> 103 us (0.90)
  waiting for transfers between devices: 36.4 us -> 28.8 us
  Pallas kernels: 45.4 us -> 42.1 us
  starting transfers between devices: 21.2 us -> 19.3 us
    ppermute x14, waiting for transfers between devices: 13.7 us -> 4.53 us  [across(): return lax.ppermute(value, 'depth', [(i, i ^ bit) for i in range(depth)])]
    pallas_call x1 -> x0, Pallas kernels: 3.39 us -> none  [per_device(): pl.pallas_call(functools.partial(probe_kernel, probes, depth), out_shape=...]
    ppermute x3, waiting for transfers between devices: 6.21 us -> 9.38 us  [along_xor(): return lax.ppermute(value, 'lat', [(i, i ^ bit) for i in range(lat)])]
    ppermute x5 -> x4, starting transfers between devices: 11.8 us -> 10 us  [along(): lax.ppermute(value, 'lat', [(i, (i + steps) % lat) for i in range(lat)])]
    ppermute x5 -> x4, waiting for transfers between devices: 16.5 us -> 14.9 us  [along(): lax.ppermute(value, 'lat', [(i, (i + steps) % lat) for i in range(lat)])]
    convert_element_type x7 -> x6, other arithmetic: 2.92 us -> 2.05 us  [total(): return (first.astype(f32) + second.astype(f32)).astype(bf16)]
  transfers between devices with their start and end apart: 22 -> 21, of which waited for: 12 -> 9; matrix products, arithmetic and copies ran while one was open for 3% -> 5% of each run, Pallas kernels for 26% -> 29%
where the time goes in v3:
time: 103 us; the launch traced here: 102 us
  Pallas kernels  42.1 us (41%)
  waiting for transfers between devices  28.8 us (28%)
  starting transfers between devices  19.3 us (19%)
  other arithmetic  6.8 us (7%)
  local copies, waits for them, and re-layouts  4.36 us (4%)
    pallas_call x5, Pallas kernels, call(): pl.pallas_call(kernel, out_shape=flat, in_specs=[spec for spec, _ in ins]...  42.1 us
    ppermute x4, waiting for transfers between devices, along(): lax.ppermute(value, 'lat', [(i, (i + steps) % lat) for i in range(lat)])  14.9 us
    ppermute x4, starting transfers between devices, along(): lax.ppermute(value, 'lat', [(i, (i + steps) % lat) for i in range(lat)])  10 us
    ppermute x3, waiting for transfers between devices, along_xor(): return lax.ppermute(value, 'lat', [(i, i ^ bit) for i in range(lat)])  9.38 us
    ppermute x14, starting transfers between devices, across(): return lax.ppermute(value, 'depth', [(i, i ^ bit) for i in range(depth)])  9.1 us
    ppermute x14, waiting for transfers between devices, across(): return lax.ppermute(value, 'depth', [(i, i ^ bit) for i in range(depth)])  4.53 us
    unnamed x24, local copies, waits for them, and re-layouts  3.08 us
  transfers between devices with their start and end apart: 21, of which 9 were waited for; matrix products, arithmetic and copies ran while one was open for 5% of the time, Pallas kernels for 29%

profile of v3, /device:TPU:0, one launch (start us, length us, event | category | flops | bytes accessed | tf_op | source)
XLA Modules:
  0.0 102.3 jit_solution(4614404252276613713)
XLA Ops:
  0.6 0.0 copy-start
  0.6 1.3 %convert_bitcast_fusion.refs_0_ = bf16[2,256,512]{2,1,0:T(8,128)(2,1)S(1)} fusion(f32[1,2,256,512]{3,2,1,0:T(8,128)} %param.6), kind=kLoop, calls=%fused_computation.10 | loop fusion | flops 262144 | bytes 1572864 | tf_op jit(solution)/shard_map/convert_element_type | solution.py:444
  2.0 3.0 %collective-permute-start.3 = (bf16[2,256,512]{2,1,0:T(8,128)(2,1)S(1)}, bf16[2,256,512]{2,1,0:T(8,128)(2,1)S(1)}, u32[]{:S(2)}, u32[]{:S(2)}) collective-permute-start(bf16[2,256,512]{2,1,0:T(8,128)(2,1)S(1)} %convert_bitcast_fusion.refs_0_), channel_id=1, source_target_pairs={{0,16},{8,24},{16,0},{24,8},{1,17},{9,25},{17,1},{25,9},{2,18},{10... | collective-permute-start | bytes 1572872 | tf_op jit(solution)/shard_map/ppermute | solution.py:433
  5.0 0.0 collective-permute-start.1
  5.0 4.5 %collective-permute-start = (bf16[2,256,512]{2,1,0:T(8,128)(2,1)S(1)}, bf16[2,256,512]{2,1,0:T(8,128)(2,1)S(1)}, u32[]{:S(2)}, u32[]{:S(2)}) collective-permute-start(bf16[2,256,512]{2,1,0:T(8,128)(2,1)S(1)} %convert_bitcast_fusion.refs_0_), channel_id=1, source_target_pairs={{0,7},{1,0},{2,1},{3,2},{4,3},{5,4},{6,5},{7,6},{8,15},{9,8},{10,9... | collective-permute-start | bytes 1572872 | tf_op jit(solution)/shard_map/ppermute | solution.py:436
  9.5 0.1 constant_dynamic-slice_fusion
  9.6 0.1 copy.13
  9.7 0.1 reshape.12
  9.8 0.6 pad_add_fusion.meta_ref
  10.4 6.8 %first_waves.1._ = f32[6,4,2,256,256]{4,3,2,1,0:T(8,128)} custom-call(s32[10]{0:T(128)} %pad_add_fusion.meta_ref, f32[2,256,256]{2,1,0:T(8,128)} %probe_ref.1, f32[16,2,256,256]{3,2,1,0:T(8,128)} %cot_hbm.1, bf16[512,512]{1,0:T(8,128)(2,1)} %constant.17.clone.right_ref, bf16[512,512]{1,0:T(8,128)(2,1)} %constant.18.clone.left_ref), custom_call_target="tpu_custom_call" | custom-call | flops 6442450944 | bytes 8388608 | tf_op jit(solution)/shard_map/first_waves/pallas_call | solution.py:463
  17.2 4.1 %collective-permute-done.refs_1_ = bf16[2,256,512]{2,1,0:T(8,128)(2,1)S(1)} collective-permute-done((bf16[2,256,512]{2,1,0:T(8,128)(2,1)S(1)}, bf16[2,256,512]{2,1,0:T(8,128)(2,1)S(1)}, u32[]{:S(2)}, u32[]{:S(2)}) %collective-permute-start) | collective-permute-done | bytes 524320 | tf_op jit(solution)/shard_map/ppermute | solution.py:436
  21.4 0.0 collective-permute-start.2
  21.4 0.6 collective-permute-start.4
  22.0 5.2 %collective-permute-start.5 = (bf16[256,512]{1,0:T(8,128)(2,1)S(1)}, bf16[256,512]{1,0:T(8,128)(2,1)S(1)}, u32[]{:S(2)}, u32[]{:S(2)}) collective-permute-start(bf16[256,512]{1,0:T(8,128)(2,1)S(1)} %slice_bitcast_fusion.1), channel_id=1, source_target_pairs={{0,7},{1,0},{2,1},{3,2},{4,3},{5,4},{6,5},{7,6},{8,15},{9,8},{10,9... | collective-permute-start | bytes 786440 | tf_op jit(solution)/shard_map/ppermute | solution.py:436
  27.2 0.8 copy-done.5
  28.0 0.8 copy-done.6
  28.8 8.0 %near_slices.1._ = f32[6,4,2,256,256]{4,3,2,1,0:T(8,128)} custom-call(s32[10]{0:T(128)} %pad_add_fusion.meta_ref, f32[6,4,2,256,256]{4,3,2,1,0:T(8,128)} %first_waves.1._, bf16[512,512]{1,0:T(8,128)(2,1)} %constant.17.clone.right_ref, bf16[512,512]{1,0:T(8,128)(2,1)} %constant.18.clone.left_ref, ...), custom_call_target="tpu_custom_call", output_to_operand_aliasing={{}: (1, {})} | custom-call | flops 12884901888 | bytes 8388608 | tf_op jit(solution)/shard_map/near_slices/pallas_call | solution.py:463
  36.8 0.1 collective-permute-start.6
  36.9 0.0 collective-permute-done.5.refs_2_
  36.9 0.5 collective-permute-start.7
  37.5 0.1 collective-permute-start.8
  37.5 1.6 %collective-permute-done.7.refs_4_ = bf16[256,512]{1,0:T(8,128)(2,1)S(1)} collective-permute-done((bf16[256,512]{1,0:T(8,128)(2,1)S(1)}, bf16[256,512]{1,0:T(8,128)(2,1)S(1)}, u32[]{:S(2)}, u32[]{:S(2)}) %collective-permute-start.7) | collective-permute-done | bytes 262176 | tf_op jit(solution)/shard_map/ppermute | solution.py:433
  39.1 0.4 collective-permute-done.8.refs_5_
  39.5 0.0 collective-permute-done.6.refs_3_
  39.5 0.3 copy-done.10
  39.8 0.4 copy-done.11
  40.2 0.8 copy-done.7
  41.0 12.3 %far_slices.1 = (bf16[2,512,512]{2,1,0:T(8,128)(2,1)}, bf16[2,512,512]{2,1,0:T(8,128)(2,1)}, f32[6,4,2,256,256]{4,3,2,1,0:T(8,128)}, bf16[4,256,512]{2,1,0:T(8,128)(2,1)}, bf16[4,256,512]{2,1,0:T(8,128)(2,1)}) custom-call(s32[10]{0:T(128)} %pad_add_fusion.meta_ref, f32[6,4,2,256,256]{4,3,2,1,0:T(8,128)} %near_slices.1._, ...), custom_call_target="tpu_custom_call", output_to_operand_aliasing={{2}: (1, {})} | custom-call | flops 12884901888 | bytes 8388608 | tf_op jit(solution)/shard_map/far_slices/pallas_call | solution.py:463
  53.3 0.2 collective-permute-start.9
  53.5 8.7 %return_waves.1 = (f32[6,4,2,256,256]{4,3,2,1,0:T(8,128)}, bf16[4,2,64,256]{3,2,1,0:T(8,128)(2,1)}) custom-call(s32[10]{0:T(128)} %pad_add_fusion.meta_ref, f32[6,4,2,256,256]{4,3,2,1,0:T(8,128)} %get-tuple-element.38._, bf16[4,256,512]{2,1,0:T(8,128)(2,1)} %get-tuple-element.39.x_hbm, ...), custom_call_target="tpu_custom_call", output_to_operand_aliasing={{0}: (1, {})} | custom-call | flops 12884901888 | bytes 8388608 | tf_op jit(solution)/shard_map/return_waves/pallas_call | solution.py:463
  62.2 0.9 slice_bitcast_fusion.5
  63.1 2.0 %collective-permute-start.14 = (bf16[2,64,256]{2,1,0:T(8,128)(2,1)S(1)}, bf16[2,64,256]{2,1,0:T(8,128)(2,1)S(1)}, u32[]{:S(2)}, u32[]{:S(2)}) collective-permute-start(bf16[2,64,256]{2,1,0:T(8,128)(2,1)S(1)} %get-tuple-element.61), channel_id=1, source_target_pairs={{0,24},{8,16},{16,8},{24,0},{1,25},{9,17},{17,9},{25,1},{2,26},{10... | collective-permute-start | bytes 196616 | tf_op jit(solution)/shard_map/ppermute | solution.py:433
  65.2 0.1 collective-permute-start.13
  65.3 0.1 collective-permute-start.12
  65.4 0.0 collective-permute-done.9
  65.4 0.3 add_convert_fusion.1
  65.6 0.1 fusion.6
  65.7 1.9 %collective-permute-start.11 = (bf16[256,512]{1,0:T(8,128)(2,1)S(1)}, bf16[256,512]{1,0:T(8,128)(2,1)S(1)}, u32[]{:S(2)}, u32[]{:S(2)}) collective-permute-start(bf16[256,512]{1,0:T(8,128)(2,1)S(1)} %get-tuple-element.59), channel_id=1, source_target_pairs={{0,16},{8,24},{16,0},{24,8},{1,17},{9,25},{17,1},{25,9},{2,18},{10... | collective-permute-start | bytes 786440 | tf_op jit(solution)/shard_map/ppermute | solution.py:433
  67.6 0.0 collective-permute-start.10
  67.6 6.3 %near_gradients.1 = (bf16[2,512,512]{2,1,0:T(8,128)(2,1)}, bf16[2,512,512]{2,1,0:T(8,128)(2,1)}, f32[6,4,2,256,256]{4,3,2,1,0:T(8,128)}) custom-call(s32[10]{0:T(128)} %pad_add_fusion.meta_ref, f32[6,4,2,256,256]{4,3,2,1,0:T(8,128)} %get-tuple-element.41._), custom_call_target="tpu_custom_call", output_to_operand_aliasing={{2}: (1, {})} | custom-call | flops 12884901888 | bytes 8388608 | tf_op jit(solution)/shard_map/near_gradients/pallas_call | solution.py:463
  73.9 0.0 collective-permute-done.14
  73.9 0.0 collective-permute-done.13
  73.9 0.9 fusion.4
  74.8 0.2 collective-permute-done.11
  75.0 3.7 %collective-permute-done.10 = bf16[256,512]{1,0:T(8,128)(2,1)S(1)} collective-permute-done((bf16[256,512]{1,0:T(8,128)(2,1)S(1)}, bf16[256,512]{1,0:T(8,128)(2,1)S(1)}, u32[]{:S(2)}, u32[]{:S(2)}) %collective-permute-start.10) | collective-permute-done | bytes 262176 | tf_op jit(solution)/shard_map/ppermute | solution.py:436
  78.8 0.1 fusion
  78.8 0.1 collective-permute-start.15
  78.9 0.1 collective-permute-start.16
  79.0 0.1 pad_maximum_fusion
  79.0 0.4 collective-permute-start.17
  79.4 2.3 %collective-permute-done.15 = bf16[2,512,512]{2,1,0:T(8,128)(2,1)S(1)} collective-permute-done((bf16[2,512,512]{2,1,0:T(8,128)(2,1)}, bf16[2,512,512]{2,1,0:T(8,128)(2,1)S(1)}, u32[]{:S(2)}, u32[]{:S(2)}) %collective-permute-start.15) | collective-permute-done | bytes 1048608 | tf_op jit(solution)/shard_map/ppermute | solution.py:433
  81.8 1.5 %add_convert_fusion = bf16[2,512,512]{2,1,0:T(8,128)(2,1)S(1)} fusion(bf16[2,512,512]{2,1,0:T(8,128)(2,1)S(1)} %collective-permute-done.15, bf16[2,512,512]{2,1,0:T(8,128)(2,1)} %get-tuple-element.51), kind=kLoop, calls=%fused_computation | loop fusion | flops 2097152 | bytes 3145728 | tf_op jit(solution)/shard_map/convert_element_type | solution.py:419
  83.3 0.1 fusion.1
  83.4 0.0 collective-permute-done.16
  83.4 0.1 collective-permute-start.19
  83.5 0.1 pad_maximum_fusion.1
  83.6 0.3 collective-permute-start.18
  83.9 3.9 %collective-permute-done.19 = bf16[2,64,256]{2,1,0:T(8,128)(2,1)S(1)} collective-permute-done((bf16[2,64,256]{2,1,0:T(8,128)(2,1)S(1)}, bf16[2,64,256]{2,1,0:T(8,128)(2,1)S(1)}, u32[]{:S(2)}, u32[]{:S(2)}) %collective-permute-start.19) | collective-permute-done | bytes 65568 | tf_op jit(solution)/shard_map/ppermute | solution.py:439
  87.8 0.1 collective-permute-start.20
  87.9 5.5 %collective-permute-done.20 = bf16[2,64,256]{2,1,0:T(8,128)(2,1)S(1)} collective-permute-done((bf16[2,64,256]{2,1,0:T(8,128)(2,1)S(1)}, bf16[2,64,256]{2,1,0:T(8,128)(2,1)S(1)}, u32[]{:S(2)}, u32[]{:S(2)}) %collective-permute-start.20) | collective-permute-done | bytes 65568 | tf_op jit(solution)/shard_map/ppermute | solution.py:439
  93.3 0.7 fusion.5
  94.0 7.1 %collective-permute-done.18 = bf16[2,256,512]{2,1,0:T(8,128)(2,1)S(1)} collective-permute-done((bf16[2,256,512]{2,1,0:T(8,128)(2,1)S(1)}, bf16[2,256,512]{2,1,0:T(8,128)(2,1)S(1)}, u32[]{:S(2)}, u32[]{:S(2)}) %collective-permute-start.18) | collective-permute-done | bytes 524320 | tf_op jit(solution)/shard_map/ppermute | solution.py:436
  101.1 0.1 add_convert_fusion.3
  101.2 1.1 %add_bitcast_fusion = f32[1,2,256,512]{3,2,1,0:T(8,128)} fusion(bf16[2,256,512]{2,1,0:T(8,128)(2,1)S(1)} %collective-permute-done.18, bf16[1,256,512]{2,1,0:T(8,128)(2,1)S(1)} %get-tuple-element.57, bf16[1,256,512]{2,1,0:T(8,128)(2,1)S(1)} %get-tuple-element.56), kind=kLoop, calls=%fused_computation.2 | loop fusion | flops 1048576 | bytes 2097152 | tf_op jit(solution)/shard_map/broadcast_in_dim | solution.py:645
  (29 shorter events, 0.1 us)
Async XLA Ops:
  0.6 8.9 %copy-start = (s32[16,2]{0,1:T(2,128)S(1)}, s32[16,2]{0,1:T(2,128)}, u32[]{:S(2)}) copy-start(s32[16,2]{0,1:T(2,128)} %param.8) | copy-start | bytes 388
  1.9 15.3 %copy-start.2 = (bf16[2,256,512]{2,1,0:T(8,128)(2,1)}, bf16[2,256,512]{2,1,0:T(8,128)(2,1)S(1)}, u32[]{:S(2)}) copy-start(bf16[2,256,512]{2,1,0:T(8,128)(2,1)S(1)} %convert_bitcast_fusion.refs_0_) | copy-start | bytes 1572868
  2.0 19.4 %collective-permute-start.3 = (bf16[2,256,512]{2,1,0:T(8,128)(2,1)S(1)}, bf16[2,256,512]{2,1,0:T(8,128)(2,1)S(1)}, u32[]{:S(2)}, u32[]{:S(2)}) collective-permute-start(bf16[2,256,512]{2,1,0:T(8,128)(2,1)S(1)} %convert_bitcast_fusion.refs_0_), channel_id=1, source_target_pairs={{0,16},{8,24},{16,0},{24,8},{1,17},{9,25},{17,1},{25,9},{2,18},{10... | collective-permute-start | bytes 1572872 | tf_op jit(solution)/shard_map/ppermute | solution.py:433
  5.0 22.2 %collective-permute-start.1 = (bf16[2,256,512]{2,1,0:T(8,128)(2,1)S(1)}, bf16[2,256,512]{2,1,0:T(8,128)(2,1)S(1)}, u32[]{:S(2)}, u32[]{:S(2)}) collective-permute-start(bf16[2,256,512]{2,1,0:T(8,128)(2,1)S(1)} %convert_bitcast_fusion.refs_0_), channel_id=1, source_target_pairs={{0,8},{8,0},{16,24},{24,16},{1,9},{9,1},{17,25},{25,17},{2,10},{10... | collective-permute-start | bytes 1572872 | tf_op jit(solution)/shard_map/ppermute | solution.py:433
  5.0 16.4 %collective-permute-start = (bf16[2,256,512]{2,1,0:T(8,128)(2,1)S(1)}, bf16[2,256,512]{2,1,0:T(8,128)(2,1)S(1)}, u32[]{:S(2)}, u32[]{:S(2)}) collective-permute-start(bf16[2,256,512]{2,1,0:T(8,128)(2,1)S(1)} %convert_bitcast_fusion.refs_0_), channel_id=1, source_target_pairs={{0,7},{1,0},{2,1},{3,2},{4,3},{5,4},{6,5},{7,6},{8,15},{9,8},{10,9... | collective-permute-start | bytes 1572872 | tf_op jit(solution)/shard_map/ppermute | solution.py:436
  21.4 5.8 %copy-start.3 = (bf16[2,256,512]{2,1,0:T(8,128)(2,1)}, bf16[2,256,512]{2,1,0:T(8,128)(2,1)S(1)}, u32[]{:S(2)}) copy-start(bf16[2,256,512]{2,1,0:T(8,128)(2,1)S(1)} %collective-permute-done.refs_1_) | copy-start | bytes 1572868
  21.4 5.8 %collective-permute-start.2 = (bf16[2,256,512]{2,1,0:T(8,128)(2,1)S(1)}, bf16[2,256,512]{2,1,0:T(8,128)(2,1)S(1)}, u32[]{:S(2)}, u32[]{:S(2)}) collective-permute-start(bf16[2,256,512]{2,1,0:T(8,128)(2,1)S(1)} %collective-permute-done.refs_1_), channel_id=1, source_target_pairs={{0,8},{8,0},{16,24},{24,16},{1,9},{9,1},{17,25},{25,17},{2,10},{10... | collective-permute-start | bytes 1572872 | tf_op jit(solution)/shard_map/ppermute | solution.py:433
  21.4 15.4 %copy-start.4 = (bf16[2,256,512]{2,1,0:T(8,128)(2,1)}, bf16[2,256,512]{2,1,0:T(8,128)(2,1)S(1)}, u32[]{:S(2)}) copy-start(bf16[2,256,512]{2,1,0:T(8,128)(2,1)S(1)} %collective-permute-done.3.refs_0_) | copy-start | bytes 1572868
  21.4 15.4 %collective-permute-start.4 = (bf16[256,512]{1,0:T(8,128)(2,1)S(1)}, bf16[256,512]{1,0:T(8,128)(2,1)S(1)}, u32[]{:S(2)}, u32[]{:S(2)}) collective-permute-start(bf16[256,512]{1,0:T(8,128)(2,1)S(1)} %slice_bitcast_fusion.2), channel_id=1, source_target_pairs={{0,16},{8,24},{16,0},{24,8},{1,17},{9,25},{17,1},{25,9},{2,18},{10... | collective-permute-start | bytes 786440 | tf_op jit(solution)/shard_map/ppermute | solution.py:433
  22.0 14.9 %collective-permute-start.5 = (bf16[256,512]{1,0:T(8,128)(2,1)S(1)}, bf16[256,512]{1,0:T(8,128)(2,1)S(1)}, u32[]{:S(2)}, u32[]{:S(2)}) collective-permute-start(bf16[256,512]{1,0:T(8,128)(2,1)S(1)} %slice_bitcast_fusion.1), channel_id=1, source_target_pairs={{0,7},{1,0},{2,1},{3,2},{4,3},{5,4},{6,5},{7,6},{8,15},{9,8},{10,9... | collective-permute-start | bytes 786440 | tf_op jit(solution)/shard_map/ppermute | solution.py:436
  27.2 0.8 copy-start.5
  28.0 0.8 copy-start.6
  36.8 2.7 %collective-permute-start.6 = (bf16[2,256,512]{2,1,0:T(8,128)(2,1)S(1)}, bf16[2,256,512]{2,1,0:T(8,128)(2,1)S(1)}, u32[]{:S(2)}, u32[]{:S(2)}) collective-permute-start(bf16[2,256,512]{2,1,0:T(8,128)(2,1)S(1)} %collective-permute-done.3.refs_0_), channel_id=1, source_target_pairs={{0,8},{8,0},{16,24},{24,16},{1,9},{9,1},{17,25},{25,17},{2,10},{10... | collective-permute-start | bytes 1572872 | tf_op jit(solution)/shard_map/ppermute | solution.py:433
  36.9 2.6 %copy-start.9 = (bf16[256,512]{1,0:T(8,128)(2,1)}, bf16[256,512]{1,0:T(8,128)(2,1)S(1)}, u32[]{:S(2)}) copy-start(bf16[256,512]{1,0:T(8,128)(2,1)S(1)} %collective-permute-done.5.refs_2_) | copy-start | bytes 786436
  36.9 2.6 %copy-start.8 = (bf16[256,512]{1,0:T(8,128)(2,1)}, bf16[256,512]{1,0:T(8,128)(2,1)S(1)}, u32[]{:S(2)}) copy-start(bf16[256,512]{1,0:T(8,128)(2,1)S(1)} %collective-permute-done.4.refs_1_) | copy-start | bytes 786436
  36.9 2.2 %collective-permute-start.7 = (bf16[256,512]{1,0:T(8,128)(2,1)S(1)}, bf16[256,512]{1,0:T(8,128)(2,1)S(1)}, u32[]{:S(2)}, u32[]{:S(2)}) collective-permute-start(bf16[256,512]{1,0:T(8,128)(2,1)S(1)} %collective-permute-done.4.refs_1_), channel_id=1, source_target_pairs={{0,8},{8,0},{16,24},{24,16},{1,9},{9,1},{17,25},{25,17},{2,10},{10... | collective-permute-start | bytes 786440 | tf_op jit(solution)/shard_map/ppermute | solution.py:433
  37.5 2.1 %collective-permute-start.8 = (bf16[256,512]{1,0:T(8,128)(2,1)S(1)}, bf16[256,512]{1,0:T(8,128)(2,1)S(1)}, u32[]{:S(2)}, u32[]{:S(2)}) collective-permute-start(bf16[256,512]{1,0:T(8,128)(2,1)S(1)} %collective-permute-done.5.refs_2_), channel_id=1, source_target_pairs={{0,8},{8,0},{16,24},{24,16},{1,9},{9,1},{17,25},{25,17},{2,10},{10... | collective-permute-start | bytes 786440 | tf_op jit(solution)/shard_map/ppermute | solution.py:433
  39.1 0.7 copy-start.10
  39.5 0.7 copy-start.11
  40.2 0.8 copy-start.7
  53.3 12.0 %collective-permute-start.9 = (bf16[2,512,512]{2,1,0:T(8,128)(2,1)}, bf16[2,512,512]{2,1,0:T(8,128)(2,1)S(1)}, u32[]{:S(2)}, u32[]{:S(2)}) collective-permute-start(bf16[2,512,512]{2,1,0:T(8,128)(2,1)} %get-tuple-element.36), channel_id=1, source_target_pairs={{0,8},{8,0},{16,24},{24,16},{1,9},{9,1},{17,25},{25,17},{2,10},{10... | collective-permute-start | bytes 3145736 | tf_op jit(solution)/shard_map/ppermute | solution.py:433
  53.5 11.8 %copy-start.1 = (bf16[2,512,512]{2,1,0:T(8,128)(2,1)S(1)}, bf16[2,512,512]{2,1,0:T(8,128)(2,1)}, u32[]{:S(2)}) copy-start(bf16[2,512,512]{2,1,0:T(8,128)(2,1)} %get-tuple-element.35) | copy-start | bytes 3145732
  63.1 10.8 %collective-permute-start.14 = (bf16[2,64,256]{2,1,0:T(8,128)(2,1)S(1)}, bf16[2,64,256]{2,1,0:T(8,128)(2,1)S(1)}, u32[]{:S(2)}, u32[]{:S(2)}) collective-permute-start(bf16[2,64,256]{2,1,0:T(8,128)(2,1)S(1)} %get-tuple-element.61), channel_id=1, source_target_pairs={{0,24},{8,16},{16,8},{24,0},{1,25},{9,17},{17,9},{25,1},{2,26},{10... | collective-permute-start | bytes 196616 | tf_op jit(solution)/shard_map/ppermute | solution.py:433
  65.2 8.8 %collective-permute-start.13 = (bf16[2,64,256]{2,1,0:T(8,128)(2,1)S(1)}, bf16[2,64,256]{2,1,0:T(8,128)(2,1)S(1)}, u32[]{:S(2)}, u32[]{:S(2)}) collective-permute-start(bf16[2,64,256]{2,1,0:T(8,128)(2,1)S(1)} %get-tuple-element.62), channel_id=1, source_target_pairs={{0,16},{8,24},{16,0},{24,8},{1,17},{9,25},{17,1},{25,9},{2,18},{10... | collective-permute-start | bytes 196616 | tf_op jit(solution)/shard_map/ppermute | solution.py:433
  65.3 8.7 %collective-permute-start.12 = (bf16[2,64,256]{2,1,0:T(8,128)(2,1)S(1)}, bf16[2,64,256]{2,1,0:T(8,128)(2,1)S(1)}, u32[]{:S(2)}, u32[]{:S(2)}) collective-permute-start(bf16[2,64,256]{2,1,0:T(8,128)(2,1)S(1)} %get-tuple-element.63), channel_id=1, source_target_pairs={{0,8},{8,0},{16,24},{24,16},{1,9},{9,1},{17,25},{25,17},{2,10},{10... | collective-permute-start | bytes 196616 | tf_op jit(solution)/shard_map/ppermute | solution.py:433
  65.7 9.3 %collective-permute-start.11 = (bf16[256,512]{1,0:T(8,128)(2,1)S(1)}, bf16[256,512]{1,0:T(8,128)(2,1)S(1)}, u32[]{:S(2)}, u32[]{:S(2)}) collective-permute-start(bf16[256,512]{1,0:T(8,128)(2,1)S(1)} %get-tuple-element.59), channel_id=1, source_target_pairs={{0,16},{8,24},{16,0},{24,8},{1,17},{9,25},{17,1},{25,9},{2,18},{10... | collective-permute-start | bytes 786440 | tf_op jit(solution)/shard_map/ppermute | solution.py:433
  67.6 11.1 %collective-permute-start.10 = (bf16[256,512]{1,0:T(8,128)(2,1)S(1)}, bf16[256,512]{1,0:T(8,128)(2,1)S(1)}, u32[]{:S(2)}, u32[]{:S(2)}) collective-permute-start(bf16[256,512]{1,0:T(8,128)(2,1)S(1)} %get-tuple-element.60), channel_id=1, source_target_pairs={{0,1},{1,2},{2,3},{3,4},{4,5},{5,6},{6,7},{7,0},{8,9},{9,10},{10,1... | collective-permute-start | bytes 786440 | tf_op jit(solution)/shard_map/ppermute | solution.py:436
  78.8 2.9 %collective-permute-start.15 = (bf16[2,512,512]{2,1,0:T(8,128)(2,1)}, bf16[2,512,512]{2,1,0:T(8,128)(2,1)S(1)}, u32[]{:S(2)}, u32[]{:S(2)}) collective-permute-start(bf16[2,512,512]{2,1,0:T(8,128)(2,1)} %get-tuple-element.52), channel_id=1, source_target_pairs={{0,8},{8,0},{16,24},{24,16},{1,9},{9,1},{17,25},{25,17},{2,10},{10... | collective-permute-start | bytes 3145736 | tf_op jit(solution)/shard_map/ppermute | solution.py:433
  78.9 4.5 %collective-permute-start.16 = (bf16[2,64,256]{2,1,0:T(8,128)(2,1)S(1)}, bf16[2,64,256]{2,1,0:T(8,128)(2,1)S(1)}, u32[]{:S(2)}, u32[]{:S(2)}) collective-permute-start(bf16[2,64,256]{2,1,0:T(8,128)(2,1)S(1)} %fusion.4), channel_id=1, source_target_pairs={{0,1},{1,0},{2,3},{3,2},{4,5},{5,4},{6,7},{7,6},{8,9},{9,8},{10,11... | collective-permute-start | bytes 196616 | tf_op jit(solution)/shard_map/ppermute | solution.py:439
  79.0 15.0 %collective-permute-start.17 = (bf16[2,256,512]{2,1,0:T(8,128)(2,1)S(1)}, bf16[2,256,512]{2,1,0:T(8,128)(2,1)S(1)}, u32[]{:S(2)}, u32[]{:S(2)}) collective-permute-start(bf16[2,256,512]{2,1,0:T(8,128)(2,1)S(1)} %pad_maximum_fusion), channel_id=1, source_target_pairs={{0,16},{8,24},{16,0},{24,8},{1,17},{9,25},{17,1},{25,9},{2,18},{10... | collective-permute-start | bytes 1572872 | tf_op jit(solution)/shard_map/ppermute | solution.py:433
  83.4 4.3 %collective-permute-start.19 = (bf16[2,64,256]{2,1,0:T(8,128)(2,1)S(1)}, bf16[2,64,256]{2,1,0:T(8,128)(2,1)S(1)}, u32[]{:S(2)}, u32[]{:S(2)}) collective-permute-start(bf16[2,64,256]{2,1,0:T(8,128)(2,1)S(1)} %add_convert_fusion.7), channel_id=1, source_target_pairs={{0,2},{1,3},{2,0},{3,1},{4,6},{5,7},{6,4},{7,5},{8,10},{9,11},{10,... | collective-permute-start | bytes 196616 | tf_op jit(solution)/shard_map/ppermute | solution.py:439
  83.6 17.5 %collective-permute-start.18 = (bf16[2,256,512]{2,1,0:T(8,128)(2,1)S(1)}, bf16[2,256,512]{2,1,0:T(8,128)(2,1)S(1)}, u32[]{:S(2)}, u32[]{:S(2)}) collective-permute-start(bf16[2,256,512]{2,1,0:T(8,128)(2,1)S(1)} %pad_maximum_fusion.1), channel_id=1, source_target_pairs={{0,1},{1,2},{2,3},{3,4},{4,5},{5,6},{6,7},{7,0},{8,9},{9,10},{10,1... | collective-permute-start | bytes 1572872 | tf_op jit(solution)/shard_map/ppermute | solution.py:436
  87.8 5.6 %collective-permute-start.20 = (bf16[2,64,256]{2,1,0:T(8,128)(2,1)S(1)}, bf16[2,64,256]{2,1,0:T(8,128)(2,1)S(1)}, u32[]{:S(2)}, u32[]{:S(2)}) collective-permute-start(bf16[2,64,256]{2,1,0:T(8,128)(2,1)S(1)} %add_convert_fusion.6), channel_id=1, source_target_pairs={{0,4},{1,5},{2,6},{3,7},{4,0},{5,1},{6,2},{7,3},{8,12},{9,13},{10,... | collective-permute-start | bytes 196616 | tf_op jit(solution)/shard_map/ppermute | solution.py:439

commit v4 on v3

--- a/solution.py
+++ b/solution.py
@@ -15,7 +15,7 @@
 f32 = jnp.float32
 bf16 = jnp.bfloat16
 CHUNK = 16
-VMEM_LIMIT = 54 * 2**20
+VMEM_LIMIT = 36 * 2**20
 COST = 6
 
 
@@ -36,32 +36,65 @@
     return right.astype(ml_dtypes.bfloat16), left.astype(ml_dtypes.bfloat16)
 
 
-def propagate(x_ref, right_ref, left_ref, z_ref, out_ref):
+def half_steps(x_ref, right_ref, left_ref, z_ref, out_refs):
     w = z_ref.shape[1]
-    z = jnp.dot(x_ref[...], right_ref[...], preferred_element_type=f32)
-    z_ref[:w] = z[:, :w].astype(bf16)
-    z_ref[w:] = z[:, w:].astype(bf16)
-    y = jnp.dot(left_ref[...], z_ref[...], preferred_element_type=f32)
-    out_ref[0] = y[:w].astype(out_ref.dtype)
-    out_ref[1] = y[w:].astype(out_ref.dtype)
+
+    def first():
+        z = jnp.dot(x_ref[...], right_ref[...], preferred_element_type=f32)
+        z_ref[:w] = z[:, :w].astype(bf16)
+        z_ref[w:] = z[:, w:].astype(bf16)
+
+    def second():
+        y = jnp.dot(left_ref[...], z_ref[...], preferred_element_type=f32)
+        for out_ref in out_refs:
+            out_ref[0] = y[:w].astype(out_ref.dtype)
+            out_ref[1] = y[w:].astype(out_ref.dtype)
+
+    return first, second
 
 
 class Alternating:
     def __init__(self):
-        self.waiting = None
+        self.queue = []
+        self.held = None
+
+    def release(self):
+        if self.held is not None:
+            self.queue.append(self.held)
+        self.held = None
+
+    def run(self, count):
+        for task in self.queue[:count]:
+            task()
+        del self.queue[:count]
 
     def flush(self):
-        if self.waiting is not None:
-            self.waiting()
-        self.waiting = None
-
-    def matrix(self, task):
-        self.flush()
-        self.waiting = task
-
-    def vector(self, task):
+        self.release()
+        self.run(len(self.queue))
+
+    def matrix(self, steps, then=None):
+        first, second = steps
+
+        def finish():
+            second()
+            finish.done = True
+            if then is not None:
+                then()
+
+        finish.done = False
+        self.queue.append(first)
+        self.release()
+        self.held = finish
+        return finish
+
+    def vector(self, task, need=None):
+        if need is not None and not need.done:
+            if need is self.held:
+                self.release()
+            while not need.done:
+                self.run(1)
         task()
-        self.flush()
+        self.run(2)
 
 
 class Copies:
@@ -195,17 +228,21 @@
         x_ref[p, :, w:] = (ki * lr - kr * li).astype(bf16)
 
     def spread(p):
-        propagate(x_ref.at[p], right_ref, left_ref, z_ref.at[p % 2], init_ref.at[1, p])
-        leaving.append(copies.start(init_ref.at[1, p], init_hbm.at[1 - high, p]))
+        def leave():
+            leaving.append(copies.start(init_ref.at[1, p], init_hbm.at[1 - high, p]))
+
+        tasks.matrix(
+            half_steps(x_ref.at[p], right_ref, left_ref, z_ref.at[p], [init_ref.at[1, p]]), leave
+        )
 
     def launch(p):
-        init_ref[0, p, 0] = moved(p, probe_ref[0])
-        init_ref[0, p, 1] = moved(p, probe_ref[1])
+        init_ref[0, p, 0] = moved(p, probe_ref[0]).astype(bf16)
+        init_ref[0, p, 1] = moved(p, probe_ref[1]).astype(bf16)
         leaving.append(copies.start(init_ref.at[0, p], init_hbm.at[high, p]))
 
     for p in range(probes):
         tasks.vector(functools.partial(cotangent, p))
-        tasks.matrix(functools.partial(spread, p))
+        spread(p)
         tasks.vector(functools.partial(launch, p))
     tasks.flush()
     for copy in leaving:
@@ -215,29 +252,33 @@
 def near_kernel(probes, depth, pieces, meta_ref, _, right_ref, left_ref, *refs):
     n = len(pieces)
     half = depth // 2
-    piece_refs, (waves_hbm, ext_ref, a_ref, x_ref, z_ref, sems) = refs[:n], refs[n:]
-    w = a_ref.shape[-1]
+    piece_refs, refs = refs[:n], refs[n:]
+    waves_hbm, ext_ref, in_ref, a_ref, out_ref, x_ref, z_ref, sems = refs
+    w = in_ref.shape[-1]
     copies = Copies(sems)
-    arriving = [copies.start(waves_hbm.at[0, p], a_ref.at[0, p]) for p in range(probes)]
+    arriving = [copies.start(waves_hbm.at[0, p], in_ref.at[p]) for p in range(probes)]
     for copy in load_pieces(meta_ref, depth, copies, pieces, piece_refs, ext_ref, 0, w):
         copy.wait()
     leaving = []
     tasks = Alternating()
-
-    def spread(k, p):
-        propagate(x_ref.at[p], right_ref, left_ref, z_ref.at[p % 2], a_ref.at[k + 1, p])
-        leaving.append(copies.start(a_ref.at[k + 1, p], waves_hbm.at[2 + k, p]))
-
+    before = [None] * probes
     for k in range(half):
         for p in range(probes):
             if k == 0:
                 arriving[p].wait()
-            if probes == 1:
-                tasks.flush()
+            wave = in_ref.at[p] if k == 0 else a_ref.at[(k - 1) % 2, p]
             tasks.vector(
-                lambda: times_window(meta_ref, ext_ref, k, p, a_ref.at[k, p], to_product(x_ref.at[p]))
-            )
-            tasks.matrix(functools.partial(spread, k, p))
+                lambda: times_window(meta_ref, ext_ref, k, p, wave, to_product(x_ref.at[p])),
+                before[p],
+            )
+            outs = [out_ref.at[k, p]] + ([a_ref.at[k % 2, p]] if k < half - 1 else [])
+
+            def leave(k=k, p=p):
+                leaving.append(copies.start(out_ref.at[k, p], waves_hbm.at[2 + k, p]))
+
+            before[p] = tasks.matrix(
+                half_steps(x_ref.at[p], right_ref, left_ref, z_ref.at[p], outs), leave
+            )
     tasks.flush()
     for copy in leaving:
         copy.wait()
@@ -248,54 +289,56 @@
     half = depth // 2
     piece_refs, refs = refs[:n], refs[n:]
     g_hbm, refs = refs[:half], refs[half:]
-    waves_hbm, next_hbm, v_hbm, ext_ref, g_ref, a_ref, b_ref, xa_ref, xb_ref, z_ref, sems = refs
-    w = a_ref.shape[-1]
+    waves_hbm, next_hbm, v_hbm, ext_ref, g_ref, in_ref, a_ref, b_ref, xa_ref, xb_ref, z_ref, sems = refs
+    w = in_ref.shape[-1]
     high = meta_ref[1]
     copies = Copies(sems)
-    a_in = [copies.start(waves_hbm.at[1 + half, p], a_ref.at[0, p]) for p in range(probes)]
-    b_in = [copies.start(waves_hbm.at[1, p], b_ref.at[0, p]) for p in range(probes)]
+    a_in = [copies.start(waves_hbm.at[1 + half, p], in_ref.at[0, p]) for p in range(probes)]
+    b_in = [copies.start(waves_hbm.at[1, p], in_ref.at[1, p]) for p in range(probes)]
     for copy in load_pieces(meta_ref, depth, copies, pieces, piece_refs, ext_ref, half, w):
         copy.wait()
     tasks = Alternating()
-
-    def spread(p, x, out):
-        propagate(x, right_ref, left_ref, z_ref.at[p % 2], out)
-
+    a_waves = [each(in_ref.at[0], probes)]
+    a_waves += [each(a_ref.at[k], probes) for k in range(half - 1)]
+    before = [None] * probes
     for k in range(half - 1):
         for p in range(probes):
             if k == 0:
                 a_in[p].wait()
-            if probes == 1:
-                tasks.flush()
             tasks.vector(
                 lambda: times_window(
-                    meta_ref, ext_ref, k, p, a_ref.at[k, p], to_product(xa_ref.at[p])
-                )
-            )
-            tasks.matrix(functools.partial(spread, p, xa_ref.at[p], a_ref.at[k + 1, p]))
+                    meta_ref, ext_ref, k, p, a_waves[k][p], to_product(xa_ref.at[p])
+                ),
+                before[p],
+            )
+            before[p] = tasks.matrix(
+                half_steps(xa_ref.at[p], right_ref, left_ref, z_ref.at[p], [a_waves[k + 1][p]])
+            )
     leaving = []
+    before = [None] * probes
     for k in range(half):
         last = k == half - 1
-        now, later = k % 2, (k + 1) % 2
         at = half - 1 - k
-        parts = gradient_parts(
-            meta_ref, g_ref.at[at], each(a_ref.at[at], probes), each(b_ref.at[now], probes), probes
-        )
+        b_now = each(in_ref.at[1] if k == 0 else b_ref.at[(k - 1) % 2], probes)
         for p in range(probes):
             if k == 0:
                 b_in[p].wait()
-            if probes == 1:
-                tasks.flush()
             tasks.vector(
-                lambda: times_window(
-                    meta_ref, ext_ref, at, p, b_ref.at[now, p], to_product(xb_ref.at[p])
-                )
+                lambda: times_window(meta_ref, ext_ref, at, p, b_now[p], to_product(xb_ref.at[p])),
+                before[p],
             )
             if last:
                 leaving.append(copies.start(xb_ref.at[p], next_hbm.at[p]))
+        tasks.flush()
+        parts = gradient_parts(meta_ref, g_ref.at[at], a_waves[at], b_now, probes)
         for p in range(probes):
             if not last:
-                tasks.matrix(functools.partial(spread, p, xb_ref.at[p], b_ref.at[later, p]))
+                before[p] = tasks.matrix(
+                    half_steps(
+                        xb_ref.at[p], right_ref, left_ref, z_ref.at[p], [b_ref.at[k % 2, p]]
+                    )
+                )
+        for p in range(probes):
             tasks.vector(parts[p])
         tasks.flush()
         if k == 0:
@@ -309,7 +352,7 @@
                         v_ref[rows, :w] = real.astype(bf16)
                         v_ref[rows, w:] = -imag.astype(bf16)
 
-                    times_window(meta_ref, ext_ref, half - 1, p, a_ref.at[half - 1, p], write)
+                    times_window(meta_ref, ext_ref, half - 1, p, a_waves[half - 1][p], write)
 
     leaving.append(copies.start(xa_ref, v_hbm))
     for slot in range(half):
@@ -323,7 +366,7 @@
     n = len(pieces)
     half = depth // 2
     piece_refs, refs = refs[:n], refs[n:]
-    waves_hbm, lam_hbm, ext_ref, b_ref, x_ref, v_ref, z_ref, t_ref, lam_ref, sems = refs
+    waves_hbm, lam_hbm, ext_ref, b_ref, out_ref, x_ref, v_ref, z_ref, t_ref, lam_ref, sems = refs
     w = x_ref.shape[1]
     copies = Copies(sems)
     x_in = [copies.start(x_hbm.at[p], x_ref.at[p]) for p in range(probes)]
@@ -332,27 +375,32 @@
     tasks = Alternating()
     leaving = []
 
-    def spread(k, p):
-        propagate(x_ref.at[p], right_ref, left_ref, z_ref.at[p % 2], b_ref.at[k, p])
-        leaving.append(copies.start(b_ref.at[k, p], waves_hbm.at[2 + half + k, p]))
-
     def multiply(k, p):
         if k == 0 and p == 0:
             for copy in arrived:
                 copy.wait()
         times_window(
-            meta_ref, ext_ref, half - 1 - k, p, b_ref.at[k, p], to_product(x_ref.at[p])
+            meta_ref, ext_ref, half - 1 - k, p, b_ref.at[k % 2, p], to_product(x_ref.at[p])
         )
 
     for k in range(half):
+        ready = []
         for p in range(probes):
             if k == 0:
                 x_in[p].wait()
-            tasks.matrix(functools.partial(spread, k, p))
-            if p:
-                tasks.vector(functools.partial(multiply, k, p - 1))
-        tasks.flush()
-        multiply(k, probes - 1)
+
+            def leave(k=k, p=p):
+                leaving.append(copies.start(out_ref.at[k, p], waves_hbm.at[2 + half + k, p]))
+
+            outs = [b_ref.at[k % 2, p], out_ref.at[k, p]]
+            ready.append(
+                tasks.matrix(
+                    half_steps(x_ref.at[p], right_ref, left_ref, z_ref.at[p], outs), leave
+                )
+            )
+        for p in range(probes):
+            tasks.vector(functools.partial(multiply, k, p), ready[p])
+    tasks.flush()
     low = meta_ref[1] == 0
     for plane in range(2):
         total = None
@@ -455,7 +503,7 @@
     wave = (probes, 2, w, w)
     product = (probes, w, 2 * w)
     g_shape = (2, 2 * w, columns)
-    z_scratch = pltpu.VMEM((2, 2 * w, w), bf16)
+    z_scratch = pltpu.VMEM((probes, 2 * w, w), bf16)
     ext_scratch = pltpu.VMEM((half, 2, 2 * w, columns), bf16)
 
     def call(kernel, name, steps, outs, ins, scratch, copies, limit=VMEM_LIMIT, aliases={}):
@@ -476,7 +524,8 @@
     shape = jax.ShapeDtypeStruct
     sides_in = [(vmem, right), (vmem, left)]
 
-    all_waves = shape((2 + depth,) + wave, f32)
+    rows = max(2 + depth, 32 * 2**20 // (4 * probes * w * w))
+    all_waves = shape((rows,) + wave, bf16)
     init = call(
         functools.partial(start_kernel, probes, scale),
         "first_waves",
@@ -485,7 +534,7 @@
         [(smem, meta), (vmem, probe), (hbm, exit_cotangent)] + sides_in,
         [
             pltpu.VMEM(wave, f32),
-            pltpu.VMEM((2,) + wave, f32),
+            pltpu.VMEM((2,) + wave, bf16),
             pltpu.VMEM(product, bf16),
             z_scratch,
         ],
@@ -534,7 +583,14 @@
         half,
         all_waves,
         [(smem, meta), (hbm, init)] + sides_in + arrays,
-        [ext_scratch, pltpu.VMEM((half + 1,) + wave, f32), pltpu.VMEM(product, bf16), z_scratch],
+        [
+            ext_scratch,
+            pltpu.VMEM(wave, bf16),
+            pltpu.VMEM((2,) + wave, f32),
+            pltpu.VMEM((half,) + wave, bf16),
+            pltpu.VMEM(product, bf16),
+            z_scratch,
+        ],
         probes * (half + 1) + len(names),
         aliases={1: 0},
     )
@@ -550,7 +606,8 @@
         [
             ext_scratch,
             pltpu.VMEM((half,) + g_shape, bf16),
-            pltpu.VMEM((half,) + wave, f32),
+            pltpu.VMEM((2,) + wave, bf16),
+            pltpu.VMEM((half - 1,) + wave, f32),
             pltpu.VMEM((2,) + wave, f32),
             pltpu.VMEM(product, bf16),
             pltpu.VMEM(product, bf16),
@@ -568,7 +625,8 @@
         [(smem, meta), (hbm, waves), (hbm, next_x), (hbm, v)] + sides_in + arrays,
         [
             ext_scratch,
-            pltpu.VMEM((half,) + wave, f32),
+            pltpu.VMEM((2,) + wave, f32),
+            pltpu.VMEM((half,) + wave, bf16),
             pltpu.VMEM(product, bf16),
             pltpu.VMEM(product, bf16),
             z_scratch,
@@ -602,8 +660,8 @@
         [(smem, after(meta, far_sums)), (hbm, waves)],
         [
             pltpu.VMEM((half,) + g_shape, bf16),
-            pltpu.VMEM((half,) + wave, f32),
-            pltpu.VMEM((half,) + wave, f32),
+            pltpu.VMEM((half,) + wave, bf16),
+            pltpu.VMEM((half,) + wave, bf16),
         ],
         3 * half,
         aliases={1: half},

time: 103 us -> 89.5 us (0.87)
  Pallas kernels: 42.1 us -> 30.4 us
  waiting for transfers between devices: 28.8 us -> 33 us
  local copies, waits for them, and re-layouts: 4.36 us -> 0.4 us
  other arithmetic: 6.8 us -> 4.77 us
    pallas_call x5, Pallas kernels: 42.1 us -> 30.4 us  [call(): pl.pallas_call(kernel, out_shape=flat, in_specs=[spec for spec, _ in ins]...]
    unnamed x24 -> x8, local copies, waits for them, and re-layouts: 3.08 us -> 0.02 us
    ppermute x14, waiting for transfers between devices: 4.53 us -> 7.32 us  [across(): return lax.ppermute(value, 'depth', [(i, i ^ bit) for i in range(depth)])]
    ppermute x3, waiting for transfers between devices: 9.38 us -> 10.6 us  [along_xor(): return lax.ppermute(value, 'lat', [(i, i ^ bit) for i in range(lat)])]
    convert_element_type x6, other arithmetic: 2.05 us -> 0.87 us  [total(): return (first.astype(f32) + second.astype(f32)).astype(bf16)]
  transfers between devices with their start and end apart: 21 -> 21, of which waited for: 9 -> 10; matrix products, arithmetic and copies ran while one was open for 5% -> 3% of each run, Pallas kernels for 29% -> 25%
where the time goes in v4:
time: 89.5 us; the launch traced here: 88.7 us
  waiting for transfers between devices  33 us (37%)
  Pallas kernels  30.4 us (34%)
  starting transfers between devices  19.3 us (22%)
  other arithmetic  4.77 us (5%)
    pallas_call x5, Pallas kernels, call(): pl.pallas_call(kernel, out_shape=flat, in_specs=[spec for spec, _ in ins]...  30.4 us
    ppermute x4, waiting for transfers between devices, along(): lax.ppermute(value, 'lat', [(i, (i + steps) % lat) for i in range(lat)])  15.1 us
    ppermute x3, waiting for transfers between devices, along_xor(): return lax.ppermute(value, 'lat', [(i, i ^ bit) for i in range(lat)])  10.6 us
    ppermute x4, starting transfers between devices, along(): lax.ppermute(value, 'lat', [(i, (i + steps) % lat) for i in range(lat)])  10 us
    ppermute x14, starting transfers between devices, across(): return lax.ppermute(value, 'depth', [(i, i ^ bit) for i in range(depth)])  9.04 us
    ppermute x14, waiting for transfers between devices, across(): return lax.ppermute(value, 'depth', [(i, i ^ bit) for i in range(depth)])  7.32 us
  transfers between devices with their start and end apart: 21, of which 10 were waited for; matrix products, arithmetic and copies ran while one was open for 3% of the time, Pallas kernels for 25%

profile of v4, /device:TPU:0, one launch (start us, length us, event | category | flops | bytes accessed | tf_op | source)
XLA Modules:
  0.0 88.7 jit_solution(3165485716808825714)
XLA Ops:
  0.6 0.0 copy-start
  0.6 1.3 %convert_bitcast_fusion.refs_0_ = bf16[2,256,512]{2,1,0:T(8,128)(2,1)S(1)} fusion(f32[1,2,256,512]{3,2,1,0:T(8,128)} %param.6), kind=kLoop, calls=%fused_computation.10 | loop fusion | flops 262144 | bytes 1572864 | tf_op jit(solution)/shard_map/convert_element_type | solution.py:492
  1.9 3.0 %collective-permute-start.3 = (bf16[2,256,512]{2,1,0:T(8,128)(2,1)S(1)}, bf16[2,256,512]{2,1,0:T(8,128)(2,1)S(1)}, u32[]{:S(2)}, u32[]{:S(2)}) collective-permute-start(bf16[2,256,512]{2,1,0:T(8,128)(2,1)S(1)} %convert_bitcast_fusion.refs_0_), channel_id=1, source_target_pairs={{0,16},{8,24},{16,0},{24,8},{1,17},{9,25},{17,1},{25,9},{2,18},{10... | collective-permute-start | bytes 1572872 | tf_op jit(solution)/shard_map/ppermute | solution.py:481
  5.0 0.0 collective-permute-start.1
  5.0 4.5 %collective-permute-start = (bf16[2,256,512]{2,1,0:T(8,128)(2,1)S(1)}, bf16[2,256,512]{2,1,0:T(8,128)(2,1)S(1)}, u32[]{:S(2)}, u32[]{:S(2)}) collective-permute-start(bf16[2,256,512]{2,1,0:T(8,128)(2,1)S(1)} %convert_bitcast_fusion.refs_0_), channel_id=1, source_target_pairs={{0,7},{1,0},{2,1},{3,2},{4,3},{5,4},{6,5},{7,6},{8,15},{9,8},{10,9... | collective-permute-start | bytes 1572872 | tf_op jit(solution)/shard_map/ppermute | solution.py:484
  9.5 0.1 constant_dynamic-slice_fusion
  9.6 0.1 copy.13
  9.7 0.1 reshape.12
  9.8 0.6 pad_add_fusion.meta_ref
  10.4 6.4 %first_waves.1._ = bf16[32,4,2,256,256]{4,3,2,1,0:T(8,128)(2,1)} custom-call(s32[10]{0:T(128)} %pad_add_fusion.meta_ref, f32[2,256,256]{2,1,0:T(8,128)} %probe_ref.1, f32[16,2,256,256]{3,2,1,0:T(8,128)} %cot_hbm.1, bf16[512,512]{1,0:T(8,128)(2,1)} %constant.17.clone.right_ref, bf16[512,512]{1,0:T(8,128)(2,1)} %constant.18.clone.left_ref), custom_call_target="tpu_custom_call" | custom-call | flops 6442450944 | bytes 8388608 | tf_op jit(solution)/shard_map/first_waves/pallas_call | solution.py:511
  16.8 4.6 %collective-permute-done.refs_1_ = bf16[2,256,512]{2,1,0:T(8,128)(2,1)S(1)} collective-permute-done((bf16[2,256,512]{2,1,0:T(8,128)(2,1)S(1)}, bf16[2,256,512]{2,1,0:T(8,128)(2,1)S(1)}, u32[]{:S(2)}, u32[]{:S(2)}) %collective-permute-start) | collective-permute-done | bytes 524320 | tf_op jit(solution)/shard_map/ppermute | solution.py:484
  21.4 0.0 collective-permute-start.2
  21.4 0.0 collective-permute-done.3.refs_0_
  21.4 0.6 collective-permute-start.4
  22.0 5.2 %collective-permute-start.5 = (bf16[256,512]{1,0:T(8,128)(2,1)S(1)}, bf16[256,512]{1,0:T(8,128)(2,1)S(1)}, u32[]{:S(2)}, u32[]{:S(2)}) collective-permute-start(bf16[256,512]{1,0:T(8,128)(2,1)S(1)} %slice_bitcast_fusion.1), channel_id=1, source_target_pairs={{0,7},{1,0},{2,1},{3,2},{4,3},{5,4},{6,5},{7,6},{8,15},{9,8},{10,9... | collective-permute-start | bytes 786440 | tf_op jit(solution)/shard_map/ppermute | solution.py:484
  27.2 0.0 collective-permute-done.1.refs_2_
  27.2 0.0 collective-permute-done.2.refs_3_
  27.2 0.0 copy-done.1
  27.2 5.9 %near_slices.1._ = bf16[32,4,2,256,256]{4,3,2,1,0:T(8,128)(2,1)} custom-call(s32[10]{0:T(128)S(1)} %copy-done.3, bf16[32,4,2,256,256]{4,3,2,1,0:T(8,128)(2,1)} %first_waves.1._, bf16[512,512]{1,0:T(8,128)(2,1)S(1)} %copy-done.2, bf16[512,512]{1,0:T(8,128)(2,1)S(1)} %copy-done.1, ...), custom_call_target="tpu_custom_call", output_to_operand_aliasing={{}: (1, {})} | custom-call | flops 12884901888 | bytes 8388608 | tf_op jit(solution)/shard_map/near_slices/pallas_call | solution.py:511
  33.2 0.1 collective-permute-start.6
  33.2 0.0 collective-permute-done.5.refs_2_
  33.2 0.0 collective-permute-done.4.refs_1_
  33.3 0.5 collective-permute-start.7
  33.7 0.1 collective-permute-start.8
  33.8 1.7 %collective-permute-done.7.refs_4_ = bf16[256,512]{1,0:T(8,128)(2,1)S(1)} collective-permute-done((bf16[256,512]{1,0:T(8,128)(2,1)S(1)}, bf16[256,512]{1,0:T(8,128)(2,1)S(1)}, u32[]{:S(2)}, u32[]{:S(2)}) %collective-permute-start.7) | collective-permute-done | bytes 262176 | tf_op jit(solution)/shard_map/ppermute | solution.py:481
  35.5 0.4 collective-permute-done.8.refs_5_
  35.9 0.0 collective-permute-done.6.refs_3_
  35.9 8.3 %far_slices.1 = (bf16[2,512,512]{2,1,0:T(8,128)(2,1)S(1)}, bf16[2,512,512]{2,1,0:T(8,128)(2,1)S(1)}, bf16[32,4,2,256,256]{4,3,2,1,0:T(8,128)(2,1)}, bf16[4,256,5...) custom-call(s32[10]{0:T(128)S(1)} %copy-done.3, ...), custom_call_target="tpu_custom_call", output_to_operand_aliasing={{2}: (1, {})} | custom-call | flops 12884901888 | bytes 8388608 | tf_op jit(solution)/shard_map/far_slices/pallas_call | solution.py:511
  44.2 0.2 collective-permute-start.9
  44.4 5.5 %return_waves.1 = (bf16[32,4,2,256,256]{4,3,2,1,0:T(8,128)(2,1)}, bf16[4,2,64,256]{3,2,1,0:T(8,128)(2,1)S(1)}) custom-call(s32[10]{0:T(128)S(1)} %copy-done.3, bf16[32,4,2,256,256]{4,3,2,1,0:T(8,128)(2,1)} %get-tuple-element.38._, bf16[4,256,512]{2,1,0:T(8,128)(2,1)S(1)} %get-tuple-element.39.x_hbm, ...), custom_call_target="tpu_custom_call", output_to_operand_aliasing={{0}: (1, {})} | custom-call | flops 12884901888 | bytes 8388608 | tf_op jit(solution)/shard_map/return_waves/pallas_call | solution.py:511
  50.0 2.0 %collective-permute-start.14 = (bf16[2,64,256]{2,1,0:T(8,128)(2,1)S(1)}, bf16[2,64,256]{2,1,0:T(8,128)(2,1)S(1)}, u32[]{:S(2)}, u32[]{:S(2)}) collective-permute-start(bf16[2,64,256]{2,1,0:T(8,128)(2,1)S(1)} %get-tuple-element.61), channel_id=1, source_target_pairs={{0,24},{8,16},{16,8},{24,0},{1,25},{9,17},{17,9},{25,1},{2,26},{10... | collective-permute-start | bytes 196616 | tf_op jit(solution)/shard_map/ppermute | solution.py:481
  52.0 0.1 collective-permute-start.13
  52.1 0.1 collective-permute-start.12
  52.2 0.0 collective-permute-done.9
  52.2 0.3 add_convert_fusion.1
  52.5 0.1 fusion.6
  52.6 1.9 %collective-permute-start.11 = (bf16[256,512]{1,0:T(8,128)(2,1)S(1)}, bf16[256,512]{1,0:T(8,128)(2,1)S(1)}, u32[]{:S(2)}, u32[]{:S(2)}) collective-permute-start(bf16[256,512]{1,0:T(8,128)(2,1)S(1)} %get-tuple-element.59), channel_id=1, source_target_pairs={{0,16},{8,24},{16,0},{24,8},{1,17},{9,25},{17,1},{25,9},{2,18},{10... | collective-permute-start | bytes 786440 | tf_op jit(solution)/shard_map/ppermute | solution.py:481
  54.5 0.0 collective-permute-start.10
  54.5 4.2 %near_gradients.1 = (bf16[2,512,512]{2,1,0:T(8,128)(2,1)S(1)}, bf16[2,512,512]{2,1,0:T(8,128)(2,1)S(1)}, bf16[32,4,2,256,256]{4,3,2,1,0:T(8,128)(2,1)}) custom-call(s32[10]{0:T(128)S(1)} %copy-done.3, bf16[32,4,2,256,256]{4,3,2,1,0:T(8,128)(2,1)} %get-tuple-element.41._), custom_call_target="tpu_custom_call", output_to_operand_aliasing={{2}: (1, {})} | custom-call | flops 12884901888 | bytes 8388608 | tf_op jit(solution)/shard_map/near_gradients/pallas_call | solution.py:511
  58.6 0.0 collective-permute-done.14
  58.7 0.0 collective-permute-done.13
  58.7 0.0 collective-permute-done.12
  58.7 3.1 %collective-permute-done.11 = bf16[256,512]{1,0:T(8,128)(2,1)S(1)} collective-permute-done((bf16[256,512]{1,0:T(8,128)(2,1)S(1)}, bf16[256,512]{1,0:T(8,128)(2,1)S(1)}, u32[]{:S(2)}, u32[]{:S(2)}) %collective-permute-start.11) | collective-permute-done | bytes 262176 | tf_op jit(solution)/shard_map/ppermute | solution.py:481
  61.9 3.7 %collective-permute-done.10 = bf16[256,512]{1,0:T(8,128)(2,1)S(1)} collective-permute-done((bf16[256,512]{1,0:T(8,128)(2,1)S(1)}, bf16[256,512]{1,0:T(8,128)(2,1)S(1)}, u32[]{:S(2)}, u32[]{:S(2)}) %collective-permute-start.10) | collective-permute-done | bytes 262176 | tf_op jit(solution)/shard_map/ppermute | solution.py:484
  65.6 0.1 fusion
  65.7 0.1 collective-permute-start.15
  65.8 0.1 collective-permute-start.16
  65.8 0.1 pad_maximum_fusion
  65.9 0.4 collective-permute-start.17
  66.3 2.1 %collective-permute-done.15 = bf16[2,512,512]{2,1,0:T(8,128)(2,1)S(1)} collective-permute-done((bf16[2,512,512]{2,1,0:T(8,128)(2,1)S(1)}, bf16[2,512,512]{2,1,0:T(8,128)(2,1)S(1)}, u32[]{:S(2)}, u32[]{:S(2)}) %collective-permute-start.15) | collective-permute-done | bytes 1048608 | tf_op jit(solution)/shard_map/ppermute | solution.py:481
  68.4 0.3 add_convert_fusion
  68.7 0.1 fusion.1
  68.8 1.4 %collective-permute-done.16 = bf16[2,64,256]{2,1,0:T(8,128)(2,1)S(1)} collective-permute-done((bf16[2,64,256]{2,1,0:T(8,128)(2,1)S(1)}, bf16[2,64,256]{2,1,0:T(8,128)(2,1)S(1)}, u32[]{:S(2)}, u32[]{:S(2)}) %collective-permute-start.16) | collective-permute-done | bytes 65568 | tf_op jit(solution)/shard_map/ppermute | solution.py:487
  70.3 0.1 collective-permute-start.19
  70.4 0.1 pad_maximum_fusion.1
  70.4 0.3 collective-permute-start.18
  70.7 3.9 %collective-permute-done.19 = bf16[2,64,256]{2,1,0:T(8,128)(2,1)S(1)} collective-permute-done((bf16[2,64,256]{2,1,0:T(8,128)(2,1)S(1)}, bf16[2,64,256]{2,1,0:T(8,128)(2,1)S(1)}, u32[]{:S(2)}, u32[]{:S(2)}) %collective-permute-start.19) | collective-permute-done | bytes 65568 | tf_op jit(solution)/shard_map/ppermute | solution.py:487
  74.6 0.1 collective-permute-start.20
  74.7 5.3 %collective-permute-done.20 = bf16[2,64,256]{2,1,0:T(8,128)(2,1)S(1)} collective-permute-done((bf16[2,64,256]{2,1,0:T(8,128)(2,1)S(1)}, bf16[2,64,256]{2,1,0:T(8,128)(2,1)S(1)}, u32[]{:S(2)}, u32[]{:S(2)}) %collective-permute-start.20) | collective-permute-done | bytes 65568 | tf_op jit(solution)/shard_map/ppermute | solution.py:487
  80.0 0.7 fusion.5
  80.7 0.0 collective-permute-done.17
  80.7 6.8 %collective-permute-done.18 = bf16[2,256,512]{2,1,0:T(8,128)(2,1)S(1)} collective-permute-done((bf16[2,256,512]{2,1,0:T(8,128)(2,1)S(1)}, bf16[2,256,512]{2,1,0:T(8,128)(2,1)S(1)}, u32[]{:S(2)}, u32[]{:S(2)}) %collective-permute-start.18) | collective-permute-done | bytes 524320 | tf_op jit(solution)/shard_map/ppermute | solution.py:484
  87.5 0.1 add_convert_fusion.3
  87.6 1.1 %add_bitcast_fusion = f32[1,2,256,512]{3,2,1,0:T(8,128)} fusion(bf16[2,256,512]{2,1,0:T(8,128)(2,1)S(1)} %collective-permute-done.18, bf16[1,256,512]{2,1,0:T(8,128)(2,1)S(1)} %get-tuple-element.57, bf16[1,256,512]{2,1,0:T(8,128)(2,1)S(1)} %get-tuple-element.56), kind=kLoop, calls=%fused_computation.2 | loop fusion | flops 1048576 | bytes 2097152 | tf_op jit(solution)/shard_map/broadcast_in_dim | solution.py:703
  (13 shorter events, 0.2 us)
Async XLA Ops:
  0.6 8.9 %copy-start = (s32[16,2]{0,1:T(2,128)S(1)}, s32[16,2]{0,1:T(2,128)}, u32[]{:S(2)}) copy-start(s32[16,2]{0,1:T(2,128)} %param.8) | copy-start | bytes 388
  1.9 19.4 %collective-permute-start.3 = (bf16[2,256,512]{2,1,0:T(8,128)(2,1)S(1)}, bf16[2,256,512]{2,1,0:T(8,128)(2,1)S(1)}, u32[]{:S(2)}, u32[]{:S(2)}) collective-permute-start(bf16[2,256,512]{2,1,0:T(8,128)(2,1)S(1)} %convert_bitcast_fusion.refs_0_), channel_id=1, source_target_pairs={{0,16},{8,24},{16,0},{24,8},{1,17},{9,25},{17,1},{25,9},{2,18},{10... | collective-permute-start | bytes 1572872 | tf_op jit(solution)/shard_map/ppermute | solution.py:481
  5.0 22.2 %collective-permute-start.1 = (bf16[2,256,512]{2,1,0:T(8,128)(2,1)S(1)}, bf16[2,256,512]{2,1,0:T(8,128)(2,1)S(1)}, u32[]{:S(2)}, u32[]{:S(2)}) collective-permute-start(bf16[2,256,512]{2,1,0:T(8,128)(2,1)S(1)} %convert_bitcast_fusion.refs_0_), channel_id=1, source_target_pairs={{0,8},{8,0},{16,24},{24,16},{1,9},{9,1},{17,25},{25,17},{2,10},{10... | collective-permute-start | bytes 1572872 | tf_op jit(solution)/shard_map/ppermute | solution.py:481
  5.0 16.4 %collective-permute-start = (bf16[2,256,512]{2,1,0:T(8,128)(2,1)S(1)}, bf16[2,256,512]{2,1,0:T(8,128)(2,1)S(1)}, u32[]{:S(2)}, u32[]{:S(2)}) collective-permute-start(bf16[2,256,512]{2,1,0:T(8,128)(2,1)S(1)} %convert_bitcast_fusion.refs_0_), channel_id=1, source_target_pairs={{0,7},{1,0},{2,1},{3,2},{4,3},{5,4},{6,5},{7,6},{8,15},{9,8},{10,9... | collective-permute-start | bytes 1572872 | tf_op jit(solution)/shard_map/ppermute | solution.py:484
  10.4 16.8 %copy-start.1 = (bf16[512,512]{1,0:T(8,128)(2,1)S(1)}, bf16[512,512]{1,0:T(8,128)(2,1)}, u32[]{:S(2)}) copy-start(bf16[512,512]{1,0:T(8,128)(2,1)} %constant.18.clone.left_ref) | copy-start | bytes 1572868
  10.4 16.8 %copy-start.2 = (bf16[512,512]{1,0:T(8,128)(2,1)S(1)}, bf16[512,512]{1,0:T(8,128)(2,1)}, u32[]{:S(2)}) copy-start(bf16[512,512]{1,0:T(8,128)(2,1)} %constant.17.clone.right_ref) | copy-start | bytes 1572868
  10.4 16.8 %copy-start.3 = (s32[10]{0:T(128)S(1)}, s32[10]{0:T(128)}, u32[]{:S(2)}) copy-start(s32[10]{0:T(128)} %pad_add_fusion.meta_ref) | copy-start | bytes 124
  21.4 5.8 %collective-permute-start.2 = (bf16[2,256,512]{2,1,0:T(8,128)(2,1)S(1)}, bf16[2,256,512]{2,1,0:T(8,128)(2,1)S(1)}, u32[]{:S(2)}, u32[]{:S(2)}) collective-permute-start(bf16[2,256,512]{2,1,0:T(8,128)(2,1)S(1)} %collective-permute-done.refs_1_), channel_id=1, source_target_pairs={{0,8},{8,0},{16,24},{24,16},{1,9},{9,1},{17,25},{25,17},{2,10},{10... | collective-permute-start | bytes 1572872 | tf_op jit(solution)/shard_map/ppermute | solution.py:481
  21.4 11.8 %collective-permute-start.4 = (bf16[256,512]{1,0:T(8,128)(2,1)S(1)}, bf16[256,512]{1,0:T(8,128)(2,1)S(1)}, u32[]{:S(2)}, u32[]{:S(2)}) collective-permute-start(bf16[256,512]{1,0:T(8,128)(2,1)S(1)} %slice_bitcast_fusion.2), channel_id=1, source_target_pairs={{0,16},{8,24},{16,0},{24,8},{1,17},{9,25},{17,1},{25,9},{2,18},{10... | collective-permute-start | bytes 786440 | tf_op jit(solution)/shard_map/ppermute | solution.py:481
  22.0 11.2 %collective-permute-start.5 = (bf16[256,512]{1,0:T(8,128)(2,1)S(1)}, bf16[256,512]{1,0:T(8,128)(2,1)S(1)}, u32[]{:S(2)}, u32[]{:S(2)}) collective-permute-start(bf16[256,512]{1,0:T(8,128)(2,1)S(1)} %slice_bitcast_fusion.1), channel_id=1, source_target_pairs={{0,7},{1,0},{2,1},{3,2},{4,3},{5,4},{6,5},{7,6},{8,15},{9,8},{10,9... | collective-permute-start | bytes 786440 | tf_op jit(solution)/shard_map/ppermute | solution.py:484
  33.2 2.7 %collective-permute-start.6 = (bf16[2,256,512]{2,1,0:T(8,128)(2,1)S(1)}, bf16[2,256,512]{2,1,0:T(8,128)(2,1)S(1)}, u32[]{:S(2)}, u32[]{:S(2)}) collective-permute-start(bf16[2,256,512]{2,1,0:T(8,128)(2,1)S(1)} %collective-permute-done.3.refs_0_), channel_id=1, source_target_pairs={{0,8},{8,0},{16,24},{24,16},{1,9},{9,1},{17,25},{25,17},{2,10},{10... | collective-permute-start | bytes 1572872 | tf_op jit(solution)/shard_map/ppermute | solution.py:481
  33.3 2.3 %collective-permute-start.7 = (bf16[256,512]{1,0:T(8,128)(2,1)S(1)}, bf16[256,512]{1,0:T(8,128)(2,1)S(1)}, u32[]{:S(2)}, u32[]{:S(2)}) collective-permute-start(bf16[256,512]{1,0:T(8,128)(2,1)S(1)} %collective-permute-done.4.refs_1_), channel_id=1, source_target_pairs={{0,8},{8,0},{16,24},{24,16},{1,9},{9,1},{17,25},{25,17},{2,10},{10... | collective-permute-start | bytes 786440 | tf_op jit(solution)/shard_map/ppermute | solution.py:481
  33.7 2.1 %collective-permute-start.8 = (bf16[256,512]{1,0:T(8,128)(2,1)S(1)}, bf16[256,512]{1,0:T(8,128)(2,1)S(1)}, u32[]{:S(2)}, u32[]{:S(2)}) collective-permute-start(bf16[256,512]{1,0:T(8,128)(2,1)S(1)} %collective-permute-done.5.refs_2_), channel_id=1, source_target_pairs={{0,8},{8,0},{16,24},{24,16},{1,9},{9,1},{17,25},{25,17},{2,10},{10... | collective-permute-start | bytes 786440 | tf_op jit(solution)/shard_map/ppermute | solution.py:481
  44.2 8.0 %collective-permute-start.9 = (bf16[2,512,512]{2,1,0:T(8,128)(2,1)S(1)}, bf16[2,512,512]{2,1,0:T(8,128)(2,1)S(1)}, u32[]{:S(2)}, u32[]{:S(2)}) collective-permute-start(bf16[2,512,512]{2,1,0:T(8,128)(2,1)S(1)} %get-tuple-element.36), channel_id=1, source_target_pairs={{0,8},{8,0},{16,24},{24,16},{1,9},{9,1},{17,25},{25,17},{2,10},{10... | collective-permute-start | bytes 3145736 | tf_op jit(solution)/shard_map/ppermute | solution.py:481
  50.0 8.7 %collective-permute-start.14 = (bf16[2,64,256]{2,1,0:T(8,128)(2,1)S(1)}, bf16[2,64,256]{2,1,0:T(8,128)(2,1)S(1)}, u32[]{:S(2)}, u32[]{:S(2)}) collective-permute-start(bf16[2,64,256]{2,1,0:T(8,128)(2,1)S(1)} %get-tuple-element.61), channel_id=1, source_target_pairs={{0,24},{8,16},{16,8},{24,0},{1,25},{9,17},{17,9},{25,1},{2,26},{10... | collective-permute-start | bytes 196616 | tf_op jit(solution)/shard_map/ppermute | solution.py:481
  52.0 6.7 %collective-permute-start.13 = (bf16[2,64,256]{2,1,0:T(8,128)(2,1)S(1)}, bf16[2,64,256]{2,1,0:T(8,128)(2,1)S(1)}, u32[]{:S(2)}, u32[]{:S(2)}) collective-permute-start(bf16[2,64,256]{2,1,0:T(8,128)(2,1)S(1)} %get-tuple-element.62), channel_id=1, source_target_pairs={{0,16},{8,24},{16,0},{24,8},{1,17},{9,25},{17,1},{25,9},{2,18},{10... | collective-permute-start | bytes 196616 | tf_op jit(solution)/shard_map/ppermute | solution.py:481
  52.1 6.6 %collective-permute-start.12 = (bf16[2,64,256]{2,1,0:T(8,128)(2,1)S(1)}, bf16[2,64,256]{2,1,0:T(8,128)(2,1)S(1)}, u32[]{:S(2)}, u32[]{:S(2)}) collective-permute-start(bf16[2,64,256]{2,1,0:T(8,128)(2,1)S(1)} %get-tuple-element.63), channel_id=1, source_target_pairs={{0,8},{8,0},{16,24},{24,16},{1,9},{9,1},{17,25},{25,17},{2,10},{10... | collective-permute-start | bytes 196616 | tf_op jit(solution)/shard_map/ppermute | solution.py:481
  52.6 9.3 %collective-permute-start.11 = (bf16[256,512]{1,0:T(8,128)(2,1)S(1)}, bf16[256,512]{1,0:T(8,128)(2,1)S(1)}, u32[]{:S(2)}, u32[]{:S(2)}) collective-permute-start(bf16[256,512]{1,0:T(8,128)(2,1)S(1)} %get-tuple-element.59), channel_id=1, source_target_pairs={{0,16},{8,24},{16,0},{24,8},{1,17},{9,25},{17,1},{25,9},{2,18},{10... | collective-permute-start | bytes 786440 | tf_op jit(solution)/shard_map/ppermute | solution.py:481
  54.5 11.1 %collective-permute-start.10 = (bf16[256,512]{1,0:T(8,128)(2,1)S(1)}, bf16[256,512]{1,0:T(8,128)(2,1)S(1)}, u32[]{:S(2)}, u32[]{:S(2)}) collective-permute-start(bf16[256,512]{1,0:T(8,128)(2,1)S(1)} %get-tuple-element.60), channel_id=1, source_target_pairs={{0,1},{1,2},{2,3},{3,4},{4,5},{5,6},{6,7},{7,0},{8,9},{9,10},{10,1... | collective-permute-start | bytes 786440 | tf_op jit(solution)/shard_map/ppermute | solution.py:484
  65.7 2.7 %collective-permute-start.15 = (bf16[2,512,512]{2,1,0:T(8,128)(2,1)S(1)}, bf16[2,512,512]{2,1,0:T(8,128)(2,1)S(1)}, u32[]{:S(2)}, u32[]{:S(2)}) collective-permute-start(bf16[2,512,512]{2,1,0:T(8,128)(2,1)S(1)} %get-tuple-element.52), channel_id=1, source_target_pairs={{0,8},{8,0},{16,24},{24,16},{1,9},{9,1},{17,25},{25,17},{2,10},{10... | collective-permute-start | bytes 3145736 | tf_op jit(solution)/shard_map/ppermute | solution.py:481
  65.8 4.5 %collective-permute-start.16 = (bf16[2,64,256]{2,1,0:T(8,128)(2,1)S(1)}, bf16[2,64,256]{2,1,0:T(8,128)(2,1)S(1)}, u32[]{:S(2)}, u32[]{:S(2)}) collective-permute-start(bf16[2,64,256]{2,1,0:T(8,128)(2,1)S(1)} %fusion.4), channel_id=1, source_target_pairs={{0,1},{1,0},{2,3},{3,2},{4,5},{5,4},{6,7},{7,6},{8,9},{9,8},{10,11... | collective-permute-start | bytes 196616 | tf_op jit(solution)/shard_map/ppermute | solution.py:487
  65.9 14.8 %collective-permute-start.17 = (bf16[2,256,512]{2,1,0:T(8,128)(2,1)S(1)}, bf16[2,256,512]{2,1,0:T(8,128)(2,1)S(1)}, u32[]{:S(2)}, u32[]{:S(2)}) collective-permute-start(bf16[2,256,512]{2,1,0:T(8,128)(2,1)S(1)} %pad_maximum_fusion), channel_id=1, source_target_pairs={{0,16},{8,24},{16,0},{24,8},{1,17},{9,25},{17,1},{25,9},{2,18},{10... | collective-permute-start | bytes 1572872 | tf_op jit(solution)/shard_map/ppermute | solution.py:481
  70.3 4.3 %collective-permute-start.19 = (bf16[2,64,256]{2,1,0:T(8,128)(2,1)S(1)}, bf16[2,64,256]{2,1,0:T(8,128)(2,1)S(1)}, u32[]{:S(2)}, u32[]{:S(2)}) collective-permute-start(bf16[2,64,256]{2,1,0:T(8,128)(2,1)S(1)} %add_convert_fusion.7), channel_id=1, source_target_pairs={{0,2},{1,3},{2,0},{3,1},{4,6},{5,7},{6,4},{7,5},{8,10},{9,11},{10,... | collective-permute-start | bytes 196616 | tf_op jit(solution)/shard_map/ppermute | solution.py:487
  70.4 17.0 %collective-permute-start.18 = (bf16[2,256,512]{2,1,0:T(8,128)(2,1)S(1)}, bf16[2,256,512]{2,1,0:T(8,128)(2,1)S(1)}, u32[]{:S(2)}, u32[]{:S(2)}) collective-permute-start(bf16[2,256,512]{2,1,0:T(8,128)(2,1)S(1)} %pad_maximum_fusion.1), channel_id=1, source_target_pairs={{0,1},{1,2},{2,3},{3,4},{4,5},{5,6},{6,7},{7,0},{8,9},{9,10},{10,1... | collective-permute-start | bytes 1572872 | tf_op jit(solution)/shard_map/ppermute | solution.py:484
  74.6 5.4 %collective-permute-start.20 = (bf16[2,64,256]{2,1,0:T(8,128)(2,1)S(1)}, bf16[2,64,256]{2,1,0:T(8,128)(2,1)S(1)}, u32[]{:S(2)}, u32[]{:S(2)}) collective-permute-start(bf16[2,64,256]{2,1,0:T(8,128)(2,1)S(1)} %add_convert_fusion.6), channel_id=1, source_target_pairs={{0,4},{1,5},{2,6},{3,7},{4,0},{5,1},{6,2},{7,3},{8,12},{9,13},{10,... | collective-permute-start | bytes 196616 | tf_op jit(solution)/shard_map/ppermute | solution.py:487

commit v5 on v4

--- a/solution.py
+++ b/solution.py
@@ -675,11 +675,14 @@
         owns[slot] = (real, total(imag, shifted[slot]))
     near_grads = after(near_grads, owns, crossed, part)
     near_sums = core_sums(dict(enumerate(near_grads)))
-    lat_bits = [1 << i for i in range(lat.bit_length() - 1)]
-    butterfly = not lat & (lat - 1)
-    if butterfly:
-        moved = along_xor(part, lat_bits[0])
-        part = total(part, after(moved, near_sums))
+    power_of_two = not lat & (lat - 1)
+    if power_of_two:
+        part_sum = part.astype(f32)
+        arriving = {other: along_xor(part, other) for other in range(1, lat // 2)}
+        near_sums, arriving = after((near_sums, arriving))
+        for moved in arriving.values():
+            part_sum = part_sum + moved.astype(f32)
+        part = part_sum.astype(bf16)
     for slot, both in near_sums.items():
         halo_grads[slot] = (both[0, w:], both[1, w:])
         both = after(both, halo_grads[slot], part)
@@ -702,9 +705,8 @@
             owns[slot ^ bit] = (total(kept[0], sent[0]), total(kept[1], sent[1]))
     object_grad = (jnp.stack(owns[0]).astype(f32) + from_below.astype(f32))[None]
 
-    if butterfly:
-        for bit in lat_bits[1:]:
-            part = total(part, along_xor(part, bit))
+    if power_of_two:
+        part = total(part, along_xor(part, lat // 2))
     else:
         part = lax.psum(part.astype(f32), "lat")
     return (object_grad, part.astype(f32))

time: 89.5 us -> 91.6 us (1.023)
  starting transfers between devices: 19.3 us -> 23.4 us
  waiting for transfers between devices: 33 us -> 31.5 us
    ppermute x3 -> x4, starting transfers between devices: 0.21 us -> 3.61 us  [along_xor(): return lax.ppermute(value, 'lat', [(i, i ^ bit) for i in range(lat)])]
    ppermute x3 -> x4, waiting for transfers between devices: 10.6 us -> 7.76 us  [along_xor(): return lax.ppermute(value, 'lat', [(i, i ^ bit) for i in range(lat)])]
  transfers between devices with their start and end apart: 21 -> 22, of which waited for: 10 -> 10; matrix products, arithmetic and copies ran while one was open for 3% -> 3% of each run, Pallas kernels for 25% -> 24%
where the time goes in v5:
time: 91.6 us; the launch traced here: 91.4 us
  waiting for transfers between devices  31.5 us (34%)
  Pallas kernels  30.4 us (33%)
  starting transfers between devices  23.4 us (26%)
  other arithmetic  4.85 us (5%)
    pallas_call x5, Pallas kernels, call(): pl.pallas_call(kernel, out_shape=flat, in_specs=[spec for spec, _ in ins]...  30.4 us
    ppermute x4, waiting for transfers between devices, along(): lax.ppermute(value, 'lat', [(i, (i + steps) % lat) for i in range(lat)])  15.5 us
    ppermute x4, starting transfers between devices, along(): lax.ppermute(value, 'lat', [(i, (i + steps) % lat) for i in range(lat)])  10.8 us
    ppermute x14, starting transfers between devices, across(): return lax.ppermute(value, 'depth', [(i, i ^ bit) for i in range(depth)])  9.03 us
    ppermute x14, waiting for transfers between devices, across(): return lax.ppermute(value, 'depth', [(i, i ^ bit) for i in range(depth)])  8.22 us
    ppermute x4, waiting for transfers between devices, along_xor(): return lax.ppermute(value, 'lat', [(i, i ^ bit) for i in range(lat)])  7.76 us
    ppermute x4, starting transfers between devices, along_xor(): return lax.ppermute(value, 'lat', [(i, i ^ bit) for i in range(lat)])  3.61 us
  transfers between devices with their start and end apart: 22, of which 10 were waited for; matrix products, arithmetic and copies ran while one was open for 3% of the time, Pallas kernels for 24%

profile of v5, /device:TPU:0, one launch (start us, length us, event | category | flops | bytes accessed | tf_op | source)
XLA Modules:
  0.0 91.4 jit_solution(12757511208222060566)
XLA Ops:
  0.6 0.0 copy-start
  0.6 1.3 %convert_bitcast_fusion.refs_0_ = bf16[2,256,512]{2,1,0:T(8,128)(2,1)S(1)} fusion(f32[1,2,256,512]{3,2,1,0:T(8,128)} %param.6), kind=kLoop, calls=%fused_computation.10 | loop fusion | flops 262144 | bytes 1572864 | tf_op jit(solution)/shard_map/convert_element_type | solution.py:492
  1.9 3.0 %collective-permute-start.3 = (bf16[2,256,512]{2,1,0:T(8,128)(2,1)S(1)}, bf16[2,256,512]{2,1,0:T(8,128)(2,1)S(1)}, u32[]{:S(2)}, u32[]{:S(2)}) collective-permute-start(bf16[2,256,512]{2,1,0:T(8,128)(2,1)S(1)} %convert_bitcast_fusion.refs_0_), channel_id=1, source_target_pairs={{0,16},{8,24},{16,0},{24,8},{1,17},{9,25},{17,1},{25,9},{2,18},{10... | collective-permute-start | bytes 1572872 | tf_op jit(solution)/shard_map/ppermute | solution.py:481
  5.0 0.0 collective-permute-start.1
  5.0 4.5 %collective-permute-start = (bf16[2,256,512]{2,1,0:T(8,128)(2,1)S(1)}, bf16[2,256,512]{2,1,0:T(8,128)(2,1)S(1)}, u32[]{:S(2)}, u32[]{:S(2)}) collective-permute-start(bf16[2,256,512]{2,1,0:T(8,128)(2,1)S(1)} %convert_bitcast_fusion.refs_0_), channel_id=1, source_target_pairs={{0,7},{1,0},{2,1},{3,2},{4,3},{5,4},{6,5},{7,6},{8,15},{9,8},{10,9... | collective-permute-start | bytes 1572872 | tf_op jit(solution)/shard_map/ppermute | solution.py:484
  9.5 0.1 constant_dynamic-slice_fusion
  9.6 0.1 copy.13
  9.7 0.1 reshape.12
  9.8 0.7 pad_add_fusion.meta_ref
  10.4 6.4 %first_waves.1._ = bf16[32,4,2,256,256]{4,3,2,1,0:T(8,128)(2,1)} custom-call(s32[10]{0:T(128)} %pad_add_fusion.meta_ref, f32[2,256,256]{2,1,0:T(8,128)} %probe_ref.1, f32[16,2,256,256]{3,2,1,0:T(8,128)} %cot_hbm.1, bf16[512,512]{1,0:T(8,128)(2,1)} %constant.17.clone.right_ref, bf16[512,512]{1,0:T(8,128)(2,1)} %constant.18.clone.left_ref), custom_call_target="tpu_custom_call" | custom-call | flops 6442450944 | bytes 8388608 | tf_op jit(solution)/shard_map/first_waves/pallas_call | solution.py:511
  16.9 4.5 %collective-permute-done.refs_1_ = bf16[2,256,512]{2,1,0:T(8,128)(2,1)S(1)} collective-permute-done((bf16[2,256,512]{2,1,0:T(8,128)(2,1)S(1)}, bf16[2,256,512]{2,1,0:T(8,128)(2,1)S(1)}, u32[]{:S(2)}, u32[]{:S(2)}) %collective-permute-start) | collective-permute-done | bytes 524320 | tf_op jit(solution)/shard_map/ppermute | solution.py:484
  21.4 0.0 collective-permute-start.2
  21.4 0.0 collective-permute-done.3.refs_0_
  21.4 0.6 collective-permute-start.4
  22.0 5.2 %collective-permute-start.5 = (bf16[256,512]{1,0:T(8,128)(2,1)S(1)}, bf16[256,512]{1,0:T(8,128)(2,1)S(1)}, u32[]{:S(2)}, u32[]{:S(2)}) collective-permute-start(bf16[256,512]{1,0:T(8,128)(2,1)S(1)} %slice_bitcast_fusion), channel_id=1, source_target_pairs={{0,7},{1,0},{2,1},{3,2},{4,3},{5,4},{6,5},{7,6},{8,15},{9,8},{10,9... | collective-permute-start | bytes 786440 | tf_op jit(solution)/shard_map/ppermute | solution.py:484
  27.2 0.0 collective-permute-done.1.refs_2_
  27.2 0.0 collective-permute-done.2.refs_3_
  27.2 5.9 %near_slices.1._ = bf16[32,4,2,256,256]{4,3,2,1,0:T(8,128)(2,1)} custom-call(s32[10]{0:T(128)S(1)} %copy-done.3, bf16[32,4,2,256,256]{4,3,2,1,0:T(8,128)(2,1)} %first_waves.1._, bf16[512,512]{1,0:T(8,128)(2,1)S(1)} %copy-done.2, bf16[512,512]{1,0:T(8,128)(2,1)S(1)} %copy-done.1, ...), custom_call_target="tpu_custom_call", output_to_operand_aliasing={{}: (1, {})} | custom-call | flops 12884901888 | bytes 8388608 | tf_op jit(solution)/shard_map/near_slices/pallas_call | solution.py:511
  33.1 0.1 collective-permute-start.6
  33.2 0.0 collective-permute-done.5.refs_2_
  33.2 0.0 collective-permute-done.4.refs_1_
  33.2 0.5 collective-permute-start.7
  33.7 0.1 collective-permute-start.8
  33.8 1.7 %collective-permute-done.7.refs_4_ = bf16[256,512]{1,0:T(8,128)(2,1)S(1)} collective-permute-done((bf16[256,512]{1,0:T(8,128)(2,1)S(1)}, bf16[256,512]{1,0:T(8,128)(2,1)S(1)}, u32[]{:S(2)}, u32[]{:S(2)}) %collective-permute-start.7) | collective-permute-done | bytes 262176 | tf_op jit(solution)/shard_map/ppermute | solution.py:481
  35.5 0.4 collective-permute-done.8.refs_5_
  35.9 0.0 collective-permute-done.6.refs_3_
  35.9 8.3 %far_slices.1 = (bf16[2,512,512]{2,1,0:T(8,128)(2,1)S(1)}, bf16[2,512,512]{2,1,0:T(8,128)(2,1)S(1)}, bf16[32,4,2,256,256]{4,3,2,1,0:T(8,128)(2,1)}, bf16[4,256,5...) custom-call(s32[10]{0:T(128)S(1)} %copy-done.3, ...), custom_call_target="tpu_custom_call", output_to_operand_aliasing={{2}: (1, {})} | custom-call | flops 12884901888 | bytes 8388608 | tf_op jit(solution)/shard_map/far_slices/pallas_call | solution.py:511
  44.2 0.2 collective-permute-start.9
  44.4 5.5 %return_waves.1 = (bf16[32,4,2,256,256]{4,3,2,1,0:T(8,128)(2,1)}, bf16[4,2,64,256]{3,2,1,0:T(8,128)(2,1)S(1)}) custom-call(s32[10]{0:T(128)S(1)} %copy-done.3, bf16[32,4,2,256,256]{4,3,2,1,0:T(8,128)(2,1)} %get-tuple-element.41._, bf16[4,256,512]{2,1,0:T(8,128)(2,1)S(1)} %get-tuple-element.42.x_hbm, ...), custom_call_target="tpu_custom_call", output_to_operand_aliasing={{0}: (1, {})} | custom-call | flops 12884901888 | bytes 8388608 | tf_op jit(solution)/shard_map/return_waves/pallas_call | solution.py:511
  50.0 2.0 %collective-permute-start.14 = (bf16[2,64,256]{2,1,0:T(8,128)(2,1)S(1)}, bf16[2,64,256]{2,1,0:T(8,128)(2,1)S(1)}, u32[]{:S(2)}, u32[]{:S(2)}) collective-permute-start(bf16[2,64,256]{2,1,0:T(8,128)(2,1)S(1)} %get-tuple-element.67), channel_id=1, source_target_pairs={{0,24},{8,16},{16,8},{24,0},{1,25},{9,17},{17,9},{25,1},{2,26},{10... | collective-permute-start | bytes 196616 | tf_op jit(solution)/shard_map/ppermute | solution.py:481
  52.0 0.1 collective-permute-start.13
  52.1 0.1 collective-permute-start.12
  52.2 0.0 collective-permute-done.9
  52.2 0.3 add_convert_fusion.1
  52.5 0.1 fusion.6
  52.6 1.9 %collective-permute-start.11 = (bf16[256,512]{1,0:T(8,128)(2,1)S(1)}, bf16[256,512]{1,0:T(8,128)(2,1)S(1)}, u32[]{:S(2)}, u32[]{:S(2)}) collective-permute-start(bf16[256,512]{1,0:T(8,128)(2,1)S(1)} %get-tuple-element.65), channel_id=1, source_target_pairs={{0,16},{8,24},{16,0},{24,8},{1,17},{9,25},{17,1},{25,9},{2,18},{10... | collective-permute-start | bytes 786440 | tf_op jit(solution)/shard_map/ppermute | solution.py:481
  54.4 0.0 collective-permute-start.10
  54.5 4.2 %near_gradients.1 = (bf16[2,512,512]{2,1,0:T(8,128)(2,1)S(1)}, bf16[2,512,512]{2,1,0:T(8,128)(2,1)S(1)}, bf16[32,4,2,256,256]{4,3,2,1,0:T(8,128)(2,1)}) custom-call(s32[10]{0:T(128)S(1)} %copy-done.3, bf16[32,4,2,256,256]{4,3,2,1,0:T(8,128)(2,1)} %get-tuple-element.44._), custom_call_target="tpu_custom_call", output_to_operand_aliasing={{2}: (1, {})} | custom-call | flops 12884901888 | bytes 8388608 | tf_op jit(solution)/shard_map/near_gradients/pallas_call | solution.py:511
  58.6 0.0 collective-permute-done.14
  58.6 0.0 collective-permute-done.13
  58.7 0.0 collective-permute-done.12
  58.7 3.1 %collective-permute-done.11 = bf16[256,512]{1,0:T(8,128)(2,1)S(1)} collective-permute-done((bf16[256,512]{1,0:T(8,128)(2,1)S(1)}, bf16[256,512]{1,0:T(8,128)(2,1)S(1)}, u32[]{:S(2)}, u32[]{:S(2)}) %collective-permute-start.11) | collective-permute-done | bytes 262176 | tf_op jit(solution)/shard_map/ppermute | solution.py:481
  61.9 3.7 %collective-permute-done.10 = bf16[256,512]{1,0:T(8,128)(2,1)S(1)} collective-permute-done((bf16[256,512]{1,0:T(8,128)(2,1)S(1)}, bf16[256,512]{1,0:T(8,128)(2,1)S(1)}, u32[]{:S(2)}, u32[]{:S(2)}) %collective-permute-start.10) | collective-permute-done | bytes 262176 | tf_op jit(solution)/shard_map/ppermute | solution.py:484
  65.6 0.1 fusion
  65.7 0.1 collective-permute-start.15
  65.7 0.1 collective-permute-start.18
  65.8 0.1 collective-permute-start.17
  65.9 3.4 %collective-permute-start.16 = (bf16[2,64,256]{2,1,0:T(8,128)(2,1)S(1)}, bf16[2,64,256]{2,1,0:T(8,128)(2,1)S(1)}, u32[]{:S(2)}, u32[]{:S(2)}) collective-permute-start(bf16[2,64,256]{2,1,0:T(8,128)(2,1)S(1)} %fusion.4), channel_id=1, source_target_pairs={{0,1},{1,0},{2,3},{3,2},{4,5},{5,4},{6,7},{7,6},{8,9},{9,8},{10,11... | collective-permute-start | bytes 196616 | tf_op jit(solution)/shard_map/ppermute | solution.py:487
  69.3 0.1 pad_maximum_fusion
  69.3 0.4 collective-permute-start.19
  69.8 0.0 collective-permute-done.15
  69.8 0.3 add_convert_fusion
  70.1 1.5 %collective-permute-done.18 = bf16[2,64,256]{2,1,0:T(8,128)(2,1)S(1)} collective-permute-done((bf16[2,64,256]{2,1,0:T(8,128)(2,1)S(1)}, bf16[2,64,256]{2,1,0:T(8,128)(2,1)S(1)}, u32[]{:S(2)}, u32[]{:S(2)}) %collective-permute-start.18) | collective-permute-done | bytes 65568 | tf_op jit(solution)/shard_map/ppermute | solution.py:487
  71.6 1.0 %collective-permute-done.16 = bf16[2,64,256]{2,1,0:T(8,128)(2,1)S(1)} collective-permute-done((bf16[2,64,256]{2,1,0:T(8,128)(2,1)S(1)}, bf16[2,64,256]{2,1,0:T(8,128)(2,1)S(1)}, u32[]{:S(2)}, u32[]{:S(2)}) %collective-permute-start.16) | collective-permute-done | bytes 65568 | tf_op jit(solution)/shard_map/ppermute | solution.py:487
  72.6 0.1 fusion.1
  72.7 0.1 pad_maximum_fusion.1
  72.7 1.1 %collective-permute-start.20 = (bf16[2,256,512]{2,1,0:T(8,128)(2,1)S(1)}, bf16[2,256,512]{2,1,0:T(8,128)(2,1)S(1)}, u32[]{:S(2)}, u32[]{:S(2)}) collective-permute-start(bf16[2,256,512]{2,1,0:T(8,128)(2,1)S(1)} %pad_maximum_fusion.1), channel_id=1, source_target_pairs={{0,1},{1,2},{2,3},{3,4},{4,5},{5,6},{6,7},{7,0},{8,9},{9,10},{10,1... | collective-permute-start | bytes 1572872 | tf_op jit(solution)/shard_map/ppermute | solution.py:484
  73.8 0.1 collective-permute-start.21
  73.9 5.3 %collective-permute-done.21 = bf16[2,64,256]{2,1,0:T(8,128)(2,1)S(1)} collective-permute-done((bf16[2,64,256]{2,1,0:T(8,128)(2,1)S(1)}, bf16[2,64,256]{2,1,0:T(8,128)(2,1)S(1)}, u32[]{:S(2)}, u32[]{:S(2)}) %collective-permute-start.21) | collective-permute-done | bytes 65568 | tf_op jit(solution)/shard_map/ppermute | solution.py:487
  79.2 0.7 fusion.5
  79.9 3.0 %collective-permute-done.19 = bf16[2,256,512]{2,1,0:T(8,128)(2,1)S(1)} collective-permute-done((bf16[2,256,512]{2,1,0:T(8,128)(2,1)S(1)}, bf16[2,256,512]{2,1,0:T(8,128)(2,1)S(1)}, u32[]{:S(2)}, u32[]{:S(2)}) %collective-permute-start.19) | collective-permute-done | bytes 524320 | tf_op jit(solution)/shard_map/ppermute | solution.py:481
  82.9 7.3 %collective-permute-done.20 = bf16[2,256,512]{2,1,0:T(8,128)(2,1)S(1)} collective-permute-done((bf16[2,256,512]{2,1,0:T(8,128)(2,1)S(1)}, bf16[2,256,512]{2,1,0:T(8,128)(2,1)S(1)}, u32[]{:S(2)}, u32[]{:S(2)}) %collective-permute-start.20) | collective-permute-done | bytes 524320 | tf_op jit(solution)/shard_map/ppermute | solution.py:484
  90.1 0.1 add_convert_fusion.3
  90.3 1.1 %add_bitcast_fusion = f32[1,2,256,512]{3,2,1,0:T(8,128)} fusion(bf16[2,256,512]{2,1,0:T(8,128)(2,1)S(1)} %collective-permute-done.20, bf16[1,256,512]{2,1,0:T(8,128)(2,1)S(1)} %get-tuple-element.63, bf16[1,256,512]{2,1,0:T(8,128)(2,1)S(1)} %get-tuple-element.62), kind=kLoop, calls=%fused_computation.2 | loop fusion | flops 1048576 | bytes 2097152 | tf_op jit(solution)/shard_map/broadcast_in_dim | solution.py:706
  (14 shorter events, 0.2 us)
Async XLA Ops:
  0.6 8.9 %copy-start = (s32[16,2]{0,1:T(2,128)S(1)}, s32[16,2]{0,1:T(2,128)}, u32[]{:S(2)}) copy-start(s32[16,2]{0,1:T(2,128)} %param.8) | copy-start | bytes 388
  1.9 19.4 %collective-permute-start.3 = (bf16[2,256,512]{2,1,0:T(8,128)(2,1)S(1)}, bf16[2,256,512]{2,1,0:T(8,128)(2,1)S(1)}, u32[]{:S(2)}, u32[]{:S(2)}) collective-permute-start(bf16[2,256,512]{2,1,0:T(8,128)(2,1)S(1)} %convert_bitcast_fusion.refs_0_), channel_id=1, source_target_pairs={{0,16},{8,24},{16,0},{24,8},{1,17},{9,25},{17,1},{25,9},{2,18},{10... | collective-permute-start | bytes 1572872 | tf_op jit(solution)/shard_map/ppermute | solution.py:481
  5.0 22.2 %collective-permute-start.1 = (bf16[2,256,512]{2,1,0:T(8,128)(2,1)S(1)}, bf16[2,256,512]{2,1,0:T(8,128)(2,1)S(1)}, u32[]{:S(2)}, u32[]{:S(2)}) collective-permute-start(bf16[2,256,512]{2,1,0:T(8,128)(2,1)S(1)} %convert_bitcast_fusion.refs_0_), channel_id=1, source_target_pairs={{0,8},{8,0},{16,24},{24,16},{1,9},{9,1},{17,25},{25,17},{2,10},{10... | collective-permute-start | bytes 1572872 | tf_op jit(solution)/shard_map/ppermute | solution.py:481
  5.0 16.4 %collective-permute-start = (bf16[2,256,512]{2,1,0:T(8,128)(2,1)S(1)}, bf16[2,256,512]{2,1,0:T(8,128)(2,1)S(1)}, u32[]{:S(2)}, u32[]{:S(2)}) collective-permute-start(bf16[2,256,512]{2,1,0:T(8,128)(2,1)S(1)} %convert_bitcast_fusion.refs_0_), channel_id=1, source_target_pairs={{0,7},{1,0},{2,1},{3,2},{4,3},{5,4},{6,5},{7,6},{8,15},{9,8},{10,9... | collective-permute-start | bytes 1572872 | tf_op jit(solution)/shard_map/ppermute | solution.py:484
  10.4 16.7 %copy-start.1 = (bf16[512,512]{1,0:T(8,128)(2,1)S(1)}, bf16[512,512]{1,0:T(8,128)(2,1)}, u32[]{:S(2)}) copy-start(bf16[512,512]{1,0:T(8,128)(2,1)} %constant.18.clone.left_ref) | copy-start | bytes 1572868
  10.4 16.7 %copy-start.2 = (bf16[512,512]{1,0:T(8,128)(2,1)S(1)}, bf16[512,512]{1,0:T(8,128)(2,1)}, u32[]{:S(2)}) copy-start(bf16[512,512]{1,0:T(8,128)(2,1)} %constant.17.clone.right_ref) | copy-start | bytes 1572868
  10.4 16.8 %copy-start.3 = (s32[10]{0:T(128)S(1)}, s32[10]{0:T(128)}, u32[]{:S(2)}) copy-start(s32[10]{0:T(128)} %pad_add_fusion.meta_ref) | copy-start | bytes 124
  21.4 5.8 %collective-permute-start.2 = (bf16[2,256,512]{2,1,0:T(8,128)(2,1)S(1)}, bf16[2,256,512]{2,1,0:T(8,128)(2,1)S(1)}, u32[]{:S(2)}, u32[]{:S(2)}) collective-permute-start(bf16[2,256,512]{2,1,0:T(8,128)(2,1)S(1)} %collective-permute-done.refs_1_), channel_id=1, source_target_pairs={{0,8},{8,0},{16,24},{24,16},{1,9},{9,1},{17,25},{25,17},{2,10},{10... | collective-permute-start | bytes 1572872 | tf_op jit(solution)/shard_map/ppermute | solution.py:481
  21.4 11.8 %collective-permute-start.4 = (bf16[256,512]{1,0:T(8,128)(2,1)S(1)}, bf16[256,512]{1,0:T(8,128)(2,1)S(1)}, u32[]{:S(2)}, u32[]{:S(2)}) collective-permute-start(bf16[256,512]{1,0:T(8,128)(2,1)S(1)} %slice_bitcast_fusion.1), channel_id=1, source_target_pairs={{0,16},{8,24},{16,0},{24,8},{1,17},{9,25},{17,1},{25,9},{2,18},{10... | collective-permute-start | bytes 786440 | tf_op jit(solution)/shard_map/ppermute | solution.py:481
  22.0 11.2 %collective-permute-start.5 = (bf16[256,512]{1,0:T(8,128)(2,1)S(1)}, bf16[256,512]{1,0:T(8,128)(2,1)S(1)}, u32[]{:S(2)}, u32[]{:S(2)}) collective-permute-start(bf16[256,512]{1,0:T(8,128)(2,1)S(1)} %slice_bitcast_fusion), channel_id=1, source_target_pairs={{0,7},{1,0},{2,1},{3,2},{4,3},{5,4},{6,5},{7,6},{8,15},{9,8},{10,9... | collective-permute-start | bytes 786440 | tf_op jit(solution)/shard_map/ppermute | solution.py:484
  33.1 2.7 %collective-permute-start.6 = (bf16[2,256,512]{2,1,0:T(8,128)(2,1)S(1)}, bf16[2,256,512]{2,1,0:T(8,128)(2,1)S(1)}, u32[]{:S(2)}, u32[]{:S(2)}) collective-permute-start(bf16[2,256,512]{2,1,0:T(8,128)(2,1)S(1)} %collective-permute-done.3.refs_0_), channel_id=1, source_target_pairs={{0,8},{8,0},{16,24},{24,16},{1,9},{9,1},{17,25},{25,17},{2,10},{10... | collective-permute-start | bytes 1572872 | tf_op jit(solution)/shard_map/ppermute | solution.py:481
  33.2 2.3 %collective-permute-start.7 = (bf16[256,512]{1,0:T(8,128)(2,1)S(1)}, bf16[256,512]{1,0:T(8,128)(2,1)S(1)}, u32[]{:S(2)}, u32[]{:S(2)}) collective-permute-start(bf16[256,512]{1,0:T(8,128)(2,1)S(1)} %collective-permute-done.4.refs_1_), channel_id=1, source_target_pairs={{0,8},{8,0},{16,24},{24,16},{1,9},{9,1},{17,25},{25,17},{2,10},{10... | collective-permute-start | bytes 786440 | tf_op jit(solution)/shard_map/ppermute | solution.py:481
  33.7 2.1 %collective-permute-start.8 = (bf16[256,512]{1,0:T(8,128)(2,1)S(1)}, bf16[256,512]{1,0:T(8,128)(2,1)S(1)}, u32[]{:S(2)}, u32[]{:S(2)}) collective-permute-start(bf16[256,512]{1,0:T(8,128)(2,1)S(1)} %collective-permute-done.5.refs_2_), channel_id=1, source_target_pairs={{0,8},{8,0},{16,24},{24,16},{1,9},{9,1},{17,25},{25,17},{2,10},{10... | collective-permute-start | bytes 786440 | tf_op jit(solution)/shard_map/ppermute | solution.py:481
  44.2 8.0 %collective-permute-start.9 = (bf16[2,512,512]{2,1,0:T(8,128)(2,1)S(1)}, bf16[2,512,512]{2,1,0:T(8,128)(2,1)S(1)}, u32[]{:S(2)}, u32[]{:S(2)}) collective-permute-start(bf16[2,512,512]{2,1,0:T(8,128)(2,1)S(1)} %get-tuple-element.39), channel_id=1, source_target_pairs={{0,8},{8,0},{16,24},{24,16},{1,9},{9,1},{17,25},{25,17},{2,10},{10... | collective-permute-start | bytes 3145736 | tf_op jit(solution)/shard_map/ppermute | solution.py:481
  50.0 8.7 %collective-permute-start.14 = (bf16[2,64,256]{2,1,0:T(8,128)(2,1)S(1)}, bf16[2,64,256]{2,1,0:T(8,128)(2,1)S(1)}, u32[]{:S(2)}, u32[]{:S(2)}) collective-permute-start(bf16[2,64,256]{2,1,0:T(8,128)(2,1)S(1)} %get-tuple-element.67), channel_id=1, source_target_pairs={{0,24},{8,16},{16,8},{24,0},{1,25},{9,17},{17,9},{25,1},{2,26},{10... | collective-permute-start | bytes 196616 | tf_op jit(solution)/shard_map/ppermute | solution.py:481
  52.0 6.7 %collective-permute-start.13 = (bf16[2,64,256]{2,1,0:T(8,128)(2,1)S(1)}, bf16[2,64,256]{2,1,0:T(8,128)(2,1)S(1)}, u32[]{:S(2)}, u32[]{:S(2)}) collective-permute-start(bf16[2,64,256]{2,1,0:T(8,128)(2,1)S(1)} %get-tuple-element.68), channel_id=1, source_target_pairs={{0,16},{8,24},{16,0},{24,8},{1,17},{9,25},{17,1},{25,9},{2,18},{10... | collective-permute-start | bytes 196616 | tf_op jit(solution)/shard_map/ppermute | solution.py:481
  52.1 6.6 %collective-permute-start.12 = (bf16[2,64,256]{2,1,0:T(8,128)(2,1)S(1)}, bf16[2,64,256]{2,1,0:T(8,128)(2,1)S(1)}, u32[]{:S(2)}, u32[]{:S(2)}) collective-permute-start(bf16[2,64,256]{2,1,0:T(8,128)(2,1)S(1)} %get-tuple-element.69), channel_id=1, source_target_pairs={{0,8},{8,0},{16,24},{24,16},{1,9},{9,1},{17,25},{25,17},{2,10},{10... | collective-permute-start | bytes 196616 | tf_op jit(solution)/shard_map/ppermute | solution.py:481
  52.6 9.3 %collective-permute-start.11 = (bf16[256,512]{1,0:T(8,128)(2,1)S(1)}, bf16[256,512]{1,0:T(8,128)(2,1)S(1)}, u32[]{:S(2)}, u32[]{:S(2)}) collective-permute-start(bf16[256,512]{1,0:T(8,128)(2,1)S(1)} %get-tuple-element.65), channel_id=1, source_target_pairs={{0,16},{8,24},{16,0},{24,8},{1,17},{9,25},{17,1},{25,9},{2,18},{10... | collective-permute-start | bytes 786440 | tf_op jit(solution)/shard_map/ppermute | solution.py:481
  54.4 11.1 %collective-permute-start.10 = (bf16[256,512]{1,0:T(8,128)(2,1)S(1)}, bf16[256,512]{1,0:T(8,128)(2,1)S(1)}, u32[]{:S(2)}, u32[]{:S(2)}) collective-permute-start(bf16[256,512]{1,0:T(8,128)(2,1)S(1)} %get-tuple-element.66), channel_id=1, source_target_pairs={{0,1},{1,2},{2,3},{3,4},{4,5},{5,6},{6,7},{7,0},{8,9},{9,10},{10,1... | collective-permute-start | bytes 786440 | tf_op jit(solution)/shard_map/ppermute | solution.py:484
  65.7 4.1 %collective-permute-start.15 = (bf16[2,512,512]{2,1,0:T(8,128)(2,1)S(1)}, bf16[2,512,512]{2,1,0:T(8,128)(2,1)S(1)}, u32[]{:S(2)}, u32[]{:S(2)}) collective-permute-start(bf16[2,512,512]{2,1,0:T(8,128)(2,1)S(1)} %get-tuple-element.55), channel_id=1, source_target_pairs={{0,8},{8,0},{16,24},{24,16},{1,9},{9,1},{17,25},{25,17},{2,10},{10... | collective-permute-start | bytes 3145736 | tf_op jit(solution)/shard_map/ppermute | solution.py:481
  65.7 5.9 %collective-permute-start.18 = (bf16[2,64,256]{2,1,0:T(8,128)(2,1)S(1)}, bf16[2,64,256]{2,1,0:T(8,128)(2,1)S(1)}, u32[]{:S(2)}, u32[]{:S(2)}) collective-permute-start(bf16[2,64,256]{2,1,0:T(8,128)(2,1)S(1)} %fusion.4), channel_id=1, source_target_pairs={{0,3},{1,2},{2,1},{3,0},{4,7},{5,6},{6,5},{7,4},{8,11},{9,10},{10,... | collective-permute-start | bytes 196616 | tf_op jit(solution)/shard_map/ppermute | solution.py:487
  65.8 5.8 %collective-permute-start.17 = (bf16[2,64,256]{2,1,0:T(8,128)(2,1)S(1)}, bf16[2,64,256]{2,1,0:T(8,128)(2,1)S(1)}, u32[]{:S(2)}, u32[]{:S(2)}) collective-permute-start(bf16[2,64,256]{2,1,0:T(8,128)(2,1)S(1)} %fusion.4), channel_id=1, source_target_pairs={{0,2},{1,3},{2,0},{3,1},{4,6},{5,7},{6,4},{7,5},{8,10},{9,11},{10,... | collective-permute-start | bytes 196616 | tf_op jit(solution)/shard_map/ppermute | solution.py:487
  65.9 6.7 %collective-permute-start.16 = (bf16[2,64,256]{2,1,0:T(8,128)(2,1)S(1)}, bf16[2,64,256]{2,1,0:T(8,128)(2,1)S(1)}, u32[]{:S(2)}, u32[]{:S(2)}) collective-permute-start(bf16[2,64,256]{2,1,0:T(8,128)(2,1)S(1)} %fusion.4), channel_id=1, source_target_pairs={{0,1},{1,0},{2,3},{3,2},{4,5},{5,4},{6,7},{7,6},{8,9},{9,8},{10,11... | collective-permute-start | bytes 196616 | tf_op jit(solution)/shard_map/ppermute | solution.py:487
  69.3 13.5 %collective-permute-start.19 = (bf16[2,256,512]{2,1,0:T(8,128)(2,1)S(1)}, bf16[2,256,512]{2,1,0:T(8,128)(2,1)S(1)}, u32[]{:S(2)}, u32[]{:S(2)}) collective-permute-start(bf16[2,256,512]{2,1,0:T(8,128)(2,1)S(1)} %pad_maximum_fusion), channel_id=1, source_target_pairs={{0,16},{8,24},{16,0},{24,8},{1,17},{9,25},{17,1},{25,9},{2,18},{10... | collective-permute-start | bytes 1572872 | tf_op jit(solution)/shard_map/ppermute | solution.py:481
  72.7 17.4 %collective-permute-start.20 = (bf16[2,256,512]{2,1,0:T(8,128)(2,1)S(1)}, bf16[2,256,512]{2,1,0:T(8,128)(2,1)S(1)}, u32[]{:S(2)}, u32[]{:S(2)}) collective-permute-start(bf16[2,256,512]{2,1,0:T(8,128)(2,1)S(1)} %pad_maximum_fusion.1), channel_id=1, source_target_pairs={{0,1},{1,2},{2,3},{3,4},{4,5},{5,6},{6,7},{7,0},{8,9},{9,10},{10,1... | collective-permute-start | bytes 1572872 | tf_op jit(solution)/shard_map/ppermute | solution.py:484
  73.8 5.4 %collective-permute-start.21 = (bf16[2,64,256]{2,1,0:T(8,128)(2,1)S(1)}, bf16[2,64,256]{2,1,0:T(8,128)(2,1)S(1)}, u32[]{:S(2)}, u32[]{:S(2)}) collective-permute-start(bf16[2,64,256]{2,1,0:T(8,128)(2,1)S(1)} %add_convert_fusion.6), channel_id=1, source_target_pairs={{0,4},{1,5},{2,6},{3,7},{4,0},{5,1},{6,2},{7,3},{8,12},{9,13},{10,... | collective-permute-start | bytes 196616 | tf_op jit(solution)/shard_map/ppermute | solution.py:487

commit v6 on v4

--- a/solution.py
+++ b/solution.py
@@ -649,7 +649,7 @@
         owns[slot] = (both[0, :w], both[1, :w])
         halo_grads[slot] = (both[0, w:], both[1, w:])
     shifted = {slot: along(halo_grads[slot][1], 1) for slot in owns}
-    crossed = {slot: across(halo_grads[slot][0], half) for slot in owns if slot & half}
+    crossed = {slot: across(halo_grads[slot][0], half) for slot in owns if half == 2}
     part_sum = part[0].astype(f32)
     arriving = [across(part[slot], slot) for slot in range(1, depth)]
     near_grads, _ = call(
@@ -669,11 +669,6 @@
     for moved in after(arriving, near_grads):
         part_sum = part_sum + moved.astype(f32)
     part = part_sum.astype(bf16)
-    shifted, crossed = after((shifted, crossed), near_grads)
-    for slot in list(owns):
-        real, imag = owns[slot]
-        owns[slot] = (real, total(imag, shifted[slot]))
-    near_grads = after(near_grads, owns, crossed, part)
     near_sums = core_sums(dict(enumerate(near_grads)))
     lat_bits = [1 << i for i in range(lat.bit_length() - 1)]
     butterfly = not lat & (lat - 1)
@@ -689,14 +684,16 @@
         for slot in sorted((s for s in owns if s & bit), reverse=True):
             halo_real, halo_imag = halo_grads.pop(slot)
             real, imag = owns.pop(slot)
-            halo_real = crossed[slot] if bit == half else across(halo_real, bit)
-            if slot not in shifted:
-                imag = total(imag, along(halo_imag, 1))
-            sent = across(jnp.stack([real, imag]), bit)
+            halo_real = crossed[slot] if slot in crossed else across(halo_real, bit)
             kept = halo_grads[slot ^ bit]
             halo_grads[slot ^ bit] = (total(kept[0], halo_real), kept[1])
+            moved = shifted[slot] if slot in shifted else along(halo_imag, 1)
             if len(halo_grads) == 1:
-                from_below = along(jnp.stack(halo_grads[0]), 1)
+                stacked = jnp.stack(halo_grads[0])
+                from_below = along(stacked, 1)
+                moved = after(moved, stacked)
+            sent = across(jnp.stack([real, total(imag, moved)]), bit)
+            if from_below is not None:
                 sent = after(sent, from_below)
             kept = owns[slot ^ bit]
             owns[slot ^ bit] = (total(kept[0], sent[0]), total(kept[1], sent[1]))

time: 89.5 us -> 89.6 us (level)
  waiting for transfers between devices: 33 us -> 28.6 us
  starting transfers between devices: 19.3 us -> 23 us
    ppermute x4, waiting for transfers between devices: 15.1 us -> 6.96 us  [along(): lax.ppermute(value, 'lat', [(i, (i + steps) % lat) for i in range(lat)])]
    ppermute x3, waiting for transfers between devices: 10.6 us -> 14.1 us  [along_xor(): return lax.ppermute(value, 'lat', [(i, i ^ bit) for i in range(lat)])]
    ppermute x14, starting transfers between devices: 9.04 us -> 11.2 us  [across(): return lax.ppermute(value, 'depth', [(i, i ^ bit) for i in range(depth)])]
    ppermute x3, starting transfers between devices: 0.21 us -> 2.09 us  [along_xor(): return lax.ppermute(value, 'lat', [(i, i ^ bit) for i in range(lat)])]
  transfers between devices with their start and end apart: 21 -> 21, of which waited for: 10 -> 10; matrix products, arithmetic and copies ran while one was open for 3% -> 3% of each run, Pallas kernels for 25% -> 20%
where the time goes in v6:
time: 89.6 us; the launch traced here: 88 us
  Pallas kernels  30.4 us (34%)
  waiting for transfers between devices  28.6 us (32%)
  starting transfers between devices  23 us (26%)
  other arithmetic  4.77 us (5%)
    pallas_call x5, Pallas kernels, call(): pl.pallas_call(kernel, out_shape=flat, in_specs=[spec for spec, _ in ins]...  30.4 us
    ppermute x3, waiting for transfers between devices, along_xor(): return lax.ppermute(value, 'lat', [(i, i ^ bit) for i in range(lat)])  14.1 us
    ppermute x14, starting transfers between devices, across(): return lax.ppermute(value, 'depth', [(i, i ^ bit) for i in range(depth)])  11.2 us
    ppermute x4, starting transfers between devices, along(): lax.ppermute(value, 'lat', [(i, (i + steps) % lat) for i in range(lat)])  9.77 us
    ppermute x14, waiting for transfers between devices, across(): return lax.ppermute(value, 'depth', [(i, i ^ bit) for i in range(depth)])  7.45 us
    ppermute x4, waiting for transfers between devices, along(): lax.ppermute(value, 'lat', [(i, (i + steps) % lat) for i in range(lat)])  6.96 us
    ppermute x3, starting transfers between devices, along_xor(): return lax.ppermute(value, 'lat', [(i, i ^ bit) for i in range(lat)])  2.09 us
  transfers between devices with their start and end apart: 21, of which 10 were waited for; matrix products, arithmetic and copies ran while one was open for 3% of the time, Pallas kernels for 20%

profile of v6, /device:TPU:0, one launch (start us, length us, event | category | flops | bytes accessed | tf_op | source)
XLA Modules:
  0.0 88.0 jit_solution(3789832737558185276)
XLA Ops:
  0.6 0.0 copy-start
  0.6 1.3 %convert_bitcast_fusion.refs_0_ = bf16[2,256,512]{2,1,0:T(8,128)(2,1)S(1)} fusion(f32[1,2,256,512]{3,2,1,0:T(8,128)} %param.6), kind=kLoop, calls=%fused_computation.10 | loop fusion | flops 262144 | bytes 1572864 | tf_op jit(solution)/shard_map/convert_element_type | solution.py:492
  1.9 3.0 %collective-permute-start.3 = (bf16[2,256,512]{2,1,0:T(8,128)(2,1)S(1)}, bf16[2,256,512]{2,1,0:T(8,128)(2,1)S(1)}, u32[]{:S(2)}, u32[]{:S(2)}) collective-permute-start(bf16[2,256,512]{2,1,0:T(8,128)(2,1)S(1)} %convert_bitcast_fusion.refs_0_), channel_id=1, source_target_pairs={{0,16},{8,24},{16,0},{24,8},{1,17},{9,25},{17,1},{25,9},{2,18},{10... | collective-permute-start | bytes 1572872 | tf_op jit(solution)/shard_map/ppermute | solution.py:481
  5.0 0.0 collective-permute-start.1
  5.0 4.5 %collective-permute-start = (bf16[2,256,512]{2,1,0:T(8,128)(2,1)S(1)}, bf16[2,256,512]{2,1,0:T(8,128)(2,1)S(1)}, u32[]{:S(2)}, u32[]{:S(2)}) collective-permute-start(bf16[2,256,512]{2,1,0:T(8,128)(2,1)S(1)} %convert_bitcast_fusion.refs_0_), channel_id=1, source_target_pairs={{0,7},{1,0},{2,1},{3,2},{4,3},{5,4},{6,5},{7,6},{8,15},{9,8},{10,9... | collective-permute-start | bytes 1572872 | tf_op jit(solution)/shard_map/ppermute | solution.py:484
  9.5 0.0 copy-done
  9.5 0.1 constant_dynamic-slice_fusion
  9.6 0.1 copy.13
  9.7 0.1 reshape.12
  9.8 0.6 pad_add_fusion.meta_ref
  10.4 6.4 %first_waves.1._ = bf16[32,4,2,256,256]{4,3,2,1,0:T(8,128)(2,1)} custom-call(s32[10]{0:T(128)} %pad_add_fusion.meta_ref, f32[2,256,256]{2,1,0:T(8,128)} %probe_ref.1, f32[16,2,256,256]{3,2,1,0:T(8,128)} %cot_hbm.1, bf16[512,512]{1,0:T(8,128)(2,1)} %constant.17.clone.right_ref, bf16[512,512]{1,0:T(8,128)(2,1)} %constant.18.clone.left_ref), custom_call_target="tpu_custom_call" | custom-call | flops 6442450944 | bytes 8388608 | tf_op jit(solution)/shard_map/first_waves/pallas_call | solution.py:511
  16.8 4.6 %collective-permute-done.refs_1_ = bf16[2,256,512]{2,1,0:T(8,128)(2,1)S(1)} collective-permute-done((bf16[2,256,512]{2,1,0:T(8,128)(2,1)S(1)}, bf16[2,256,512]{2,1,0:T(8,128)(2,1)S(1)}, u32[]{:S(2)}, u32[]{:S(2)}) %collective-permute-start) | collective-permute-done | bytes 524320 | tf_op jit(solution)/shard_map/ppermute | solution.py:484
  21.4 0.0 collective-permute-start.2
  21.4 0.0 collective-permute-done.3.refs_0_
  21.4 0.6 collective-permute-start.4
  22.0 5.2 %collective-permute-start.5 = (bf16[256,512]{1,0:T(8,128)(2,1)S(1)}, bf16[256,512]{1,0:T(8,128)(2,1)S(1)}, u32[]{:S(2)}, u32[]{:S(2)}) collective-permute-start(bf16[256,512]{1,0:T(8,128)(2,1)S(1)} %slice_bitcast_fusion.1), channel_id=1, source_target_pairs={{0,7},{1,0},{2,1},{3,2},{4,3},{5,4},{6,5},{7,6},{8,15},{9,8},{10,9... | collective-permute-start | bytes 786440 | tf_op jit(solution)/shard_map/ppermute | solution.py:484
  27.2 0.0 collective-permute-done.1.refs_2_
  27.2 0.0 collective-permute-done.2.refs_3_
  27.2 5.9 %near_slices.1._ = bf16[32,4,2,256,256]{4,3,2,1,0:T(8,128)(2,1)} custom-call(s32[10]{0:T(128)S(1)} %copy-done.3, bf16[32,4,2,256,256]{4,3,2,1,0:T(8,128)(2,1)} %first_waves.1._, bf16[512,512]{1,0:T(8,128)(2,1)S(1)} %copy-done.2, bf16[512,512]{1,0:T(8,128)(2,1)S(1)} %copy-done.1, ...), custom_call_target="tpu_custom_call", output_to_operand_aliasing={{}: (1, {})} | custom-call | flops 12884901888 | bytes 8388608 | tf_op jit(solution)/shard_map/near_slices/pallas_call | solution.py:511
  33.2 0.1 collective-permute-start.6
  33.2 0.0 collective-permute-done.5.refs_2_
  33.2 0.0 collective-permute-done.4.refs_1_
  33.3 0.5 collective-permute-start.7
  33.7 0.1 collective-permute-start.8
  33.8 1.7 %collective-permute-done.7.refs_4_ = bf16[256,512]{1,0:T(8,128)(2,1)S(1)} collective-permute-done((bf16[256,512]{1,0:T(8,128)(2,1)S(1)}, bf16[256,512]{1,0:T(8,128)(2,1)S(1)}, u32[]{:S(2)}, u32[]{:S(2)}) %collective-permute-start.7) | collective-permute-done | bytes 262176 | tf_op jit(solution)/shard_map/ppermute | solution.py:481
  35.5 0.4 collective-permute-done.8.refs_5_
  35.9 0.0 collective-permute-done.6.refs_3_
  35.9 8.3 %far_slices.1 = (bf16[2,512,512]{2,1,0:T(8,128)(2,1)S(1)}, bf16[2,512,512]{2,1,0:T(8,128)(2,1)S(1)}, bf16[32,4,2,256,256]{4,3,2,1,0:T(8,128)(2,1)}, bf16[4,256,5...) custom-call(s32[10]{0:T(128)S(1)} %copy-done.3, ...), custom_call_target="tpu_custom_call", output_to_operand_aliasing={{2}: (1, {})} | custom-call | flops 12884901888 | bytes 8388608 | tf_op jit(solution)/shard_map/far_slices/pallas_call | solution.py:511
  44.2 0.2 collective-permute-start.9
  44.4 5.5 %return_waves.1 = (bf16[32,4,2,256,256]{4,3,2,1,0:T(8,128)(2,1)}, bf16[4,2,64,256]{3,2,1,0:T(8,128)(2,1)S(1)}) custom-call(s32[10]{0:T(128)S(1)} %copy-done.3, bf16[32,4,2,256,256]{4,3,2,1,0:T(8,128)(2,1)} %get-tuple-element.35._, bf16[4,256,512]{2,1,0:T(8,128)(2,1)S(1)} %get-tuple-element.36.x_hbm, ...), custom_call_target="tpu_custom_call", output_to_operand_aliasing={{0}: (1, {})} | custom-call | flops 12884901888 | bytes 8388608 | tf_op jit(solution)/shard_map/return_waves/pallas_call | solution.py:511
  49.9 0.0 collective-permute-done.9
  50.0 0.3 add_convert_fusion.1
  50.3 4.2 %near_gradients.1 = (bf16[2,512,512]{2,1,0:T(8,128)(2,1)S(1)}, bf16[2,512,512]{2,1,0:T(8,128)(2,1)S(1)}, bf16[32,4,2,256,256]{4,3,2,1,0:T(8,128)(2,1)}) custom-call(s32[10]{0:T(128)S(1)} %copy-done.3, bf16[32,4,2,256,256]{4,3,2,1,0:T(8,128)(2,1)} %get-tuple-element.38._), custom_call_target="tpu_custom_call", output_to_operand_aliasing={{2}: (1, {})} | custom-call | flops 12884901888 | bytes 8388608 | tf_op jit(solution)/shard_map/near_gradients/pallas_call | solution.py:511
  54.5 0.4 collective-permute-start.10
  54.9 1.8 %collective-permute-start.13 = (bf16[2,64,256]{2,1,0:T(8,128)(2,1)S(1)}, bf16[2,64,256]{2,1,0:T(8,128)(2,1)S(1)}, u32[]{:S(2)}, u32[]{:S(2)}) collective-permute-start(bf16[2,64,256]{2,1,0:T(8,128)(2,1)S(1)} %get-tuple-element.55), channel_id=1, source_target_pairs={{0,24},{8,16},{16,8},{24,0},{1,25},{9,17},{17,9},{25,1},{2,26},{10... | collective-permute-start | bytes 196616 | tf_op jit(solution)/shard_map/ppermute | solution.py:481
  56.7 0.3 collective-permute-start.12
  57.0 0.0 collective-permute-start.11
  57.1 0.1 fusion.7
  57.1 1.8 %collective-permute-start.16 = (bf16[256,512]{1,0:T(8,128)(2,1)S(1)}, bf16[256,512]{1,0:T(8,128)(2,1)S(1)}, u32[]{:S(2)}, u32[]{:S(2)}) collective-permute-start(bf16[256,512]{1,0:T(8,128)(2,1)S(1)} %get-tuple-element.53), channel_id=1, source_target_pairs={{0,16},{8,24},{16,0},{24,8},{1,17},{9,25},{17,1},{25,9},{2,18},{10... | collective-permute-start | bytes 786440 | tf_op jit(solution)/shard_map/ppermute | solution.py:481
  58.9 0.2 collective-permute-done.13
  59.2 0.0 collective-permute-start.15
  59.2 2.4 %collective-permute-done.12 = bf16[2,64,256]{2,1,0:T(8,128)(2,1)S(1)} collective-permute-done((bf16[2,64,256]{2,1,0:T(8,128)(2,1)S(1)}, bf16[2,64,256]{2,1,0:T(8,128)(2,1)S(1)}, u32[]{:S(2)}, u32[]{:S(2)}) %collective-permute-start.12) | collective-permute-done | bytes 65568 | tf_op jit(solution)/shard_map/ppermute | solution.py:481
  61.6 0.0 collective-permute-done.11
  61.7 0.1 collective-permute-start.14
  61.7 0.0 collective-permute-done.10
  61.7 0.3 add_convert_fusion
  62.1 8.7 %collective-permute-done.14 = bf16[2,64,256]{2,1,0:T(8,128)(2,1)S(1)} collective-permute-done((bf16[2,64,256]{2,1,0:T(8,128)(2,1)S(1)}, bf16[2,64,256]{2,1,0:T(8,128)(2,1)S(1)}, u32[]{:S(2)}, u32[]{:S(2)}) %collective-permute-start.14) | collective-permute-done | bytes 65568 | tf_op jit(solution)/shard_map/ppermute | solution.py:487
  70.8 0.1 collective-permute-start.19
  70.9 0.0 collective-permute-done.16
  70.9 0.1 fusion.1
  71.0 0.1 pad_maximum_fusion
  71.0 0.1 collective-permute-start.18
  71.1 0.0 collective-permute-done.15
  71.1 0.1 fusion.2
  71.2 0.1 pad_maximum_fusion.1
  71.3 2.3 %collective-permute-start.17 = (bf16[2,256,512]{2,1,0:T(8,128)(2,1)S(1)}, bf16[2,256,512]{2,1,0:T(8,128)(2,1)S(1)}, u32[]{:S(2)}, u32[]{:S(2)}) collective-permute-start(bf16[2,256,512]{2,1,0:T(8,128)(2,1)S(1)} %pad_maximum_fusion.1), channel_id=1, source_target_pairs={{0,16},{8,24},{16,0},{24,8},{1,17},{9,25},{17,1},{25,9},{2,18},{10... | collective-permute-start | bytes 1572872 | tf_op jit(solution)/shard_map/ppermute | solution.py:481
  73.6 1.6 %collective-permute-done.19 = bf16[2,64,256]{2,1,0:T(8,128)(2,1)S(1)} collective-permute-done((bf16[2,64,256]{2,1,0:T(8,128)(2,1)S(1)}, bf16[2,64,256]{2,1,0:T(8,128)(2,1)S(1)}, u32[]{:S(2)}, u32[]{:S(2)}) %collective-permute-start.19) | collective-permute-done | bytes 65568 | tf_op jit(solution)/shard_map/ppermute | solution.py:487
  75.2 1.9 %collective-permute-start.20 = (bf16[2,64,256]{2,1,0:T(8,128)(2,1)S(1)}, bf16[2,64,256]{2,1,0:T(8,128)(2,1)S(1)}, u32[]{:S(2)}, u32[]{:S(2)}) collective-permute-start(bf16[2,64,256]{2,1,0:T(8,128)(2,1)S(1)} %add_convert_fusion.6), channel_id=1, source_target_pairs={{0,4},{1,5},{2,6},{3,7},{4,0},{5,1},{6,2},{7,3},{8,12},{9,13},{10,... | collective-permute-start | bytes 196616 | tf_op jit(solution)/shard_map/ppermute | solution.py:487
  77.1 3.8 %collective-permute-done.20 = bf16[2,64,256]{2,1,0:T(8,128)(2,1)S(1)} collective-permute-done((bf16[2,64,256]{2,1,0:T(8,128)(2,1)S(1)}, bf16[2,64,256]{2,1,0:T(8,128)(2,1)S(1)}, u32[]{:S(2)}, u32[]{:S(2)}) %collective-permute-start.20) | collective-permute-done | bytes 65568 | tf_op jit(solution)/shard_map/ppermute | solution.py:487
  81.0 0.7 fusion.6
  81.6 2.7 %collective-permute-done.17 = bf16[2,256,512]{2,1,0:T(8,128)(2,1)S(1)} collective-permute-done((bf16[2,256,512]{2,1,0:T(8,128)(2,1)S(1)}, bf16[2,256,512]{2,1,0:T(8,128)(2,1)S(1)}, u32[]{:S(2)}, u32[]{:S(2)}) %collective-permute-start.17) | collective-permute-done | bytes 524320 | tf_op jit(solution)/shard_map/ppermute | solution.py:481
  84.3 2.4 %collective-permute-done.18 = bf16[2,256,512]{2,1,0:T(8,128)(2,1)S(1)} collective-permute-done((bf16[2,256,512]{2,1,0:T(8,128)(2,1)S(1)}, bf16[2,256,512]{2,1,0:T(8,128)(2,1)S(1)}, u32[]{:S(2)}, u32[]{:S(2)}) %collective-permute-start.18) | collective-permute-done | bytes 524320 | tf_op jit(solution)/shard_map/ppermute | solution.py:484
  86.7 0.1 add_convert_fusion.3
  86.8 1.1 %add_bitcast_fusion = f32[1,2,256,512]{3,2,1,0:T(8,128)} fusion(bf16[2,256,512]{2,1,0:T(8,128)(2,1)S(1)} %collective-permute-done.18, bf16[1,256,512]{2,1,0:T(8,128)(2,1)S(1)} %get-tuple-element.51, bf16[1,256,512]{2,1,0:T(8,128)(2,1)S(1)} %get-tuple-element.50), kind=kLoop, calls=%fused_computation.2 | loop fusion | flops 1048576 | bytes 2097152 | tf_op jit(solution)/shard_map/broadcast_in_dim | solution.py:700
  (13 shorter events, 0.2 us)
Async XLA Ops:
  0.6 8.9 %copy-start = (s32[16,2]{0,1:T(2,128)S(1)}, s32[16,2]{0,1:T(2,128)}, u32[]{:S(2)}) copy-start(s32[16,2]{0,1:T(2,128)} %param.8) | copy-start | bytes 388
  1.9 19.4 %collective-permute-start.3 = (bf16[2,256,512]{2,1,0:T(8,128)(2,1)S(1)}, bf16[2,256,512]{2,1,0:T(8,128)(2,1)S(1)}, u32[]{:S(2)}, u32[]{:S(2)}) collective-permute-start(bf16[2,256,512]{2,1,0:T(8,128)(2,1)S(1)} %convert_bitcast_fusion.refs_0_), channel_id=1, source_target_pairs={{0,16},{8,24},{16,0},{24,8},{1,17},{9,25},{17,1},{25,9},{2,18},{10... | collective-permute-start | bytes 1572872 | tf_op jit(solution)/shard_map/ppermute | solution.py:481
  5.0 22.2 %collective-permute-start.1 = (bf16[2,256,512]{2,1,0:T(8,128)(2,1)S(1)}, bf16[2,256,512]{2,1,0:T(8,128)(2,1)S(1)}, u32[]{:S(2)}, u32[]{:S(2)}) collective-permute-start(bf16[2,256,512]{2,1,0:T(8,128)(2,1)S(1)} %convert_bitcast_fusion.refs_0_), channel_id=1, source_target_pairs={{0,8},{8,0},{16,24},{24,16},{1,9},{9,1},{17,25},{25,17},{2,10},{10... | collective-permute-start | bytes 1572872 | tf_op jit(solution)/shard_map/ppermute | solution.py:481
  5.0 16.4 %collective-permute-start = (bf16[2,256,512]{2,1,0:T(8,128)(2,1)S(1)}, bf16[2,256,512]{2,1,0:T(8,128)(2,1)S(1)}, u32[]{:S(2)}, u32[]{:S(2)}) collective-permute-start(bf16[2,256,512]{2,1,0:T(8,128)(2,1)S(1)} %convert_bitcast_fusion.refs_0_), channel_id=1, source_target_pairs={{0,7},{1,0},{2,1},{3,2},{4,3},{5,4},{6,5},{7,6},{8,15},{9,8},{10,9... | collective-permute-start | bytes 1572872 | tf_op jit(solution)/shard_map/ppermute | solution.py:484
  10.4 16.8 %copy-start.1 = (bf16[512,512]{1,0:T(8,128)(2,1)S(1)}, bf16[512,512]{1,0:T(8,128)(2,1)}, u32[]{:S(2)}) copy-start(bf16[512,512]{1,0:T(8,128)(2,1)} %constant.18.clone.left_ref) | copy-start | bytes 1572868
  10.4 16.8 %copy-start.2 = (bf16[512,512]{1,0:T(8,128)(2,1)S(1)}, bf16[512,512]{1,0:T(8,128)(2,1)}, u32[]{:S(2)}) copy-start(bf16[512,512]{1,0:T(8,128)(2,1)} %constant.17.clone.right_ref) | copy-start | bytes 1572868
  10.4 16.8 %copy-start.3 = (s32[10]{0:T(128)S(1)}, s32[10]{0:T(128)}, u32[]{:S(2)}) copy-start(s32[10]{0:T(128)} %pad_add_fusion.meta_ref) | copy-start | bytes 124
  21.4 5.8 %collective-permute-start.2 = (bf16[2,256,512]{2,1,0:T(8,128)(2,1)S(1)}, bf16[2,256,512]{2,1,0:T(8,128)(2,1)S(1)}, u32[]{:S(2)}, u32[]{:S(2)}) collective-permute-start(bf16[2,256,512]{2,1,0:T(8,128)(2,1)S(1)} %collective-permute-done.refs_1_), channel_id=1, source_target_pairs={{0,8},{8,0},{16,24},{24,16},{1,9},{9,1},{17,25},{25,17},{2,10},{10... | collective-permute-start | bytes 1572872 | tf_op jit(solution)/shard_map/ppermute | solution.py:481
  21.4 11.8 %collective-permute-start.4 = (bf16[256,512]{1,0:T(8,128)(2,1)S(1)}, bf16[256,512]{1,0:T(8,128)(2,1)S(1)}, u32[]{:S(2)}, u32[]{:S(2)}) collective-permute-start(bf16[256,512]{1,0:T(8,128)(2,1)S(1)} %slice_bitcast_fusion.2), channel_id=1, source_target_pairs={{0,16},{8,24},{16,0},{24,8},{1,17},{9,25},{17,1},{25,9},{2,18},{10... | collective-permute-start | bytes 786440 | tf_op jit(solution)/shard_map/ppermute | solution.py:481
  22.0 11.2 %collective-permute-start.5 = (bf16[256,512]{1,0:T(8,128)(2,1)S(1)}, bf16[256,512]{1,0:T(8,128)(2,1)S(1)}, u32[]{:S(2)}, u32[]{:S(2)}) collective-permute-start(bf16[256,512]{1,0:T(8,128)(2,1)S(1)} %slice_bitcast_fusion.1), channel_id=1, source_target_pairs={{0,7},{1,0},{2,1},{3,2},{4,3},{5,4},{6,5},{7,6},{8,15},{9,8},{10,9... | collective-permute-start | bytes 786440 | tf_op jit(solution)/shard_map/ppermute | solution.py:484
  33.2 2.7 %collective-permute-start.6 = (bf16[2,256,512]{2,1,0:T(8,128)(2,1)S(1)}, bf16[2,256,512]{2,1,0:T(8,128)(2,1)S(1)}, u32[]{:S(2)}, u32[]{:S(2)}) collective-permute-start(bf16[2,256,512]{2,1,0:T(8,128)(2,1)S(1)} %collective-permute-done.3.refs_0_), channel_id=1, source_target_pairs={{0,8},{8,0},{16,24},{24,16},{1,9},{9,1},{17,25},{25,17},{2,10},{10... | collective-permute-start | bytes 1572872 | tf_op jit(solution)/shard_map/ppermute | solution.py:481
  33.3 2.3 %collective-permute-start.7 = (bf16[256,512]{1,0:T(8,128)(2,1)S(1)}, bf16[256,512]{1,0:T(8,128)(2,1)S(1)}, u32[]{:S(2)}, u32[]{:S(2)}) collective-permute-start(bf16[256,512]{1,0:T(8,128)(2,1)S(1)} %collective-permute-done.4.refs_1_), channel_id=1, source_target_pairs={{0,8},{8,0},{16,24},{24,16},{1,9},{9,1},{17,25},{25,17},{2,10},{10... | collective-permute-start | bytes 786440 | tf_op jit(solution)/shard_map/ppermute | solution.py:481
  33.7 2.1 %collective-permute-start.8 = (bf16[256,512]{1,0:T(8,128)(2,1)S(1)}, bf16[256,512]{1,0:T(8,128)(2,1)S(1)}, u32[]{:S(2)}, u32[]{:S(2)}) collective-permute-start(bf16[256,512]{1,0:T(8,128)(2,1)S(1)} %collective-permute-done.5.refs_2_), channel_id=1, source_target_pairs={{0,8},{8,0},{16,24},{24,16},{1,9},{9,1},{17,25},{25,17},{2,10},{10... | collective-permute-start | bytes 786440 | tf_op jit(solution)/shard_map/ppermute | solution.py:481
  44.2 5.7 %collective-permute-start.9 = (bf16[2,512,512]{2,1,0:T(8,128)(2,1)S(1)}, bf16[2,512,512]{2,1,0:T(8,128)(2,1)S(1)}, u32[]{:S(2)}, u32[]{:S(2)}) collective-permute-start(bf16[2,512,512]{2,1,0:T(8,128)(2,1)S(1)} %get-tuple-element.33), channel_id=1, source_target_pairs={{0,8},{8,0},{16,24},{24,16},{1,9},{9,1},{17,25},{25,17},{2,10},{10... | collective-permute-start | bytes 3145736 | tf_op jit(solution)/shard_map/ppermute | solution.py:481
  54.5 7.3 %collective-permute-start.10 = (bf16[2,512,512]{2,1,0:T(8,128)(2,1)S(1)}, bf16[2,512,512]{2,1,0:T(8,128)(2,1)S(1)}, u32[]{:S(2)}, u32[]{:S(2)}) collective-permute-start(bf16[2,512,512]{2,1,0:T(8,128)(2,1)S(1)} %get-tuple-element.40), channel_id=1, source_target_pairs={{0,8},{8,0},{16,24},{24,16},{1,9},{9,1},{17,25},{25,17},{2,10},{10... | collective-permute-start | bytes 3145736 | tf_op jit(solution)/shard_map/ppermute | solution.py:481
  54.9 4.3 %collective-permute-start.13 = (bf16[2,64,256]{2,1,0:T(8,128)(2,1)S(1)}, bf16[2,64,256]{2,1,0:T(8,128)(2,1)S(1)}, u32[]{:S(2)}, u32[]{:S(2)}) collective-permute-start(bf16[2,64,256]{2,1,0:T(8,128)(2,1)S(1)} %get-tuple-element.55), channel_id=1, source_target_pairs={{0,24},{8,16},{16,8},{24,0},{1,25},{9,17},{17,9},{25,1},{2,26},{10... | collective-permute-start | bytes 196616 | tf_op jit(solution)/shard_map/ppermute | solution.py:481
  56.7 4.9 %collective-permute-start.12 = (bf16[2,64,256]{2,1,0:T(8,128)(2,1)S(1)}, bf16[2,64,256]{2,1,0:T(8,128)(2,1)S(1)}, u32[]{:S(2)}, u32[]{:S(2)}) collective-permute-start(bf16[2,64,256]{2,1,0:T(8,128)(2,1)S(1)} %get-tuple-element.56), channel_id=1, source_target_pairs={{0,16},{8,24},{16,0},{24,8},{1,17},{9,25},{17,1},{25,9},{2,18},{10... | collective-permute-start | bytes 196616 | tf_op jit(solution)/shard_map/ppermute | solution.py:481
  57.0 4.6 %collective-permute-start.11 = (bf16[2,64,256]{2,1,0:T(8,128)(2,1)S(1)}, bf16[2,64,256]{2,1,0:T(8,128)(2,1)S(1)}, u32[]{:S(2)}, u32[]{:S(2)}) collective-permute-start(bf16[2,64,256]{2,1,0:T(8,128)(2,1)S(1)} %get-tuple-element.57), channel_id=1, source_target_pairs={{0,8},{8,0},{16,24},{24,16},{1,9},{9,1},{17,25},{25,17},{2,10},{10... | collective-permute-start | bytes 196616 | tf_op jit(solution)/shard_map/ppermute | solution.py:481
  57.1 13.8 %collective-permute-start.16 = (bf16[256,512]{1,0:T(8,128)(2,1)S(1)}, bf16[256,512]{1,0:T(8,128)(2,1)S(1)}, u32[]{:S(2)}, u32[]{:S(2)}) collective-permute-start(bf16[256,512]{1,0:T(8,128)(2,1)S(1)} %get-tuple-element.53), channel_id=1, source_target_pairs={{0,16},{8,24},{16,0},{24,8},{1,17},{9,25},{17,1},{25,9},{2,18},{10... | collective-permute-start | bytes 786440 | tf_op jit(solution)/shard_map/ppermute | solution.py:481
  59.2 11.9 %collective-permute-start.15 = (bf16[256,512]{1,0:T(8,128)(2,1)S(1)}, bf16[256,512]{1,0:T(8,128)(2,1)S(1)}, u32[]{:S(2)}, u32[]{:S(2)}) collective-permute-start(bf16[256,512]{1,0:T(8,128)(2,1)S(1)} %get-tuple-element.54), channel_id=1, source_target_pairs={{0,1},{1,2},{2,3},{3,4},{4,5},{5,6},{6,7},{7,0},{8,9},{9,10},{10,1... | collective-permute-start | bytes 786440 | tf_op jit(solution)/shard_map/ppermute | solution.py:484
  61.7 9.1 %collective-permute-start.14 = (bf16[2,64,256]{2,1,0:T(8,128)(2,1)S(1)}, bf16[2,64,256]{2,1,0:T(8,128)(2,1)S(1)}, u32[]{:S(2)}, u32[]{:S(2)}) collective-permute-start(bf16[2,64,256]{2,1,0:T(8,128)(2,1)S(1)} %fusion.5), channel_id=1, source_target_pairs={{0,1},{1,0},{2,3},{3,2},{4,5},{5,4},{6,7},{7,6},{8,9},{9,8},{10,11... | collective-permute-start | bytes 196616 | tf_op jit(solution)/shard_map/ppermute | solution.py:487
  70.8 4.3 %collective-permute-start.19 = (bf16[2,64,256]{2,1,0:T(8,128)(2,1)S(1)}, bf16[2,64,256]{2,1,0:T(8,128)(2,1)S(1)}, u32[]{:S(2)}, u32[]{:S(2)}) collective-permute-start(bf16[2,64,256]{2,1,0:T(8,128)(2,1)S(1)} %add_convert_fusion.7), channel_id=1, source_target_pairs={{0,2},{1,3},{2,0},{3,1},{4,6},{5,7},{6,4},{7,5},{8,10},{9,11},{10,... | collective-permute-start | bytes 196616 | tf_op jit(solution)/shard_map/ppermute | solution.py:487
  71.0 15.7 %collective-permute-start.18 = (bf16[2,256,512]{2,1,0:T(8,128)(2,1)S(1)}, bf16[2,256,512]{2,1,0:T(8,128)(2,1)S(1)}, u32[]{:S(2)}, u32[]{:S(2)}) collective-permute-start(bf16[2,256,512]{2,1,0:T(8,128)(2,1)S(1)} %pad_maximum_fusion), channel_id=1, source_target_pairs={{0,1},{1,2},{2,3},{3,4},{4,5},{5,6},{6,7},{7,0},{8,9},{9,10},{10,1... | collective-permute-start | bytes 1572872 | tf_op jit(solution)/shard_map/ppermute | solution.py:484
  71.3 13.1 %collective-permute-start.17 = (bf16[2,256,512]{2,1,0:T(8,128)(2,1)S(1)}, bf16[2,256,512]{2,1,0:T(8,128)(2,1)S(1)}, u32[]{:S(2)}, u32[]{:S(2)}) collective-permute-start(bf16[2,256,512]{2,1,0:T(8,128)(2,1)S(1)} %pad_maximum_fusion.1), channel_id=1, source_target_pairs={{0,16},{8,24},{16,0},{24,8},{1,17},{9,25},{17,1},{25,9},{2,18},{10... | collective-permute-start | bytes 1572872 | tf_op jit(solution)/shard_map/ppermute | solution.py:481
  75.2 5.8 %collective-permute-start.20 = (bf16[2,64,256]{2,1,0:T(8,128)(2,1)S(1)}, bf16[2,64,256]{2,1,0:T(8,128)(2,1)S(1)}, u32[]{:S(2)}, u32[]{:S(2)}) collective-permute-start(bf16[2,64,256]{2,1,0:T(8,128)(2,1)S(1)} %add_convert_fusion.6), channel_id=1, source_target_pairs={{0,4},{1,5},{2,6},{3,7},{4,0},{5,1},{6,2},{7,3},{8,12},{9,13},{10,... | collective-permute-start | bytes 196616 | tf_op jit(solution)/shard_map/ppermute | solution.py:487
